TPU v7x, 256 devices: a whole 4x4x8 slice. The times are simulated.
256 devices in a mesh: dp: 16 (over y, x), token: 16 (over z, core).
Axes of the slice: x: 4, y: 4, z: 8, core: 2. Of those that a mesh axis runs over, the one named last changes fastest.
Arguments:
- mix_input: bfloat16 [6144, 16, 768], P('dp', 'token'), may hold values from -6 to 6
- out_grad: bfloat16 [6144, 16, 768], P('dp', 'token'), may hold values from -1.5 to 1.5
- w_up: bfloat16 [16, 768, 3072], P('token'), may hold values from -0.21875 to 0.21875
- w_down: bfloat16 [16, 3072, 768], P('token'), may hold values from -0.109375 to 0.109375
- gain_first: float32 [16, 768], P('token'), may hold values from 0.25 to 1.75
- gain_second: float32 [16, 768], P('token'), may hold values from 0.25 to 1.75
- owner_dev: int32 [16, 6144, 1], P('token', 'dp'), may hold values from 0 to 15; in each aligned block of 384 rows (0 to 383, 384 to 767, ..., all dimensions but the last counted through in order) at most 56 rows name the same one
- slot_row: int32 [16, 6144], P('token', 'dp'), may hold values from 0 to 255
Outputs:
- grad_up: float32 [16, 768, 3072], P('token', 'dp')
- grad_down: float32 [16, 3072, 768], P('token', 'dp')
- row_grad: float32 [16, 4096, 768], P('token', 'dp')
Inputs may be any that keep to these rules, and one draw needn't show every extreme that they name: `owner_dev`: in the rows of one device (aligned blocks of 384 samples of one token) no owner is named by more than 56 rows, a bound that some block reaches.
All inputs are finite; a program needn't handle non-finite values.
Results may differ from a plain program's by a relative error of at most 0.015.
Values may be sent and summed in bfloat16 or wider, within the bound.
No kernel may reach another device: no remote copies, remote signals or barrier semaphores. Data moves between devices by JAX's collectives and lax.ppermute only.
A program may use at most 128 MiB of HBM per device.

v0:
```python
import jax
import jax.numpy as jnp
from jax import lax
from jax.sharding import PartitionSpec as P

HOT = 256


EPS = 1e-05
HALF_ROOT = 0.7071067811865476
INV_ROOT_TAU = 0.3989422804014327


def normalize(values):
    center = values - jnp.mean(values, axis=-1, keepdims=True)
    inv_scale = lax.rsqrt(jnp.mean(center * center, axis=-1, keepdims=True) + EPS)
    return (center * inv_scale, inv_scale)


def norm_back(grad_norm, normed, inv_scale):
    mean_grad = jnp.mean(grad_norm, axis=-1, keepdims=True)
    mean_proj = jnp.mean(grad_norm * normed, axis=-1, keepdims=True)
    return inv_scale * (grad_norm - mean_grad - normed * mean_proj)


def gelu_parts(pre_act):
    cumul = 0.5 * (1.0 + jax.scipy.special.erf(pre_act * HALF_ROOT))
    density = jnp.exp(-0.5 * pre_act * pre_act) * INV_ROOT_TAU
    return (pre_act * cumul, cumul + pre_act * density)


def contract_rows(left, right):
    return lax.dot_general(
        left, right, (((0,), (0,)), ((), ())), preferred_element_type=jnp.float32
    )


def contract_cols(left, right):
    return lax.dot_general(
        left, right, (((1,), (1,)), ((), ())), preferred_element_type=jnp.float32
    )


def per_device(mix_input, out_grad, w_up, w_down, gain_first, gain_second, owner_dev, slot_row):
    batch_rows = mix_input.shape[0]
    width = mix_input.shape[2]
    owners = lax.axis_size("dp")
    normed, inv_scale = normalize(mix_input[:, 0, :].astype(jnp.float32))
    hidden_in = (normed * gain_first[0]).astype(jnp.bfloat16)
    pre_act = jnp.dot(hidden_in, w_up[0], preferred_element_type=jnp.float32)
    act_value, act_slope = gelu_parts(pre_act)
    active = act_value.astype(jnp.bfloat16)
    outer_sum = jnp.dot(active, w_down[0], preferred_element_type=jnp.float32) + hidden_in.astype(
        jnp.float32
    )
    normed_out, inv_out = normalize(outer_sum)
    grad_wide = norm_back(
        out_grad[:, 0, :].astype(jnp.float32) * gain_second[0], normed_out, inv_out
    )
    grad_mid = grad_wide.astype(jnp.bfloat16)
    grad_act = contract_cols(grad_mid, w_down[0])
    grad_pre = (grad_act * act_slope).astype(jnp.bfloat16)
    up_whole = contract_rows(hidden_in, grad_pre)
    down_whole = contract_rows(active, grad_mid)
    grad_up, grad_down = (
        lax.psum_scatter(
            up_whole.astype(jnp.bfloat16), "dp", scatter_dimension=0, tiled=True
        ).astype(jnp.float32),
        lax.psum_scatter(
            down_whole.astype(jnp.bfloat16), "dp", scatter_dimension=0, tiled=True
        ).astype(jnp.float32),
    )
    grad_hidden = contract_cols(grad_pre, w_up[0]) + grad_wide
    grad_sum = norm_back(grad_hidden * gain_first[0], normed, inv_scale).astype(jnp.bfloat16)
    pieces = lax.axis_size("token")
    swapped = lax.all_to_all(
        grad_sum.reshape(batch_rows, pieces, width // pieces),
        "token",
        split_axis=1,
        concat_axis=1,
        tiled=True,
    )
    embed_grad = (
        grad_sum.astype(jnp.float32) + swapped.reshape(batch_rows, width).astype(jnp.float32)
    ).astype(jnp.bfloat16)
    owner_ids = owner_dev[0, :, 0]
    slot_ids = slot_row[0]
    target = owner_ids * HOT + slot_ids
    picker = (
        lax.broadcasted_iota(jnp.int32, (owners * HOT, batch_rows), 0) == target[None, :]
    ).astype(jnp.bfloat16)
    local_table = jnp.dot(picker, embed_grad, preferred_element_type=jnp.float32)
    row_grad = lax.psum_scatter(
        local_table.astype(jnp.bfloat16), "dp", scatter_dimension=0, tiled=True
    ).astype(jnp.float32)
    return (grad_up[None], grad_down[None], row_grad[None])


def solution(mesh):
    placed = (
        P("dp", "token", None),
        P("dp", "token", None),
        P("token", None, None),
        P("token", None, None),
        P("token", None),
        P("token", None),
        P("token", "dp", None),
        P("token", "dp"),
    )
    return jax.shard_map(
        per_device,
        mesh=mesh,
        in_specs=placed,
        out_specs=(P("token", "dp", None), P("token", "dp", None), P("token", "dp", None)),
        check_vma=False,
    )
```

profile of v0, /device:TPU:6, one launch (start us, length us, event | category | flops | bytes accessed | tf_op | source)
XLA Modules:
  0.0 297.8 jit_solution(995851657166844599)
XLA Ops:
  7.2 0.0 copy-start
  7.2 0.0 copy-start.2
  7.2 0.0 copy-start.3
  7.2 0.0 reduce-scatter.6.cloned.1.call-start
  7.2 1.3 convert_reduce_fusion
  8.5 1.4 fusion.37
  9.9 0.0 copy-done.2
  9.9 0.0 copy-done.3
  10.0 0.0 copy-done
  10.0 6.3 %multiply_convert_fusion = (bf16[384,3072]{1,0:T(8,128)(2,1)S(1)}, f32[384,3072]{1,0:T(8,128)}) fusion(bf16[1,768,3072]{2,1,0:T(8,128)(2,1)} %param.10, bf16[384,1,768]{2,0,1:T(8,128)(2,1)S(1)} %copy-done, f32[768]{0:T(1024)S(1)} %reduce.1, f32[384]{0:T(512)S(1)} %add_rsqrt_fusion.1, f32[384]{0:T(512)S(1)} %broadcast_multiply_fusion.5), kind=kOutput, calls=%fused_computation.19 | convolution fusion | flops 1819312128 | bytes 12392448 | tf_op jit(solution)/shard_map/dot_general | solution.py:50
  16.3 4.4 %fusion.59 = (f32[384]{0:T(512)S(1)}, f32[384,768]{1,0:T(8,128)S(1)}) fusion(f32[768]{0:T(1024)S(1)} %reduce.1, f32[384]{0:T(512)S(1)} %add_rsqrt_fusion.1, f32[384]{0:T(512)S(1)} %broadcast_multiply_fusion.5, bf16[384,1,768]{2,0,1:T(8,128)(2,1)S(1)} %copy-done, bf16[384,3072]{1,0:T(8,128)(2,1)S(1)} %get-tuple-element.7, bf16[1,3072,768]{2,1,0:T(8,128)(2,1)} %param.11), kind=kOutput, calls=%fused_computation.73 | convolution fusion | flops 1814298240 | bytes 8855040 | tf_op jit(solution)/shard_map/dot_general | solution.py:53
  20.7 0.0 copy-start.1
  20.7 0.3 multiply_reduce_fusion
  21.0 0.8 copy-done.1
  21.8 0.4 fusion.43
  22.2 4.8 %convolution_convert_fusion.1 = bf16[3072,768]{1,0:T(8,128)(2,1)} fusion(bf16[384,3072]{1,0:T(8,128)(2,1)S(1)} %get-tuple-element.7, f32[384,768]{1,0:T(8,128)S(1)} %get-tuple-element.10, bf16[384,1,768]{2,0,1:T(8,128)(2,1)S(1)} %copy-done.1, f32[384]{0:T(512)S(1)} %get-tuple-element.12, f32[384]{0:T(512)S(1)} %get-tuple-element.13, f32[768]{0:T(1024)S(1)} %reduce.2, ...), kind=kOutput, calls=%fused_computation.3 | convolution fusion | flops 1816952832 | bytes 8856576 | tf_op jit(solution)/shard_map/dot_general | solution.py:33
  27.0 0.0 reduce-scatter.6.cloned.1.call-update
  27.0 0.0 reduce-scatter.4.cloned.1.call-start
  27.1 6.8 %fusion.5 = bf16[384,3072]{1,0:T(8,128)(2,1)S(1)} fusion(f32[384,3072]{1,0:T(8,128)} %get-tuple-element.8, bf16[1,3072,768]{2,1,0:T(8,128)(2,1)} %param.11, f32[384,768]{1,0:T(8,128)S(1)} %get-tuple-element.10, bf16[384,1,768]{2,0,1:T(8,128)(2,1)S(1)} %copy-done.1, f32[384]{0:T(512)S(1)} %get-tuple-element.12, f32[384]{0:T(512)S(1)} %get-tuple-element.13, ...), kind=kOutput, calls=%fused_computation.10 | convolution fusion | flops 1826390016 | bytes 13575168 | tf_op jit(solution)/shard_map/dot_general | solution.py:39
  33.9 0.0 copy-start.6
  33.9 1.4 copy-done.6
  35.3 4.7 %convolution_convert_fusion.2 = bf16[768,3072]{1,0:T(8,128)(2,1)} fusion(bf16[384,3072]{1,0:T(8,128)(2,1)S(1)} %fusion.5, bf16[384,1,768]{2,0,1:T(8,128)(2,1)S(1)} %copy-done, f32[768]{0:T(1024)S(1)} %reduce.1, f32[384]{0:T(512)S(1)} %add_rsqrt_fusion.1, f32[384]{0:T(512)S(1)} %broadcast_multiply_fusion.5), kind=kOutput, calls=%fused_computation.4 | convolution fusion | flops 1815773184 | bytes 7673856 | tf_op jit(solution)/shard_map/dot_general | solution.py:33
  40.0 0.0 reduce-scatter.4.cloned.1.call-update
  40.0 5.7 %fusion.58 = (f32[384]{0:T(512)S(1)}, f32[384]{0:T(512)S(1)}, f32[384,768]{1,0:T(8,128)S(1)}) fusion(f32[384]{0:T(512)S(1)} %add_rsqrt_fusion.1, f32[384]{0:T(512)S(1)} %broadcast_multiply_fusion.5, bf16[384,1,768]{2,0,1:T(8,128)(2,1)S(1)} %copy-done, f32[768]{0:T(1024)S(1)} %reduce.1, f32[384]{0:T(512)S(1)} %get-tuple-element.12, ...), kind=kOutput, calls=%fused_computation.72 | convolution fusion | flops 1816657152 | bytes 10635264 | tf_op jit(solution)/shard_map/dot_general | solution.py:39
  45.7 0.4 fusion.36
  46.1 0.0 copy-start.4
  46.1 0.0 copy-start.5
  46.1 1.1 copy.11
  47.2 8.4 %all-to-all-start = ((bf16[384,16,48]{0,2,1:T(8,128)(2,1)}), bf16[384,16,48]{0,2,1:T(8,128)(2,1)S(1)}, u32[]{:S(2)}, u32[]{:S(2)}) async-start(bf16[384,16,48]{0,2,1:T(8,128)(2,1)} %bitcast.8), calls=%async_computation.2 | async-start | bytes 1179648 | tf_op jit(solution)/shard_map/all_to_all | solution.py:76
  55.6 0.2 reduce-scatter.8.cloned.1.call-start
  55.8 0.0 copy-done.4
  55.8 0.0 copy-done.5
  55.9 16.9 %all-to-all-done = bf16[384,16,48]{0,2,1:T(8,128)(2,1)S(1)} async-done(((bf16[384,16,48]{0,2,1:T(8,128)(2,1)}), bf16[384,16,48]{0,2,1:T(8,128)(2,1)S(1)}, u32[]{:S(2)}, u32[]{:S(2)}) %all-to-all-start) | async-done | bytes 589856 | tf_op jit(solution)/shard_map/all_to_all | solution.py:76
  72.8 0.1 bitcast_convert_fusion
  73.0 0.4 copy.12
  73.3 5.5 %convolution_convert_fusion = bf16[4096,768]{1,0:T(8,128)(2,1)} fusion(s32[384]{0:T(512)S(1)} %fusion.54, f32[384,768]{1,0:T(8,128)S(1)} %copy.12, bf16[384,768]{1,0:T(8,128)(2,1)S(1)} %fusion.36), kind=kOutput, calls=%fused_computation.1 | convolution fusion | flops 2421522432 | bytes 8062464 | tf_op jit(solution)/shard_map/dot_general | solution.py:92
  78.8 0.0 reduce-scatter.8.cloned.1.call-update
  78.9 34.3 %reduce-scatter.6.cloned.1.call-done = bf16[192,768]{1,0:T(8,128)(2,1)} async-done(((bf16[3072,768]{1,0:T(8,128)(2,1)}), bf16[192,768]{1,0:T(8,128)(2,1)}) %reduce-scatter.6.cloned.1.call-update) | async-done | bytes 294928 | tf_op jit(solution)/shard_map/reduce_scatter | solution.py:69
  113.2 1.8 bitcast_convert_fusion.2
  115.0 84.9 %reduce-scatter.4.cloned.1.call-done = bf16[48,3072]{1,0:T(8,128)(2,1)} async-done(((bf16[768,3072]{1,0:T(8,128)(2,1)}), bf16[48,3072]{1,0:T(8,128)(2,1)}) %reduce-scatter.4.cloned.1.call-update) | async-done | bytes 294928 | tf_op jit(solution)/shard_map/reduce_scatter | solution.py:66
  199.8 1.8 bitcast_convert_fusion.3
  201.6 87.7 %reduce-scatter.8.cloned.1.call-done = bf16[256,768]{1,0:T(8,128)(2,1)} async-done(((bf16[4096,768]{1,0:T(8,128)(2,1)}), bf16[256,768]{1,0:T(8,128)(2,1)}) %reduce-scatter.8.cloned.1.call-update) | async-done | bytes 393232 | tf_op jit(solution)/shard_map/reduce_scatter | solution.py:93
  289.4 1.9 bitcast_convert_fusion.1
  (10 shorter events, 0.1 us)
Async XLA Ops:
  7.2 2.8 copy-start
  7.2 2.7 copy-start.2
  7.2 2.7 copy-start.3
  7.2 106.0 %reduce-scatter.6.cloned.1.call-start = ((), (), s32[]{:S(2)}) async-start(), calls=%async_computation.5 | async-start | bytes 5013504 | tf_op jit(solution)/shard_map/reduce_scatter | solution.py:69
  20.7 1.1 copy-start.1
  27.0 172.8 %reduce-scatter.4.cloned.1.call-start = ((), (), s32[]{:S(2)}) async-start(), calls=%async_computation.4 | async-start | bytes 5013504 | tf_op jit(solution)/shard_map/reduce_scatter | solution.py:66
  33.9 1.4 copy-start.6
  46.1 9.8 %copy-start.4 = (s32[1,384]{1,0:T(1,128)S(1)}, s32[1,384]{1,0:T(1,128)}, u32[]{:S(2)}) copy-start(s32[1,384]{1,0:T(1,128)} %param.15) | copy-start | bytes 4612
  46.1 9.8 %copy-start.5 = (s32[1,384,1]{1,2,0:T(1,128)S(1)}, s32[1,384,1]{1,2,0:T(1,128)}, u32[]{:S(2)}) copy-start(s32[1,384,1]{1,2,0:T(1,128)} %param.14) | copy-start | bytes 4612
  47.2 25.6 %all-to-all-start = ((bf16[384,16,48]{0,2,1:T(8,128)(2,1)}), bf16[384,16,48]{0,2,1:T(8,128)(2,1)S(1)}, u32[]{:S(2)}, u32[]{:S(2)}) async-start(bf16[384,16,48]{0,2,1:T(8,128)(2,1)} %bitcast.8), calls=%async_computation.2 | async-start | bytes 1179648 | tf_op jit(solution)/shard_map/all_to_all | solution.py:76
  55.6 233.8 %reduce-scatter.8.cloned.1.call-start = ((), (), s32[]{:S(2)}) async-start(), calls=%async_computation.6 | async-start | bytes 6684672 | tf_op jit(solution)/shard_map/reduce_scatter | solution.py:93
Sparse Core Ops, SparseCore 0:
  27.1 85.9 reduce-scatter.5
  116.8 82.9 reduce-scatter.3
  203.6 85.7 reduce-scatter.7
where the time goes:
time: 298 us
  waiting for transfers between devices  224 us (75%)
  matrix products  38.2 us (13%)
  between operations  13.9 us (5%)
  other arithmetic  9.46 us (3%)
  starting transfers between devices  8.73 us (3%)
  local copies, waits for them, and re-layouts  3.64 us (1%)
    reduce_scatter x1, waiting for transfers between devices, per_device(): lax.psum_scatter(local_table.astype(jnp.bfloat16), 'dp', scatter_dimensio...  87.7 us
    reduce_scatter x1, waiting for transfers between devices, per_device(): lax.psum_scatter(up_whole.astype(jnp.bfloat16), 'dp', scatter_dimension=0...  84.9 us
    reduce_scatter x1, waiting for transfers between devices, per_device(): lax.psum_scatter(down_whole.astype(jnp.bfloat16), 'dp', scatter_dimension...  34.3 us
    all_to_all x1, waiting for transfers between devices, per_device(): lax.all_to_all(grad_sum.reshape(batch_rows, pieces, width // pieces), 'to...  16.9 us
    dot_general x2, matrix products, contract_cols(): lax.dot_general(left, right, (((1,), (1,)), ((), ())), preferred_element_...  12.5 us
    dot_general x2, matrix products, contract_rows(): lax.dot_general(left, right, (((0,), (0,)), ((), ())), preferred_element_...  9.48 us
    all_to_all x1, starting transfers between devices, per_device(): lax.all_to_all(grad_sum.reshape(batch_rows, pieces, width // pieces), 'to...  8.43 us
    dot_general x1, matrix products, per_device(): pre_act = jnp.dot(hidden_in, w_up[0], preferred_element_type=jnp.float32)  6.31 us
  transfers between devices with their start and end apart: 4, of which 4 were waited for; matrix products, arithmetic and copies ran while one was open for 9% of the time, Pallas kernels for 0%

commit v1 on v0

--- a/solution.py
+++ b/solution.py
@@ -4,6 +4,8 @@
 from jax.sharding import PartitionSpec as P
 
 HOT = 256
+CAP = 56
+SEAT = 64
 
 
 EPS = 1e-05
@@ -60,16 +62,15 @@
     grad_mid = grad_wide.astype(jnp.bfloat16)
     grad_act = contract_cols(grad_mid, w_down[0])
     grad_pre = (grad_act * act_slope).astype(jnp.bfloat16)
-    up_whole = contract_rows(hidden_in, grad_pre)
-    down_whole = contract_rows(active, grad_mid)
-    grad_up, grad_down = (
-        lax.psum_scatter(
-            up_whole.astype(jnp.bfloat16), "dp", scatter_dimension=0, tiled=True
-        ).astype(jnp.float32),
-        lax.psum_scatter(
-            down_whole.astype(jnp.bfloat16), "dp", scatter_dimension=0, tiled=True
-        ).astype(jnp.float32),
+    up_whole = contract_rows(hidden_in, grad_pre).astype(jnp.bfloat16)
+    down_whole = contract_rows(active, grad_mid).astype(jnp.bfloat16)
+    up_rows, down_rows = width // owners, down_whole.shape[0] // owners
+    both = jnp.concatenate(
+        [up_whole.reshape(owners, -1, width), down_whole.reshape(owners, -1, width)], axis=1
     )
+    both = lax.psum_scatter(both, "dp", scatter_dimension=0, tiled=False).astype(jnp.float32)
+    grad_up = both[: both.shape[0] // 2].reshape(up_rows, -1)
+    grad_down = both[both.shape[0] // 2 :].reshape(down_rows, width)
     grad_hidden = contract_cols(grad_pre, w_up[0]) + grad_wide
     grad_sum = norm_back(grad_hidden * gain_first[0], normed, inv_scale).astype(jnp.bfloat16)
     pieces = lax.axis_size("token")
@@ -83,16 +84,41 @@
     embed_grad = (
         grad_sum.astype(jnp.float32) + swapped.reshape(batch_rows, width).astype(jnp.float32)
     ).astype(jnp.bfloat16)
-    owner_ids = owner_dev[0, :, 0]
-    slot_ids = slot_row[0]
-    target = owner_ids * HOT + slot_ids
+    owner_hot = (
+        lax.broadcasted_iota(jnp.int32, (owners, batch_rows), 0) == owner_dev[0, :, 0][None, :]
+    )
+    earlier = (
+        lax.broadcasted_iota(jnp.int32, (batch_rows, batch_rows), 0)
+        < lax.broadcasted_iota(jnp.int32, (batch_rows, batch_rows), 1)
+    ).astype(jnp.bfloat16)
+    ahead = jnp.dot(owner_hot.astype(jnp.bfloat16), earlier, preferred_element_type=jnp.float32)
+    rank = jnp.sum(jnp.where(owner_hot, ahead, 0.0), axis=0).astype(jnp.int32)
+    rank_hot = lax.broadcasted_iota(jnp.int32, (SEAT, batch_rows), 0) == rank[None, :]
+    slot_next = jnp.where(owner_hot, slot_row + 1, 0).astype(jnp.bfloat16)
+    slots = contract_cols(slot_next, rank_hot.astype(jnp.bfloat16))
+    seat = owner_dev[0, :, 0] * SEAT + rank
     picker = (
-        lax.broadcasted_iota(jnp.int32, (owners * HOT, batch_rows), 0) == target[None, :]
+        lax.broadcasted_iota(jnp.int32, (owners * SEAT, batch_rows), 0) == seat[None, :]
     ).astype(jnp.bfloat16)
-    local_table = jnp.dot(picker, embed_grad, preferred_element_type=jnp.float32)
-    row_grad = lax.psum_scatter(
-        local_table.astype(jnp.bfloat16), "dp", scatter_dimension=0, tiled=True
-    ).astype(jnp.float32)
+    sent = jnp.dot(picker, embed_grad, preferred_element_type=jnp.float32).astype(jnp.bfloat16)
+    sent = jnp.concatenate(
+        [
+            sent.reshape(owners, SEAT, width)[:, :CAP],
+            jnp.pad(slots.astype(jnp.bfloat16), ((0, 0), (0, width - SEAT)))[:, None, :],
+            jnp.zeros((owners, SEAT - CAP - 1, width), jnp.bfloat16),
+        ],
+        axis=1,
+    )
+    landed = lax.all_to_all(sent, "dp", split_axis=0, concat_axis=0, tiled=True)
+    slots_in = landed[:, CAP, :SEAT].astype(jnp.int32) - 1
+    placer = (
+        lax.broadcasted_iota(jnp.int32, (HOT, owners, SEAT), 0) == slots_in[None]
+    ).astype(jnp.bfloat16)
+    row_grad = jnp.dot(
+        placer.reshape(HOT, owners * SEAT),
+        landed.reshape(owners * SEAT, width),
+        preferred_element_type=jnp.float32,
+    )
     return (grad_up[None], grad_down[None], row_grad[None])
 
 

time: 298 us -> 172 us (0.58)
  waiting for transfers between devices: 224 us -> 50.9 us
  blocking collectives: 0 us -> 37.2 us
  local copies, waits for them, and re-layouts: 3.64 us -> 16.6 us
  matrix products: 38.2 us -> 31.9 us
    reduce_scatter x3 -> x0, waiting for transfers between devices: 207 us -> none  [the longest x1 87.7 us: per_device(): lax.psum_scatter(local_table.astype(jnp.bfloat16), 'dp', scatter_dimensio...]
    all_to_all x0 -> x1, blocking collectives: none -> 37.2 us  [per_device(): landed = lax.all_to_all(sent, 'dp', split_axis=0, concat_axis=0, tiled=True)]
    unnamed x3 -> x2, waiting for transfers between devices: 0.05 us -> 34.8 us
    reshape x0 -> x1, local copies, waits for them, and re-layouts: none -> 8.47 us  [per_device(): up_whole.reshape(owners, -1, width)]
    concatenate x0 -> x2, other arithmetic: none -> 8.07 us  [the longest x1 7.58 us: per_device(): jnp.concatenate([up_whole.reshape(owners, -1, width), down_whole.reshape(...]
    broadcast_in_dim x3 -> x0, other arithmetic: 5.55 us -> none  [per_device(): return (grad_up[None], grad_down[None], row_grad[None])]
    dot_general x1, matrix products: 5.52 us -> 1.01 us  [per_device(): jnp.dot(picker, embed_grad, preferred_element_type=jnp.float32)]
    dot_general x2 -> x3, matrix products: 12.5 us -> 10.9 us  [contract_cols(): lax.dot_general(left, right, (((1,), (1,)), ((), ())), preferred_element_...]
  transfers between devices with their start and end apart: 4 -> 2, of which waited for: 4 -> 2; matrix products, arithmetic and copies ran while one was open for 9% -> 7% of each run, Pallas kernels for 0% -> 0%
where the time goes in v1:
time: 172 us; the launch traced here: 171 us
  waiting for transfers between devices  50.9 us (30%)
  blocking collectives  37.2 us (22%)
  matrix products  31.9 us (19%)
  local copies, waits for them, and re-layouts  16.6 us (10%)
  between operations  14.3 us (8%)
  other arithmetic  12 us (7%)
  starting transfers between devices  8.61 us (5%)
    all_to_all x1, blocking collectives, per_device(): landed = lax.all_to_all(sent, 'dp', split_axis=0, concat_axis=0, tiled=True)  37.2 us
    unnamed x2, waiting for transfers between devices  34.8 us
    all_to_all x1, waiting for transfers between devices, per_device(): lax.all_to_all(grad_sum.reshape(batch_rows, pieces, width // pieces), 'to...  16.1 us
    dot_general x3, matrix products, contract_cols(): lax.dot_general(left, right, (((1,), (1,)), ((), ())), preferred_element_...  10.9 us
    dot_general x2, matrix products, contract_rows(): lax.dot_general(left, right, (((0,), (0,)), ((), ())), preferred_element_...  9.41 us
    all_to_all x1, starting transfers between devices, per_device(): lax.all_to_all(grad_sum.reshape(batch_rows, pieces, width // pieces), 'to...  8.57 us
    reshape x1, local copies, waits for them, and re-layouts, per_device(): up_whole.reshape(owners, -1, width)  8.47 us
    concatenate x1, other arithmetic, per_device(): jnp.concatenate([up_whole.reshape(owners, -1, width), down_whole.reshape(...  7.58 us
  transfers between devices with their start and end apart: 2, of which 2 were waited for; matrix products, arithmetic and copies ran while one was open for 7% of the time, Pallas kernels for 0%

profile of v1, /device:TPU:6, one launch (start us, length us, event | category | flops | bytes accessed | tf_op | source)
XLA Modules:
  0.0 171.5 jit_solution(2549536862575375576)
XLA Ops:
  7.2 0.0 copy-start
  7.2 0.0 copy-start.3
  7.2 0.0 copy-start.4
  7.2 0.0 reduce-scatter.4.cloned.1.call-start
  7.2 1.3 convert_reduce_fusion
  8.5 1.4 fusion.36
  9.9 0.0 copy-done.3
  9.9 0.0 copy-done.4
  10.0 0.0 copy-done
  10.0 4.3 %multiply_convert_fusion = (bf16[384,3072]{1,0:T(8,128)(2,1)S(1)}, f32[384,3072]{1,0:T(8,128)S(1)}) fusion(bf16[1,768,3072]{2,1,0:T(8,128)(2,1)} %param.10, bf16[384,1,768]{2,0,1:T(8,128)(2,1)S(1)} %copy-done, f32[768]{0:T(1024)S(1)} %reduce.1, f32[384]{0:T(512)S(1)} %add_rsqrt_fusion.1, f32[384]{0:T(512)S(1)} %broadcast_multiply_fusion.5), kind=kOutput, calls=%fused_computation.18 | convolution fusion | flops 1819312128 | bytes 12392448 | tf_op jit(solution)/shard_map/dot_general | solution.py:52
  14.3 4.4 %fusion.68 = (f32[384]{0:T(512)S(1)}, f32[384,768]{1,0:T(8,128)S(1)}) fusion(f32[768]{0:T(1024)S(1)} %reduce.1, f32[384]{0:T(512)S(1)} %add_rsqrt_fusion.1, f32[384]{0:T(512)S(1)} %broadcast_multiply_fusion.5, bf16[384,1,768]{2,0,1:T(8,128)(2,1)S(1)} %copy-done, bf16[384,3072]{1,0:T(8,128)(2,1)S(1)} %get-tuple-element.9, bf16[1,3072,768]{2,1,0:T(8,128)(2,1)} %param.11), kind=kOutput, calls=%fused_computation.92 | convolution fusion | flops 1814298240 | bytes 8855040 | tf_op jit(solution)/shard_map/dot_general | solution.py:55
  18.7 0.0 copy-start.1
  18.7 0.3 multiply_reduce_fusion
  19.0 0.8 copy-done.1
  19.8 0.0 slice-start
  19.8 0.4 fusion.42
  20.2 0.0 slice-start.1
  20.2 4.8 %convolution_convert_fusion = bf16[3072,768]{1,0:T(8,128)(2,1)} fusion(bf16[384,3072]{1,0:T(8,128)(2,1)S(1)} %get-tuple-element.9, f32[384,768]{1,0:T(8,128)S(1)} %get-tuple-element.12, bf16[384,1,768]{2,0,1:T(8,128)(2,1)S(1)} %copy-done.1, f32[384]{0:T(512)S(1)} %get-tuple-element.14, f32[384]{0:T(512)S(1)} %get-tuple-element.15, f32[768]{0:T(1024)S(1)} %reduce.2, ...), kind=kOutput, calls=%fused_computation.2 | convolution fusion | flops 1816952832 | bytes 8856576 | tf_op jit(solution)/shard_map/dot_general | solution.py:35
  25.0 0.0 slice-done
  25.0 0.0 slice-done.1
  25.0 5.3 %fusion.5 = bf16[384,3072]{1,0:T(8,128)(2,1)S(1)} fusion(f32[384,3072]{1,0:T(8,128)S(1)} %get-tuple-element.10, bf16[1,3072,768]{2,1,0:T(8,128)(2,1)S(1)} %bitcast.93, f32[384,768]{1,0:T(8,128)S(1)} %get-tuple-element.12, bf16[384,1,768]{2,0,1:T(8,128)(2,1)S(1)} %copy-done.1, f32[384]{0:T(512)S(1)} %get-tuple-element.14, f32[384]{0:T(512)S(1)} %get-tuple-element.15, ...), kind=kOutput, calls=%fused_computation.9 | convolution fusion | flops 1826390016 | bytes 13575168 | tf_op jit(solution)/shard_map/dot_general | solution.py:41
  30.4 0.0 copy-start.7
  30.4 1.4 copy-done.7
  31.8 4.6 %convolution_convert_fusion.1 = bf16[768,3072]{1,0:T(8,128)(2,1)} fusion(bf16[384,3072]{1,0:T(8,128)(2,1)S(1)} %fusion.5, bf16[384,1,768]{2,0,1:T(8,128)(2,1)S(1)} %copy-done, f32[768]{0:T(1024)S(1)} %reduce.1, f32[384]{0:T(512)S(1)} %add_rsqrt_fusion.1, f32[384]{0:T(512)S(1)} %broadcast_multiply_fusion.5), kind=kOutput, calls=%fused_computation.3 | convolution fusion | flops 1815773184 | bytes 7673856 | tf_op jit(solution)/shard_map/dot_general | solution.py:35
  36.3 8.5 %reshape.111 = bf16[16,192,768]{2,1,0:T(8,128)(2,1)} reshape(bf16[768,3072]{1,0:T(8,128)(2,1)} %convolution_convert_fusion.1) | data formatting | bytes 9437184 | tf_op jit(solution)/shard_map/reshape | solution.py:69
  44.8 7.6 %pad_maximum_fusion = bf16[16,384,768]{2,1,0:T(8,128)(2,1)} fusion(bf16[16,192,768]{2,1,0:T(8,128)(2,1)} %bitcast.89, bf16[16,192,768]{2,1,0:T(8,128)(2,1)} %reshape.111), kind=kLoop, calls=%fused_computation | loop fusion | flops 18874368 | bytes 18874368 | tf_op jit(solution)/shard_map/concatenate | solution.py:68
  52.4 0.0 reduce-scatter.4.cloned.1.call-update
  52.4 5.5 %fusion.66 = (f32[384]{0:T(512)S(1)}, f32[384]{0:T(512)S(1)}, f32[384,768]{1,0:T(8,128)S(1)}) fusion(f32[384]{0:T(512)S(1)} %add_rsqrt_fusion.1, f32[384]{0:T(512)S(1)} %broadcast_multiply_fusion.5, bf16[384,1,768]{2,0,1:T(8,128)(2,1)S(1)} %copy-done, f32[768]{0:T(1024)S(1)} %reduce.1, f32[384]{0:T(512)S(1)} %get-tuple-element.14, ...), kind=kOutput, calls=%fused_computation.90 | convolution fusion | flops 1816657152 | bytes 10635264 | tf_op jit(solution)/shard_map/dot_general | solution.py:41
  57.9 0.4 fusion.35
  58.3 0.0 copy-start.6
  58.3 0.0 copy-start.5
  58.3 1.1 copy.15
  59.4 8.6 %all-to-all-start = ((bf16[384,16,48]{0,2,1:T(8,128)(2,1)}), bf16[384,16,48]{0,2,1:T(8,128)(2,1)S(1)}, u32[]{:S(2)}, u32[]{:S(2)}) async-start(bf16[384,16,48]{0,2,1:T(8,128)(2,1)} %bitcast.6), calls=%async_computation | async-start | bytes 1179648 | tf_op jit(solution)/shard_map/all_to_all | solution.py:77
  67.9 0.0 copy-done.6
  68.0 0.2 fusion.46
  68.2 0.0 copy-done.5
  68.2 0.1 convolution_convert_fusion.3
  68.3 0.7 copy.17
  69.0 0.1 pad.7.clone
  69.1 16.1 %all-to-all-done = bf16[384,16,48]{0,2,1:T(8,128)(2,1)S(1)} async-done(((bf16[384,16,48]{0,2,1:T(8,128)(2,1)}), bf16[384,16,48]{0,2,1:T(8,128)(2,1)S(1)}, u32[]{:S(2)}, u32[]{:S(2)}) %all-to-all-start) | async-done | bytes 589856 | tf_op jit(solution)/shard_map/all_to_all | solution.py:77
  85.2 0.1 bitcast_convert_fusion
  85.3 0.4 copy.16
  85.7 1.0 convolution_convert_fusion.2
  86.7 0.0 copy-start.2
  86.7 0.1 slice.20
  86.8 0.7 copy-done.2
  87.5 0.5 maximum_maximum_fusion
  88.0 37.2 %all_to_all.10 = bf16[16,64,768]{2,1,0:T(8,128)(2,1)S(1)} all-to-all(bf16[16,64,768]{2,1,0:T(8,128)(2,1)S(1)} %maximum_maximum_fusion), channel_id=1, replica_groups=mesh['dp'=16,'token'=16] {'dp'}, dimensions={0} | all-to-all | bytes 3145728 | tf_op jit(solution)/shard_map/all_to_all | solution.py:112
  125.2 1.7 convolution_bitcast_fusion
  126.9 34.8 %reduce-scatter.4.cloned.1.call-done = bf16[1,384,768]{2,1,0:T(8,128)(2,1)} async-done(((bf16[16,384,768]{2,1,0:T(8,128)(2,1)}), bf16[1,384,768]{2,1,0:T(8,128)(2,1)}) %reduce-scatter.4.cloned.1.call-update) | async-done | bytes 589840
  161.7 1.9 %fusion.67 = (f32[1,192,768]{2,1,0:T(8,128)}, f32[1,192,768]{2,1,0:T(8,128)S(1)}) fusion(bf16[1,384,768]{2,1,0:T(8,128)(2,1)} %reduce-scatter.4.cloned.1.call-done), kind=kLoop, calls=%fused_computation.91 | loop fusion | bytes 2359296 | tf_op jit(solution)/shard_map/slice | solution.py:73
  163.7 1.0 broadcast_in_dim_reshape.3
  (17 shorter events, 0.1 us)
Async XLA Ops:
  7.2 2.8 %copy-start = (bf16[384,1,768]{2,0,1:T(8,128)(2,1)S(1)}, bf16[384,1,768]{2,0,1:T(8,128)(2,1)}, u32[]{:S(2)}) copy-start(bf16[384,1,768]{2,0,1:T(8,128)(2,1)} %param.8) | copy-start | bytes 1769476
  7.2 2.7 %copy-start.3 = (f32[1,768]{1,0:T(1,128)S(1)}, f32[1,768]{1,0:T(1,128)}, u32[]{:S(2)}) copy-start(f32[1,768]{1,0:T(1,128)} %param.12) | copy-start | bytes 9220
  7.2 2.7 %copy-start.4 = (f32[1,768]{1,0:T(1,128)S(1)}, f32[1,768]{1,0:T(1,128)}, u32[]{:S(2)}) copy-start(f32[1,768]{1,0:T(1,128)} %param.13) | copy-start | bytes 9220
  7.2 154.5 %reduce-scatter.4.cloned.1.call-start = ((), (), s32[]{:S(2)}) async-start(), calls=%async_computation.3 | async-start | bytes 10027008
  18.7 1.1 copy-start.1
  19.8 5.3 %slice-start = ((s8[4718592]{0:T(1024)(128)(4,1)}), s8[4194304]{0:T(1024)(128)(4,1)S(1)}, s32[]{:S(2)}) async-start(s8[4718592]{0:T(1024)(128)(4,1)} %bitcast.92), calls=%async_computation.4 | async-start | bytes 8388608
  20.2 4.8 %slice-start.1 = ((s8[4718592]{0:T(1024)(128)(4,1)}), s8[524288]{0:T(1024)(128)(4,1)S(1)}, s32[]{:S(2)}) async-start(s8[4718592]{0:T(1024)(128)(4,1)} %bitcast.92), calls=%async_computation.5 | async-start | bytes 1048576
  30.4 1.4 copy-start.7
  58.3 9.7 %copy-start.6 = (s32[1,384,1]{1,2,0:T(1,128)S(1)}, s32[1,384,1]{1,2,0:T(1,128)}, u32[]{:S(2)}) copy-start(s32[1,384,1]{1,2,0:T(1,128)} %param.14) | copy-start | bytes 4612
  58.3 9.9 %copy-start.5 = (s32[1,384]{1,0:T(1,128)S(1)}, s32[1,384]{1,0:T(1,128)}, u32[]{:S(2)}) copy-start(s32[1,384]{1,0:T(1,128)} %param.15) | copy-start | bytes 4612
  59.4 25.8 %all-to-all-start = ((bf16[384,16,48]{0,2,1:T(8,128)(2,1)}), bf16[384,16,48]{0,2,1:T(8,128)(2,1)S(1)}, u32[]{:S(2)}, u32[]{:S(2)}) async-start(bf16[384,16,48]{0,2,1:T(8,128)(2,1)} %bitcast.6), calls=%async_computation | async-start | bytes 1179648 | tf_op jit(solution)/shard_map/all_to_all | solution.py:77
  86.7 0.8 copy-start.2
Sparse Core Ops, SparseCore 0:
  52.5 109.1 reduce-scatter.3

commit v2 on v0

v2 whole, which is shorter than its diff:
```python
import functools

import jax
import jax.numpy as jnp
from jax import lax
from jax.experimental import pallas as pl
from jax.experimental.pallas import tpu as pltpu
from jax.sharding import PartitionSpec as P

HOT = 256
CAP = 56
SEAT = 64
SIDE = 4
BLOCK = 48
ROWS = 16

EPS = 1e-05
HALF_ROOT = 0.7071067811865476
INV_ROOT_TAU = 0.3989422804014327
F32 = jnp.float32
BF16 = jnp.bfloat16

ROLE = ((6, 4, 0, 3), (7, 1, 2, 5))


def normalize(values):
    center = values - jnp.mean(values, axis=-1, keepdims=True)
    inv_scale = lax.rsqrt(jnp.mean(center * center, axis=-1, keepdims=True) + EPS)
    return (center * inv_scale, inv_scale)


def norm_back(grad_norm, normed, inv_scale):
    mean_grad = jnp.mean(grad_norm, axis=-1, keepdims=True)
    mean_proj = jnp.mean(grad_norm * normed, axis=-1, keepdims=True)
    return inv_scale * (grad_norm - mean_grad - normed * mean_proj)


def gelu_parts(pre_act):
    cumul = 0.5 * (1.0 + lax.erf(pre_act * HALF_ROOT))
    density = jnp.exp(-0.5 * pre_act * pre_act) * INV_ROOT_TAU
    return (pre_act * cumul, cumul + pre_act * density)


def contract_rows(left, right):
    return lax.dot_general(left, right, (((0,), (0,)), ((), ())), preferred_element_type=F32)


def contract_cols(left, right):
    return lax.dot_general(left, right, (((1,), (1,)), ((), ())), preferred_element_type=F32)


def send_out(stage, outs, sems):
    copies = [
        pltpu.make_async_copy(stage.at[pl.ds(8 * k, 8)], out, sems.at[k])
        for k, out in enumerate(outs)
    ]
    for copy in copies:
        copy.start()
    for copy in copies:
        copy.wait()


def forward_kernel(dest, mix, out_grad, w_up, w_down, gain_first, gain_second, *refs):
    hidden, slope, grad_wide, grad_mid = refs[:4]
    outs, (active, stage, sems) = refs[4:12], refs[12:]
    step = pl.program_id(0)

    @pl.when(step == 0)
    def _():
        normed, _ = normalize(mix[...].astype(F32))
        hidden[...] = (normed * gain_first[...]).astype(BF16)

    @pl.when(step < SIDE)
    def _():
        pre_act = jnp.dot(hidden[...], w_up[...], preferred_element_type=F32)
        act_value, act_slope = gelu_parts(pre_act)
        act_value = act_value.astype(BF16)
        active[step] = act_value
        slope[0] = act_slope
        part = jnp.dot(act_value, w_down[...], preferred_element_type=F32)

        @pl.when(step == 0)
        def _():
            grad_wide[...] = part + hidden[...].astype(F32)

        @pl.when(step > 0)
        def _():
            grad_wide[...] += part

    @pl.when(step == SIDE - 1)
    def _():
        normed_out, inv_out = normalize(grad_wide[...])
        wide = norm_back(out_grad[...].astype(F32) * gain_second[...], normed_out, inv_out)
        grad_wide[...] = wide
        grad_mid[...] = wide.astype(BF16)

    @pl.when(step >= SIDE)
    def _():
        part = contract_rows(active[step - SIDE], grad_mid[...]).astype(BF16)
        for k in range(16):
            stage[dest[(step - SIDE) * 16 + k]] = part[k * BLOCK : (k + 1) * BLOCK]

    @pl.when(step == 2 * SIDE - 1)
    def _():
        send_out(stage, outs, sems)


def backward_kernel(
    dest, mix, hidden, slope, grad_wide, grad_mid, w_up, w_down, gain_first, *refs
):
    grad_sum, outs = refs[0], refs[1:9]
    turned, grad_hidden, stage, sems = refs[9:]
    step = pl.program_id(0)

    @pl.when(step == 0)
    def _():
        turned[...] = hidden[...].T

    grad_act = contract_cols(grad_mid[...], w_down[...])
    grad_pre = (grad_act * slope[0]).astype(BF16)
    part = jnp.dot(turned[...], grad_pre, preferred_element_type=F32).astype(BF16)
    for k in range(16):
        stage[dest[k * 4 + step]] = part[k * BLOCK : (k + 1) * BLOCK]
    part = contract_cols(grad_pre, w_up[...])

    @pl.when(step == 0)
    def _():
        grad_hidden[...] = part + grad_wide[...]

    @pl.when(step > 0)
    def _():
        grad_hidden[...] += part

    @pl.when(step == SIDE - 1)
    def _():
        normed, inv_scale = normalize(mix[...].astype(F32))
        total = norm_back(grad_hidden[...] * gain_first[...], normed, inv_scale)
        grad_sum[...] = total.T.astype(BF16)
        send_out(stage, outs, sems)


def seat_kernel(grad_sum, swapped, owner, slot, sent):
    owners, rows = sent.shape[0], owner.shape[1]
    width = sent.shape[2]
    iota = functools.partial(lax.broadcasted_iota, jnp.int32)
    embed = (grad_sum[...].astype(F32) + swapped[...].astype(F32)).astype(BF16)
    owner_hot = iota((owners, rows), 0) == owner[...]
    earlier = (iota((rows, rows), 0) < iota((rows, rows), 1)).astype(F32).astype(BF16)
    ahead = jnp.dot(
        owner_hot.astype(F32).astype(BF16), earlier, preferred_element_type=F32
    )
    rank = jnp.sum(jnp.where(owner_hot, ahead, 0.0), axis=0, keepdims=True).astype(jnp.int32)
    rank_hot = (iota((width, rows), 0) == rank).astype(F32).astype(BF16)
    slot_next = jnp.where(owner_hot, (slot[...] + 1).astype(F32), 0.0).astype(BF16)
    slots = contract_cols(slot_next, rank_hot)
    seat = owner[...] * SEAT + rank
    picker = (iota((owners * SEAT, rows), 0) == seat).astype(F32).astype(BF16)
    chosen = contract_cols(picker, embed).reshape(owners, SEAT, width)
    at_cap = iota((1, SEAT, 1), 1) == CAP
    sent[...] = jnp.where(at_cap, slots[:, None, :], chosen).astype(BF16)


def add(*refs):
    total = refs[0].astype(F32)
    for ref in refs[1:]:
        total = total + ref.astype(F32)
    return total


def first_kernel(*refs):
    ins, outs = refs[:-4], refs[-4:]
    for axis in range(2):
        for mat in range(2):
            keep, up, down = ins[(axis * 2 + mat) * 3 : (axis * 2 + mat) * 3 + 3]
            rows = pl.ds(mat * SIDE, SIDE)
            outs[axis * 2][rows] = add(keep[:SIDE], up[...]).astype(BF16)
            outs[axis * 2 + 1][rows] = add(keep[SIDE:], down[...]).astype(BF16)


def second_kernel(*refs):
    ins, outs = refs[:-8], refs[-8:]
    for axis in range(2):
        up2, down2, mid2, keep2 = outs[axis * 4 : axis * 4 + 4]
        here = ins[axis * 8 : axis * 8 + 8]
        for mat in range(2):
            keep, up, down = here[mat * 3 : mat * 3 + 3]
            rows = slice(mat * SIDE, (mat + 1) * SIDE)
            low = add(keep[:SIDE], down[...], here[6][rows])
            high = add(keep[SIDE:], up[...], here[7][rows])
            up2[2 * mat] = low[2].astype(BF16)
            up2[2 * mat + 1] = high[1].astype(BF16)
            down2[2 * mat] = high[2].astype(BF16)
            down2[2 * mat + 1] = low[3].astype(BF16)
            mid2[2 * mat] = low[1].astype(BF16)
            mid2[2 * mat + 1] = high[3].astype(BF16)
            keep2[2 * mat] = low[0]
            keep2[2 * mat + 1] = high[0]


def third_kernel(*refs):
    ins, outs = refs[:-4], refs[-4:]
    for axis in range(2):
        mid2, up2, down2 = ins[axis * 3 : axis * 3 + 3]
        for mat in range(2):
            outs[axis * 2][mat] = add(mid2[2 * mat], up2[2 * mat]).astype(BF16)
            outs[axis * 2 + 1][mat] = add(mid2[2 * mat + 1], down2[2 * mat]).astype(BF16)


def last_kernel(*refs):
    ins, (grad_up, grad_down) = refs[:-2], refs[-2:]
    width = grad_down.shape[1]
    for axis in range(2):
        keep2, up2, down2, low2, high2 = ins[axis * 5 : axis * 5 + 5]
        for mat in range(2):
            low = add(keep2[2 * mat], down2[2 * mat + 1], low2[mat])
            high = add(keep2[2 * mat + 1], up2[2 * mat + 1], high2[mat])
            for half, value in enumerate((low, high)):
                part = 2 * axis + half
                if mat == 0:
                    grad_down[part * BLOCK : (part + 1) * BLOCK, :] = value
                else:
                    grad_up[:, part * width : (part + 1) * width] = value


def moves(axis, sign):
    pairs = []
    for index in range(SIDE * SIDE):
        y, x = divmod(index, SIDE)
        if axis == 0:
            x = (x + sign) % SIDE
        else:
            y = (y + sign) % SIDE
        pairs.append((index, y * SIDE + x))
    return pairs


def shift(value, axis, sign):
    return lax.ppermute(value, "dp", moves(axis, sign))


def block_places():
    me = lax.axis_index("dp")
    flat = jnp.arange(SIDE * SIDE * 4, dtype=jnp.int32)
    owner, part = flat // 4, flat % 4
    away_x = (owner % SIDE - me % SIDE) % SIDE
    away_y = (owner // SIDE - me // SIDE) % SIDE
    axis, half = part // 2, part % 2
    first = jnp.where(axis == 0, away_x, away_y)
    inner = jnp.where(axis == 0, away_y, away_x)
    role = jnp.zeros_like(flat)
    for h in range(2):
        for d in range(SIDE):
            role = jnp.where((half == h) & (first == d), ROLE[h][d], role)
    return (axis * 8 + role) * SIDE + inner


def params(*semantics, limit=60):
    return pltpu.CompilerParams(
        dimension_semantics=semantics or None, vmem_limit_bytes=limit * 1024 * 1024
    )


def cost(flops, size):
    return pl.CostEstimate(flops=flops, bytes_accessed=size, transcendentals=0)


def whole(shape):
    return pl.BlockSpec(shape, lambda *_: (0,) * len(shape))


ANY = pl.BlockSpec(memory_space=pl.ANY)


def per_device(mix_input, out_grad, w_up, w_down, gain_first, gain_second, owner_dev, slot_row):
    rows, _, width = mix_input.shape
    hidden_units = w_up.shape[2]
    chunk = hidden_units // SIDE
    owners = lax.axis_size("dp")
    pieces = lax.axis_size("token")
    mix, out_g = mix_input.reshape(rows, width), out_grad.reshape(rows, width)
    up_mat, down_mat = w_up[0], w_down[0]
    dest = block_places()
    group = jax.ShapeDtypeStruct((8, BLOCK, width), BF16)
    tall = whole((rows, width))
    gain = whole((1, width))
    clamp = lambda i: jnp.minimum(i, SIDE - 1)
    stage = [pltpu.VMEM((64, BLOCK, width), BF16), pltpu.SemaphoreType.DMA((8,))]
    matmul = 2 * rows * width * hidden_units
    hidden, slope, grad_wide, grad_mid, *down_parts = pl.pallas_call(
        forward_kernel,
        grid_spec=pltpu.PrefetchScalarGridSpec(
            num_scalar_prefetch=1,
            grid=(2 * SIDE,),
            in_specs=[
                tall,
                tall,
                pl.BlockSpec((width, chunk), lambda i, _: (0, clamp(i))),
                pl.BlockSpec((chunk, width), lambda i, _: (clamp(i), 0)),
                gain,
                gain,
            ],
            out_specs=[
                tall,
                pl.BlockSpec((1, rows, chunk), lambda i, _: (clamp(i), 0, 0)),
                tall,
                tall,
            ]
            + [ANY] * 8,
            scratch_shapes=[pltpu.VMEM((SIDE, rows, chunk), BF16)] + stage,
        ),
        out_shape=[
            jax.ShapeDtypeStruct((rows, width), BF16),
            jax.ShapeDtypeStruct((SIDE, rows, chunk), F32),
            jax.ShapeDtypeStruct((rows, width), F32),
            jax.ShapeDtypeStruct((rows, width), BF16),
        ]
        + [group] * 8,
        compiler_params=params("arbitrary"),
        cost_estimate=cost(3 * matmul, 25_000_000),
    )(dest, mix, out_g, up_mat, down_mat, gain_first, gain_second)

    down_got = [
        (shift(down_parts[4 * a], a, 1), shift(down_parts[4 * a + 1], a, -1)) for a in range(2)
    ]

    grad_sum, *up_parts = pl.pallas_call(
        backward_kernel,
        grid_spec=pltpu.PrefetchScalarGridSpec(
            num_scalar_prefetch=1,
            grid=(SIDE,),
            in_specs=[
                tall,
                tall,
                pl.BlockSpec((1, rows, chunk), lambda i, _: (i, 0, 0)),
                tall,
                tall,
                pl.BlockSpec((width, chunk), lambda i, _: (0, i)),
                pl.BlockSpec((chunk, width), lambda i, _: (i, 0)),
                gain,
            ],
            out_specs=[whole((width, rows))] + [ANY] * 8,
            scratch_shapes=[pltpu.VMEM((width, rows), BF16), pltpu.VMEM((rows, width), F32)]
            + stage,
        ),
        out_shape=[jax.ShapeDtypeStruct((width, rows), BF16)] + [group] * 8,
        compiler_params=params("arbitrary"),
        cost_estimate=cost(3 * matmul, 25_000_000),
    )(dest, mix, hidden, slope, grad_wide, grad_mid, up_mat, down_mat, gain_first)

    leaving = [up_parts[k] for k in (0, 1, 4, 5)]
    leaving, grad_sum, down_got = lax.optimization_barrier((leaving, grad_sum, down_got))
    up_parts = [*leaving[:2], *up_parts[2:4], *leaving[2:], *up_parts[6:]]
    up_got = [(shift(up_parts[4 * a], a, 1), shift(up_parts[4 * a + 1], a, -1)) for a in range(2)]

    swapped = lax.all_to_all(
        grad_sum.reshape(pieces, width // pieces, rows),
        "token",
        split_axis=0,
        concat_axis=0,
        tiled=True,
    ).reshape(width, rows)

    mats = ((down_parts, down_got), (up_parts, up_got))

    def lines(count, part=0):
        return pl.BlockSpec((count, ROWS, width), lambda i: (part, i, 0))

    def combine(kernel, specs, args, counts, dtypes, name):
        return pl.pallas_call(
            kernel,
            grid=(BLOCK // ROWS,),
            in_specs=specs,
            out_specs=[lines(n) for n in counts],
            out_shape=[
                jax.ShapeDtypeStruct((n, BLOCK, width), t) for n, t in zip(counts, dtypes)
            ],
            compiler_params=params("arbitrary"),
            cost_estimate=cost(1_000_000, 7_000_000),
            name=name,
        )(*args)

    args, specs = [], []
    for a in range(2):
        for parts, got in mats:
            args += [parts[4 * a + 2], *got[a]]
            specs += [lines(8), lines(4), lines(4)]
    both = combine(first_kernel, specs, args, [8] * 4, [BF16] * 4, "first_sums")
    both_got = [shift(both[2 * a + s], a, 1 - 2 * s) for a in range(2) for s in range(2)]

    swapped, _ = lax.optimization_barrier((swapped, both))
    sent = pl.pallas_call(
        seat_kernel,
        out_shape=jax.ShapeDtypeStruct((owners, SEAT, width), BF16),
        compiler_params=params(),
        cost_estimate=cost(2 * owners * SEAT * rows * width, 4_000_000),
    )(grad_sum, swapped, owner_dev.reshape(1, rows), slot_row)
    landed = lax.all_to_all(sent, "dp", split_axis=0, concat_axis=0, tiled=True)

    args, specs = [], []
    for a in range(2):
        for parts, got in mats:
            args += [parts[4 * a + 3], *got[a]]
            specs += [lines(8), lines(4, 1), lines(4, 1)]
        args += both_got[2 * a : 2 * a + 2]
        specs += [lines(8), lines(8)]
    second = combine(
        second_kernel, specs, args, [4] * 8, [BF16, BF16, BF16, F32] * 2, "second_sums"
    )
    second_got = [shift(second[4 * a + s], 1 - a, 1 - 2 * s) for a in range(2) for s in range(2)]

    args = []
    for a in range(2):
        args += [second[4 * a + 2], *second_got[2 * a : 2 * a + 2]]
    third = combine(third_kernel, [lines(4)] * 6, args, [2] * 4, [BF16] * 4, "third_sums")
    third_got = [shift(third[2 * a + s], 1 - a, 1 - 2 * s) for a in range(2) for s in range(2)]

    args = []
    for a in range(2):
        args += [second[4 * a + 3], *second_got[2 * a : 2 * a + 2], *third_got[2 * a : 2 * a + 2]]
    grad_up, grad_down = pl.pallas_call(
        last_kernel,
        out_shape=[
            jax.ShapeDtypeStruct((BLOCK, hidden_units), F32),
            jax.ShapeDtypeStruct((4 * BLOCK, width), F32),
        ],
        compiler_params=params(),
        cost_estimate=cost(1_000_000, 4_000_000),
        name="last_sums",
    )(*args)

    slots_in = landed[:, CAP, :SEAT].astype(jnp.int32) - 1
    placer = (
        lax.broadcasted_iota(jnp.int32, (HOT, owners, SEAT), 0) == slots_in[None]
    ).astype(BF16)
    row_grad = jnp.dot(
        placer.reshape(HOT, owners * SEAT),
        landed.reshape(owners * SEAT, width),
        preferred_element_type=F32,
    )
    return (grad_up[None], grad_down[None], row_grad[None])


def solution(mesh):
    placed = (
        P("dp", "token", None),
        P("dp", "token", None),
        P("token", None, None),
        P("token", None, None),
        P("token", None),
        P("token", None),
        P("token", "dp", None),
        P("token", "dp"),
    )
    return jax.shard_map(
        per_device,
        mesh=mesh,
        in_specs=placed,
        out_specs=(P("token", "dp", None), P("token", "dp", None), P("token", "dp", None)),
        check_vma=False,
    )
```

time: 298 us -> 154 us (0.52)
  waiting for transfers between devices: 224 us -> 52.2 us
  Pallas kernels: 0 us -> 53.2 us
  matrix products: 38.2 us -> 1.68 us
  starting transfers between devices: 8.73 us -> 41.8 us
  between operations: 13.9 us -> 0.84 us
  other arithmetic: 9.46 us -> 0.61 us
    reduce_scatter x3 -> x0, waiting for transfers between devices: 207 us -> none  [the longest x1 87.7 us: per_device(): lax.psum_scatter(local_table.astype(jnp.bfloat16), 'dp', scatter_dimensio...]
    pallas_call x0 -> x7, Pallas kernels: none -> 53.2 us  [the longest x1 18.2 us: per_device(): pl.pallas_call(forward_kernel, grid_spec=pltpu.PrefetchScalarGridSpec(num...]
    ppermute x0 -> x20, waiting for transfers between devices: none -> 52.1 us  [shift(): return lax.ppermute(value, 'dp', moves(axis, sign))]
    dot_general x7 -> x1, matrix products: 38.2 us -> 1.68 us  [per_device(): jnp.dot(placer.reshape(HOT, owners * SEAT), landed.reshape(owners * SEAT,...]
    ppermute x0 -> x20, starting transfers between devices: none -> 26.8 us  [shift(): return lax.ppermute(value, 'dp', moves(axis, sign))]
    all_to_all x1 -> x2, waiting for transfers between devices: 16.9 us -> 0.01 us  [the longest x1 0.01 us: per_device(): lax.all_to_all(grad_sum.reshape(pieces, width // pieces, rows), 'token',...]
    all_to_all x1 -> x2, starting transfers between devices: 8.43 us -> 15 us  [the longest x1 8.44 us: per_device(): lax.all_to_all(grad_sum.reshape(pieces, width // pieces, rows), 'token',...]
    broadcast_in_dim x3 -> x0, other arithmetic: 5.55 us -> none  [per_device(): return (grad_up[None], grad_down[None], row_grad[None])]
  transfers between devices with their start and end apart: 4 -> 22, of which waited for: 4 -> 11; matrix products, arithmetic and copies ran while one was open for 9% -> 0% of each run, Pallas kernels for 0% -> 20%
where the time goes in v2:
time: 154 us; the launch traced here: 153 us
  Pallas kernels  53.2 us (35%)
  waiting for transfers between devices  52.2 us (34%)
  starting transfers between devices  41.8 us (27%)
  local copies, waits for them, and re-layouts  2.86 us (2%)
  matrix products  1.68 us (1%)
    ppermute x20, waiting for transfers between devices, shift(): return lax.ppermute(value, 'dp', moves(axis, sign))  52.1 us
    ppermute x20, starting transfers between devices, shift(): return lax.ppermute(value, 'dp', moves(axis, sign))  26.8 us
    pallas_call x1, Pallas kernels, per_device(): pl.pallas_call(forward_kernel, grid_spec=pltpu.PrefetchScalarGridSpec(num...  18.2 us
    pallas_call x1, Pallas kernels, per_device(): pl.pallas_call(backward_kernel, grid_spec=pltpu.PrefetchScalarGridSpec(nu...  14.7 us
    pallas_call x3, Pallas kernels, combine(): pl.pallas_call(kernel, grid=(BLOCK // ROWS,), in_specs=specs, out_specs=[...  13.6 us
    all_to_all x1, starting transfers between devices, per_device(): lax.all_to_all(grad_sum.reshape(pieces, width // pieces, rows), 'token',...  8.44 us
    all_to_all x1, starting transfers between devices, per_device(): landed = lax.all_to_all(sent, 'dp', split_axis=0, concat_axis=0, tiled=True)  6.57 us
    pallas_call x1, Pallas kernels, per_device(): pl.pallas_call(seat_kernel, out_shape=jax.ShapeDtypeStruct((owners, SEAT,...  3.75 us
  transfers between devices with their start and end apart: 22, of which 11 were waited for; matrix products, arithmetic and copies ran while one was open for 0% of the time, Pallas kernels for 20%

profile of v2, /device:TPU:6, one launch (start us, length us, event | category | flops | bytes accessed | tf_op | source)
XLA Modules:
  0.0 153.1 jit_solution(6778299971491924395)
XLA Ops:
  0.6 0.6 fusion.2.dest
  1.2 18.2 %shard_map.103 = (bf16[384,768]{1,0:T(8,128)(2,1)}, f32[4,384,768]{2,1,0:T(8,128)}, f32[384,768]{1,0:T(8,128)}, bf16[384,768]{1,0:T(8,128)(2,1)}, bf16[8,48,768]...) custom-call(s32[64]{0:T(128)} %fusion.2.dest, ...), custom_call_target="tpu_custom_call" | custom-call | flops 5435817984 | bytes 25000000 | tf_op jit(solution)/shard_map/pallas_call | solution.py:289
  19.4 2.3 %collective-permute-start = (bf16[8,48,768]{2,1,0:T(8,128)(2,1)}, bf16[8,48,768]{2,1,0:T(8,128)(2,1)S(1)}, u32[]{:S(2)}, u32[]{:S(2)}) collective-permute-start(bf16[8,48,768]{2,1,0:T(8,128)(2,1)} %get-tuple-element.62), channel_id=1, source_target_pairs={{0,16},{16,32},{32,48},{48,0},{64,80},{80,96},{96,112},{112,64},{1... | collective-permute-start | bytes 1769480 | tf_op jit(solution)/shard_map/ppermute | solution.py:238
  21.7 0.0 collective-permute-start.1
  21.7 1.4 collective-permute-start.2
  23.1 1.9 %collective-permute-start.3 = (bf16[8,48,768]{2,1,0:T(8,128)(2,1)}, bf16[8,48,768]{2,1,0:T(8,128)(2,1)S(1)}, u32[]{:S(2)}, u32[]{:S(2)}) collective-permute-start(bf16[8,48,768]{2,1,0:T(8,128)(2,1)} %get-tuple-element.65), channel_id=1, source_target_pairs={{0,192},{16,208},{32,224},{48,240},{64,0},{80,16},{96,32},{112,48}... | collective-permute-start | bytes 1769480 | tf_op jit(solution)/shard_map/ppermute | solution.py:238
  25.0 14.7 %shard_map.104 = (bf16[768,384]{1,0:T(8,128)(2,1)}, bf16[8,48,768]{2,1,0:T(8,128)(2,1)}, bf16[8,48,768]{2,1,0:T(8,128)(2,1)}, bf16[8,48,768]{2,1,0:T(8,128)(2,1)...) custom-call(s32[64]{0:T(128)} %fusion.2.dest, ...), custom_call_target="tpu_custom_call" | custom-call | flops 5435817984 | bytes 25000000 | tf_op jit(solution)/shard_map/pallas_call | solution.py:326
  39.7 0.0 collective-permute-done.refs_1_
  39.7 0.0 copy-start
  39.7 0.0 collective-permute-done.1.refs_2_
  39.7 0.0 copy-start.1
  39.7 0.0 collective-permute-done.2.refs_7_.refs_9_
  39.8 0.0 copy-start.2
  39.8 0.0 collective-permute-done.3.refs_8_.refs_10_
  39.8 0.0 copy-start.3
  39.8 8.4 %all-to-all-start = ((bf16[16,48,384]{2,1,0:T(8,128)(2,1)}), bf16[16,48,384]{2,1,0:T(8,128)(2,1)}, u32[]{:S(2)}, u32[]{:S(2)}) async-start(bf16[16,48,384]{2,1,0:T(8,128)(2,1)} %bitcast.14), calls=%async_computation | async-start | bytes 1179648 | tf_op jit(solution)/shard_map/all_to_all | solution.py:355
  48.2 1.8 %collective-permute-start.4 = (bf16[8,48,768]{2,1,0:T(8,128)(2,1)}, bf16[8,48,768]{2,1,0:T(8,128)(2,1)S(1)}, u32[]{:S(2)}, u32[]{:S(2)}) collective-permute-start(bf16[8,48,768]{2,1,0:T(8,128)(2,1)} %get-tuple-element.69), channel_id=1, source_target_pairs={{0,16},{16,32},{32,48},{48,0},{64,80},{80,96},{96,112},{112,64},{1... | collective-permute-start | bytes 1769480 | tf_op jit(solution)/shard_map/ppermute | solution.py:238
  50.0 0.3 collective-permute-start.5
  50.3 0.4 collective-permute-start.6
  50.7 2.9 %collective-permute-start.7 = (bf16[8,48,768]{2,1,0:T(8,128)(2,1)}, bf16[8,48,768]{2,1,0:T(8,128)(2,1)}, u32[]{:S(2)}, u32[]{:S(2)}) collective-permute-start(bf16[8,48,768]{2,1,0:T(8,128)(2,1)} %get-tuple-element.78), channel_id=1, source_target_pairs={{0,192},{16,208},{32,224},{48,240},{64,0},{80,16},{96,32},{112,48}... | collective-permute-start | bytes 1769480 | tf_op jit(solution)/shard_map/ppermute | solution.py:238
  53.6 10.5 %collective-permute-done.4.refs_4_ = bf16[8,48,768]{2,1,0:T(8,128)(2,1)S(1)} collective-permute-done((bf16[8,48,768]{2,1,0:T(8,128)(2,1)}, bf16[8,48,768]{2,1,0:T(8,128)(2,1)S(1)}, u32[]{:S(2)}, u32[]{:S(2)}) %collective-permute-start.4) | collective-permute-done | bytes 589856 | tf_op jit(solution)/shard_map/ppermute | solution.py:238
  64.0 2.6 %collective-permute-done.5.refs_5_ = bf16[8,48,768]{2,1,0:T(8,128)(2,1)S(1)} collective-permute-done((bf16[8,48,768]{2,1,0:T(8,128)(2,1)}, bf16[8,48,768]{2,1,0:T(8,128)(2,1)S(1)}, u32[]{:S(2)}, u32[]{:S(2)}) %collective-permute-start.5) | collective-permute-done | bytes 589856 | tf_op jit(solution)/shard_map/ppermute | solution.py:238
  66.7 0.2 collective-permute-done.6.refs_10_.refs_12_
  66.8 0.0 collective-permute-done.7.refs_11_.refs_13_
  66.8 0.0 copy-done
  66.8 0.0 copy-done.1
  66.8 0.0 copy-done.2
  66.9 0.6 copy-done.5
  67.5 4.7 %first_sums.1 = (bf16[8,48,768]{2,1,0:T(8,128)(2,1)}, bf16[8,48,768]{2,1,0:T(8,128)(2,1)}, bf16[8,48,768]{2,1,0:T(8,128)(2,1)}, bf16[8,48,768]{2,1,0:T(8,128)(2,1)}) custom-call(bf16[8,48,768]{2,1,0:T(8,128)(2,1)} %get-tuple-element.71.refs_0_, bf16[8,48,768]{2,1,0:T(8,128)(2,1)} %copy-done, bf16[8,48,768]{2,1,0:T(8,128)(2,1)} %copy-done.1, ...), custom_call_target="tpu_custom_call" | custom-call | flops 1000000 | bytes 7000000 | tf_op jit(solution)/shard_map/first_sums/pallas_call | solution.py:369
  72.2 0.0 all-to-all-done
  72.2 3.8 %shard_map.105 = bf16[16,64,768]{2,1,0:T(8,128)(2,1)} custom-call(bf16[768,384]{1,0:T(8,128)(2,1)} %get-tuple-element.99.grad_sum, bf16[768,384]{1,0:T(8,128)(2,1)} %bitcast.7.swapped, s32[1,384]{1,0:T(1,128)} %bitcast.16, s32[1,384]{1,0:T(1,128)} %slot.1), custom_call_target="tpu_custom_call" | custom-call | flops 603979776 | bytes 4000000 | tf_op jit(solution)/shard_map/pallas_call | solution.py:391
  76.0 6.6 %all-to-all-start.1 = ((bf16[16,64,768]{2,1,0:T(8,128)(2,1)}), bf16[16,64,768]{2,1,0:T(8,128)(2,1)S(1)}, u32[]{:S(2)}, u32[]{:S(2)}) async-start(bf16[16,64,768]{2,1,0:T(8,128)(2,1)} %shard_map.105), calls=%async_computation.1 | async-start | bytes 3145728 | tf_op jit(solution)/shard_map/all_to_all | solution.py:397
  82.6 0.2 collective-permute-start.8
  82.7 1.8 %collective-permute-start.9 = (bf16[8,48,768]{2,1,0:T(8,128)(2,1)}, bf16[8,48,768]{2,1,0:T(8,128)(2,1)S(1)}, u32[]{:S(2)}, u32[]{:S(2)}) collective-permute-start(bf16[8,48,768]{2,1,0:T(8,128)(2,1)} %get-tuple-element.80), channel_id=1, source_target_pairs={{0,48},{16,0},{32,16},{48,32},{64,112},{80,64},{96,80},{112,96},{1... | collective-permute-start | bytes 1769480 | tf_op jit(solution)/shard_map/ppermute | solution.py:238
  84.6 1.5 collective-permute-start.10
  86.1 1.8 %collective-permute-start.11 = (bf16[8,48,768]{2,1,0:T(8,128)(2,1)}, bf16[8,48,768]{2,1,0:T(8,128)(2,1)}, u32[]{:S(2)}, u32[]{:S(2)}) collective-permute-start(bf16[8,48,768]{2,1,0:T(8,128)(2,1)} %get-tuple-element.84), channel_id=1, source_target_pairs={{0,192},{16,208},{32,224},{48,240},{64,0},{80,16},{96,32},{112,48}... | collective-permute-start | bytes 1769480 | tf_op jit(solution)/shard_map/ppermute | solution.py:238
  87.8 24.2 %collective-permute-done.8.refs_6_ = bf16[8,48,768]{2,1,0:T(8,128)(2,1)S(1)} collective-permute-done((bf16[8,48,768]{2,1,0:T(8,128)(2,1)}, bf16[8,48,768]{2,1,0:T(8,128)(2,1)S(1)}, u32[]{:S(2)}, u32[]{:S(2)}) %collective-permute-start.8) | collective-permute-done | bytes 589856 | tf_op jit(solution)/shard_map/ppermute | solution.py:238
  112.0 0.0 collective-permute-done.9.refs_7_
  112.0 1.8 %collective-permute-done.10.refs_14_ = bf16[8,48,768]{2,1,0:T(8,128)(2,1)S(1)} collective-permute-done((bf16[8,48,768]{2,1,0:T(8,128)(2,1)}, bf16[8,48,768]{2,1,0:T(8,128)(2,1)S(1)}, u32[]{:S(2)}, u32[]{:S(2)}) %collective-permute-start.10) | collective-permute-done | bytes 589856 | tf_op jit(solution)/shard_map/ppermute | solution.py:238
  113.8 0.0 collective-permute-done.11.refs_15_
  113.8 0.8 copy-done.12
  114.6 5.7 %second_sums.1 = (bf16[4,48,768]{2,1,0:T(8,128)(2,1)}, bf16[4,48,768]{2,1,0:T(8,128)(2,1)}, bf16[4,48,768]{2,1,0:T(8,128)(2,1)}, f32[4,48,768]{2,1,0:T(8,128)}, ...) custom-call(bf16[8,48,768]{2,1,0:T(8,128)(2,1)} %get-tuple-element.5, ...), custom_call_target="tpu_custom_call" | custom-call | flops 1000000 | bytes 7000000 | tf_op jit(solution)/shard_map/second_sums/pallas_call | solution.py:369
  120.3 0.2 collective-permute-start.12
  120.5 3.1 %collective-permute-start.13 = (bf16[4,48,768]{2,1,0:T(8,128)(2,1)}, bf16[4,48,768]{2,1,0:T(8,128)(2,1)S(1)}, u32[]{:S(2)}, u32[]{:S(2)}) collective-permute-start(bf16[4,48,768]{2,1,0:T(8,128)(2,1)} %get-tuple-element.87), channel_id=1, source_target_pairs={{0,192},{16,208},{32,224},{48,240},{64,0},{80,16},{96,32},{112,48}... | collective-permute-start | bytes 884744 | tf_op jit(solution)/shard_map/ppermute | solution.py:238
  123.6 0.9 collective-permute-start.14
  124.5 1.1 collective-permute-start.15
  125.6 3.8 %collective-permute-done.12.refs_1_ = bf16[4,48,768]{2,1,0:T(8,128)(2,1)S(1)} collective-permute-done((bf16[4,48,768]{2,1,0:T(8,128)(2,1)}, bf16[4,48,768]{2,1,0:T(8,128)(2,1)S(1)}, u32[]{:S(2)}, u32[]{:S(2)}) %collective-permute-start.12) | collective-permute-done | bytes 294944 | tf_op jit(solution)/shard_map/ppermute | solution.py:238
  129.4 0.0 collective-permute-done.13.refs_2_
  129.4 1.5 collective-permute-done.14.refs_4_.refs_6_
  130.9 2.8 %collective-permute-done.15.refs_5_.refs_7_ = bf16[4,48,768]{2,1,0:T(8,128)(2,1)S(1)} collective-permute-done((bf16[4,48,768]{2,1,0:T(8,128)(2,1)}, bf16[4,48,768]{2,1,0:T(8,128)(2,1)S(1)}, u32[]{:S(2)}, u32[]{:S(2)}) %collective-permute-start.15) | collective-permute-done | bytes 294944 | tf_op jit(solution)/shard_map/ppermute | solution.py:238
  133.7 0.7 copy-done.9
  134.4 3.2 %third_sums.1 = (bf16[2,48,768]{2,1,0:T(8,128)(2,1)}, bf16[2,48,768]{2,1,0:T(8,128)(2,1)}, bf16[2,48,768]{2,1,0:T(8,128)(2,1)}, bf16[2,48,768]{2,1,0:T(8,128)(2,1)}) custom-call(bf16[4,48,768]{2,1,0:T(8,128)(2,1)} %get-tuple-element.88.refs_0_, bf16[4,48,768]{2,1,0:T(8,128)(2,1)} %copy-done.6, bf16[4,48,768]{2,1,0:T(8,128)(2,1)} %copy-done.7, ...), custom_call_target="tpu_custom_call" | custom-call | flops 1000000 | bytes 7000000 | tf_op jit(solution)/shard_map/third_sums/pallas_call | solution.py:369
  137.6 0.3 collective-permute-start.16
  137.9 3.0 %collective-permute-start.17 = (bf16[2,48,768]{2,1,0:T(8,128)(2,1)}, bf16[2,48,768]{2,1,0:T(8,128)(2,1)S(1)}, u32[]{:S(2)}, u32[]{:S(2)}) collective-permute-start(bf16[2,48,768]{2,1,0:T(8,128)(2,1)} %get-tuple-element.93), channel_id=1, source_target_pairs={{0,192},{16,208},{32,224},{48,240},{64,0},{80,16},{96,32},{112,48}... | collective-permute-start | bytes 442376 | tf_op jit(solution)/shard_map/ppermute | solution.py:238
  140.9 0.4 collective-permute-start.18
  141.3 1.7 %collective-permute-start.19 = (bf16[2,48,768]{2,1,0:T(8,128)(2,1)}, bf16[2,48,768]{2,1,0:T(8,128)(2,1)S(1)}, u32[]{:S(2)}, u32[]{:S(2)}) collective-permute-start(bf16[2,48,768]{2,1,0:T(8,128)(2,1)} %get-tuple-element.96), channel_id=1, source_target_pairs={{0,48},{16,0},{32,16},{48,32},{64,112},{80,64},{96,80},{112,96},{1... | collective-permute-start | bytes 442376 | tf_op jit(solution)/shard_map/ppermute | solution.py:238
  142.9 1.3 collective-permute-done.16.refs_3_
  144.2 0.0 collective-permute-done.17.refs_4_
  144.2 2.0 %collective-permute-done.18.refs_8_ = bf16[2,48,768]{2,1,0:T(8,128)(2,1)S(1)} collective-permute-done((bf16[2,48,768]{2,1,0:T(8,128)(2,1)}, bf16[2,48,768]{2,1,0:T(8,128)(2,1)S(1)}, u32[]{:S(2)}, u32[]{:S(2)}) %collective-permute-start.18) | collective-permute-done | bytes 147488 | tf_op jit(solution)/shard_map/ppermute | solution.py:238
  146.3 1.6 %collective-permute-done.19.refs_9_ = bf16[2,48,768]{2,1,0:T(8,128)(2,1)S(1)} collective-permute-done((bf16[2,48,768]{2,1,0:T(8,128)(2,1)}, bf16[2,48,768]{2,1,0:T(8,128)(2,1)S(1)}, u32[]{:S(2)}, u32[]{:S(2)}) %collective-permute-start.19) | collective-permute-done | bytes 147488 | tf_op jit(solution)/shard_map/ppermute | solution.py:238
  147.9 0.6 copy-done.16
  148.5 2.9 %last_sums.1 = (f32[48,3072]{1,0:T(8,128)}, f32[192,768]{1,0:T(8,128)}) custom-call(f32[4,48,768]{2,1,0:T(8,128)} %get-tuple-element.85.refs_0_, bf16[4,48,768]{2,1,0:T(8,128)(2,1)} %copy-done.6, bf16[4,48,768]{2,1,0:T(8,128)(2,1)} %copy-done.7, bf16[2,48,768]{2,1,0:T(8,128)(2,1)} %copy-done.13, bf16[2,48,768]{2,1,0:T(8,128)(2,1)} %copy-done.14, ...), custom_call_target="tpu_custom_call" | custom-call | flops 1000000 | bytes 4000000 | tf_op jit(solution)/shard_map/last_sums/pallas_call | solution.py:420
  151.4 0.0 all-to-all-done.1
  151.4 1.7 %convolution_bitcast_fusion = f32[1,256,768]{2,1,0:T(8,128)} fusion(bf16[16,64,768]{2,1,0:T(8,128)(2,1)S(1)} %all-to-all-done.1, s32[16,64]{1,0:T(8,128)S(1)} %bitcast.15), kind=kOutput, calls=%fused_computation | convolution fusion | flops 402915328 | bytes 2363392 | tf_op jit(solution)/shard_map/dot_general | solution.py:435
  (24 shorter events, 0.1 us)
Async XLA Ops:
  19.4 20.3 %collective-permute-start = (bf16[8,48,768]{2,1,0:T(8,128)(2,1)}, bf16[8,48,768]{2,1,0:T(8,128)(2,1)S(1)}, u32[]{:S(2)}, u32[]{:S(2)}) collective-permute-start(bf16[8,48,768]{2,1,0:T(8,128)(2,1)} %get-tuple-element.62), channel_id=1, source_target_pairs={{0,16},{16,32},{32,48},{48,0},{64,80},{80,96},{96,112},{112,64},{1... | collective-permute-start | bytes 1769480 | tf_op jit(solution)/shard_map/ppermute | solution.py:238
  21.7 18.0 %collective-permute-start.1 = (bf16[8,48,768]{2,1,0:T(8,128)(2,1)}, bf16[8,48,768]{2,1,0:T(8,128)(2,1)S(1)}, u32[]{:S(2)}, u32[]{:S(2)}) collective-permute-start(bf16[8,48,768]{2,1,0:T(8,128)(2,1)} %get-tuple-element.63), channel_id=1, source_target_pairs={{0,48},{16,0},{32,16},{48,32},{64,112},{80,64},{96,80},{112,96},{1... | collective-permute-start | bytes 1769480 | tf_op jit(solution)/shard_map/ppermute | solution.py:238
  21.7 18.0 %collective-permute-start.2 = (bf16[8,48,768]{2,1,0:T(8,128)(2,1)}, bf16[8,48,768]{2,1,0:T(8,128)(2,1)S(1)}, u32[]{:S(2)}, u32[]{:S(2)}) collective-permute-start(bf16[8,48,768]{2,1,0:T(8,128)(2,1)} %get-tuple-element.64), channel_id=1, source_target_pairs={{0,64},{16,80},{32,96},{48,112},{64,128},{80,144},{96,160},{112,17... | collective-permute-start | bytes 1769480 | tf_op jit(solution)/shard_map/ppermute | solution.py:238
  23.1 16.7 %collective-permute-start.3 = (bf16[8,48,768]{2,1,0:T(8,128)(2,1)}, bf16[8,48,768]{2,1,0:T(8,128)(2,1)S(1)}, u32[]{:S(2)}, u32[]{:S(2)}) collective-permute-start(bf16[8,48,768]{2,1,0:T(8,128)(2,1)} %get-tuple-element.65), channel_id=1, source_target_pairs={{0,192},{16,208},{32,224},{48,240},{64,0},{80,16},{96,32},{112,48}... | collective-permute-start | bytes 1769480 | tf_op jit(solution)/shard_map/ppermute | solution.py:238
  39.7 27.1 %copy-start = (bf16[8,48,768]{2,1,0:T(8,128)(2,1)}, bf16[8,48,768]{2,1,0:T(8,128)(2,1)S(1)}, u32[]{:S(2)}) copy-start(bf16[8,48,768]{2,1,0:T(8,128)(2,1)S(1)} %collective-permute-done.refs_1_) | copy-start | bytes 1769476
  39.7 27.1 %copy-start.1 = (bf16[8,48,768]{2,1,0:T(8,128)(2,1)}, bf16[8,48,768]{2,1,0:T(8,128)(2,1)S(1)}, u32[]{:S(2)}) copy-start(bf16[8,48,768]{2,1,0:T(8,128)(2,1)S(1)} %collective-permute-done.1.refs_2_) | copy-start | bytes 1769476
  39.8 27.1 %copy-start.2 = (bf16[8,48,768]{2,1,0:T(8,128)(2,1)}, bf16[8,48,768]{2,1,0:T(8,128)(2,1)S(1)}, u32[]{:S(2)}) copy-start(bf16[8,48,768]{2,1,0:T(8,128)(2,1)S(1)} %collective-permute-done.2.refs_7_.refs_9_) | copy-start | bytes 1769476
  39.8 27.1 %copy-start.3 = (bf16[8,48,768]{2,1,0:T(8,128)(2,1)}, bf16[8,48,768]{2,1,0:T(8,128)(2,1)S(1)}, u32[]{:S(2)}) copy-start(bf16[8,48,768]{2,1,0:T(8,128)(2,1)S(1)} %collective-permute-done.3.refs_8_.refs_10_) | copy-start | bytes 1769476
  39.8 32.5 %all-to-all-start = ((bf16[16,48,384]{2,1,0:T(8,128)(2,1)}), bf16[16,48,384]{2,1,0:T(8,128)(2,1)}, u32[]{:S(2)}, u32[]{:S(2)}) async-start(bf16[16,48,384]{2,1,0:T(8,128)(2,1)} %bitcast.14), calls=%async_computation | async-start | bytes 1179648 | tf_op jit(solution)/shard_map/all_to_all | solution.py:355
  48.2 15.8 %collective-permute-start.4 = (bf16[8,48,768]{2,1,0:T(8,128)(2,1)}, bf16[8,48,768]{2,1,0:T(8,128)(2,1)S(1)}, u32[]{:S(2)}, u32[]{:S(2)}) collective-permute-start(bf16[8,48,768]{2,1,0:T(8,128)(2,1)} %get-tuple-element.69), channel_id=1, source_target_pairs={{0,16},{16,32},{32,48},{48,0},{64,80},{80,96},{96,112},{112,64},{1... | collective-permute-start | bytes 1769480 | tf_op jit(solution)/shard_map/ppermute | solution.py:238
  50.0 16.7 %collective-permute-start.5 = (bf16[8,48,768]{2,1,0:T(8,128)(2,1)}, bf16[8,48,768]{2,1,0:T(8,128)(2,1)S(1)}, u32[]{:S(2)}, u32[]{:S(2)}) collective-permute-start(bf16[8,48,768]{2,1,0:T(8,128)(2,1)} %get-tuple-element.70), channel_id=1, source_target_pairs={{0,48},{16,0},{32,16},{48,32},{64,112},{80,64},{96,80},{112,96},{1... | collective-permute-start | bytes 1769480 | tf_op jit(solution)/shard_map/ppermute | solution.py:238
  50.3 16.5 %collective-permute-start.6 = (bf16[8,48,768]{2,1,0:T(8,128)(2,1)}, bf16[8,48,768]{2,1,0:T(8,128)(2,1)}, u32[]{:S(2)}, u32[]{:S(2)}) collective-permute-start(bf16[8,48,768]{2,1,0:T(8,128)(2,1)} %get-tuple-element.77), channel_id=1, source_target_pairs={{0,64},{16,80},{32,96},{48,112},{64,128},{80,144},{96,160},{112,17... | collective-permute-start | bytes 1769480 | tf_op jit(solution)/shard_map/ppermute | solution.py:238
  50.7 16.1 %collective-permute-start.7 = (bf16[8,48,768]{2,1,0:T(8,128)(2,1)}, bf16[8,48,768]{2,1,0:T(8,128)(2,1)}, u32[]{:S(2)}, u32[]{:S(2)}) collective-permute-start(bf16[8,48,768]{2,1,0:T(8,128)(2,1)} %get-tuple-element.78), channel_id=1, source_target_pairs={{0,192},{16,208},{32,224},{48,240},{64,0},{80,16},{96,32},{112,48}... | collective-permute-start | bytes 1769480 | tf_op jit(solution)/shard_map/ppermute | solution.py:238
  64.0 2.8 %copy-start.4 = (bf16[8,48,768]{2,1,0:T(8,128)(2,1)}, bf16[8,48,768]{2,1,0:T(8,128)(2,1)S(1)}, u32[]{:S(2)}) copy-start(bf16[8,48,768]{2,1,0:T(8,128)(2,1)S(1)} %collective-permute-done.4.refs_4_) | copy-start | bytes 1769476
  66.7 0.8 copy-start.5
  76.0 75.4 %all-to-all-start.1 = ((bf16[16,64,768]{2,1,0:T(8,128)(2,1)}), bf16[16,64,768]{2,1,0:T(8,128)(2,1)S(1)}, u32[]{:S(2)}, u32[]{:S(2)}) async-start(bf16[16,64,768]{2,1,0:T(8,128)(2,1)} %shard_map.105), calls=%async_computation.1 | async-start | bytes 3145728 | tf_op jit(solution)/shard_map/all_to_all | solution.py:397
  82.6 29.4 %collective-permute-start.8 = (bf16[8,48,768]{2,1,0:T(8,128)(2,1)}, bf16[8,48,768]{2,1,0:T(8,128)(2,1)S(1)}, u32[]{:S(2)}, u32[]{:S(2)}) collective-permute-start(bf16[8,48,768]{2,1,0:T(8,128)(2,1)} %get-tuple-element.79), channel_id=1, source_target_pairs={{0,16},{16,32},{32,48},{48,0},{64,80},{80,96},{96,112},{112,64},{1... | collective-permute-start | bytes 1769480 | tf_op jit(solution)/shard_map/ppermute | solution.py:238
  82.7 29.2 %collective-permute-start.9 = (bf16[8,48,768]{2,1,0:T(8,128)(2,1)}, bf16[8,48,768]{2,1,0:T(8,128)(2,1)S(1)}, u32[]{:S(2)}, u32[]{:S(2)}) collective-permute-start(bf16[8,48,768]{2,1,0:T(8,128)(2,1)} %get-tuple-element.80), channel_id=1, source_target_pairs={{0,48},{16,0},{32,16},{48,32},{64,112},{80,64},{96,80},{112,96},{1... | collective-permute-start | bytes 1769480 | tf_op jit(solution)/shard_map/ppermute | solution.py:238
  84.6 29.2 %collective-permute-start.10 = (bf16[8,48,768]{2,1,0:T(8,128)(2,1)}, bf16[8,48,768]{2,1,0:T(8,128)(2,1)S(1)}, u32[]{:S(2)}, u32[]{:S(2)}) collective-permute-start(bf16[8,48,768]{2,1,0:T(8,128)(2,1)} %get-tuple-element.83), channel_id=1, source_target_pairs={{0,64},{16,80},{32,96},{48,112},{64,128},{80,144},{96,160},{112,17... | collective-permute-start | bytes 1769480 | tf_op jit(solution)/shard_map/ppermute | solution.py:238
  86.1 27.7 %collective-permute-start.11 = (bf16[8,48,768]{2,1,0:T(8,128)(2,1)}, bf16[8,48,768]{2,1,0:T(8,128)(2,1)}, u32[]{:S(2)}, u32[]{:S(2)}) collective-permute-start(bf16[8,48,768]{2,1,0:T(8,128)(2,1)} %get-tuple-element.84), channel_id=1, source_target_pairs={{0,192},{16,208},{32,224},{48,240},{64,0},{80,16},{96,32},{112,48}... | collective-permute-start | bytes 1769480 | tf_op jit(solution)/shard_map/ppermute | solution.py:238
  112.0 1.8 %copy-start.10 = (bf16[8,48,768]{2,1,0:T(8,128)(2,1)}, bf16[8,48,768]{2,1,0:T(8,128)(2,1)S(1)}, u32[]{:S(2)}) copy-start(bf16[8,48,768]{2,1,0:T(8,128)(2,1)S(1)} %collective-permute-done.8.refs_6_) | copy-start | bytes 1769476
  112.0 1.8 %copy-start.11 = (bf16[8,48,768]{2,1,0:T(8,128)(2,1)}, bf16[8,48,768]{2,1,0:T(8,128)(2,1)S(1)}, u32[]{:S(2)}) copy-start(bf16[8,48,768]{2,1,0:T(8,128)(2,1)S(1)} %collective-permute-done.9.refs_7_) | copy-start | bytes 1769476
  113.8 0.8 copy-start.12
  120.3 9.2 %collective-permute-start.12 = (bf16[4,48,768]{2,1,0:T(8,128)(2,1)}, bf16[4,48,768]{2,1,0:T(8,128)(2,1)S(1)}, u32[]{:S(2)}, u32[]{:S(2)}) collective-permute-start(bf16[4,48,768]{2,1,0:T(8,128)(2,1)} %get-tuple-element.86), channel_id=1, source_target_pairs={{0,64},{16,80},{32,96},{48,112},{64,128},{80,144},{96,160},{112,17... | collective-permute-start | bytes 884744 | tf_op jit(solution)/shard_map/ppermute | solution.py:238
  120.5 8.9 %collective-permute-start.13 = (bf16[4,48,768]{2,1,0:T(8,128)(2,1)}, bf16[4,48,768]{2,1,0:T(8,128)(2,1)S(1)}, u32[]{:S(2)}, u32[]{:S(2)}) collective-permute-start(bf16[4,48,768]{2,1,0:T(8,128)(2,1)} %get-tuple-element.87), channel_id=1, source_target_pairs={{0,192},{16,208},{32,224},{48,240},{64,0},{80,16},{96,32},{112,48}... | collective-permute-start | bytes 884744 | tf_op jit(solution)/shard_map/ppermute | solution.py:238
  123.6 7.3 %collective-permute-start.14 = (bf16[4,48,768]{2,1,0:T(8,128)(2,1)}, bf16[4,48,768]{2,1,0:T(8,128)(2,1)S(1)}, u32[]{:S(2)}, u32[]{:S(2)}) collective-permute-start(bf16[4,48,768]{2,1,0:T(8,128)(2,1)} %get-tuple-element.90), channel_id=1, source_target_pairs={{0,16},{16,32},{32,48},{48,0},{64,80},{80,96},{96,112},{112,64},{1... | collective-permute-start | bytes 884744 | tf_op jit(solution)/shard_map/ppermute | solution.py:238
  124.5 9.2 %collective-permute-start.15 = (bf16[4,48,768]{2,1,0:T(8,128)(2,1)}, bf16[4,48,768]{2,1,0:T(8,128)(2,1)S(1)}, u32[]{:S(2)}, u32[]{:S(2)}) collective-permute-start(bf16[4,48,768]{2,1,0:T(8,128)(2,1)} %get-tuple-element.91), channel_id=1, source_target_pairs={{0,48},{16,0},{32,16},{48,32},{64,112},{80,64},{96,80},{112,96},{1... | collective-permute-start | bytes 884744 | tf_op jit(solution)/shard_map/ppermute | solution.py:238
  129.4 4.3 %copy-start.6 = (bf16[4,48,768]{2,1,0:T(8,128)(2,1)}, bf16[4,48,768]{2,1,0:T(8,128)(2,1)S(1)}, u32[]{:S(2)}) copy-start(bf16[4,48,768]{2,1,0:T(8,128)(2,1)S(1)} %collective-permute-done.12.refs_1_) | copy-start | bytes 884740
  129.4 4.3 %copy-start.7 = (bf16[4,48,768]{2,1,0:T(8,128)(2,1)}, bf16[4,48,768]{2,1,0:T(8,128)(2,1)S(1)}, u32[]{:S(2)}) copy-start(bf16[4,48,768]{2,1,0:T(8,128)(2,1)S(1)} %collective-permute-done.13.refs_2_) | copy-start | bytes 884740
  130.9 2.8 %copy-start.8 = (bf16[4,48,768]{2,1,0:T(8,128)(2,1)}, bf16[4,48,768]{2,1,0:T(8,128)(2,1)S(1)}, u32[]{:S(2)}) copy-start(bf16[4,48,768]{2,1,0:T(8,128)(2,1)S(1)} %collective-permute-done.14.refs_4_.refs_6_) | copy-start | bytes 884740
  133.7 0.7 copy-start.9
  137.6 6.6 %collective-permute-start.16 = (bf16[2,48,768]{2,1,0:T(8,128)(2,1)}, bf16[2,48,768]{2,1,0:T(8,128)(2,1)S(1)}, u32[]{:S(2)}, u32[]{:S(2)}) collective-permute-start(bf16[2,48,768]{2,1,0:T(8,128)(2,1)} %get-tuple-element.92), channel_id=1, source_target_pairs={{0,64},{16,80},{32,96},{48,112},{64,128},{80,144},{96,160},{112,17... | collective-permute-start | bytes 442376 | tf_op jit(solution)/shard_map/ppermute | solution.py:238
  137.9 6.3 %collective-permute-start.17 = (bf16[2,48,768]{2,1,0:T(8,128)(2,1)}, bf16[2,48,768]{2,1,0:T(8,128)(2,1)S(1)}, u32[]{:S(2)}, u32[]{:S(2)}) collective-permute-start(bf16[2,48,768]{2,1,0:T(8,128)(2,1)} %get-tuple-element.93), channel_id=1, source_target_pairs={{0,192},{16,208},{32,224},{48,240},{64,0},{80,16},{96,32},{112,48}... | collective-permute-start | bytes 442376 | tf_op jit(solution)/shard_map/ppermute | solution.py:238
  140.9 5.4 %collective-permute-start.18 = (bf16[2,48,768]{2,1,0:T(8,128)(2,1)}, bf16[2,48,768]{2,1,0:T(8,128)(2,1)S(1)}, u32[]{:S(2)}, u32[]{:S(2)}) collective-permute-start(bf16[2,48,768]{2,1,0:T(8,128)(2,1)} %get-tuple-element.95), channel_id=1, source_target_pairs={{0,16},{16,32},{32,48},{48,0},{64,80},{80,96},{96,112},{112,64},{1... | collective-permute-start | bytes 442376 | tf_op jit(solution)/shard_map/ppermute | solution.py:238
  141.3 6.6 %collective-permute-start.19 = (bf16[2,48,768]{2,1,0:T(8,128)(2,1)}, bf16[2,48,768]{2,1,0:T(8,128)(2,1)S(1)}, u32[]{:S(2)}, u32[]{:S(2)}) collective-permute-start(bf16[2,48,768]{2,1,0:T(8,128)(2,1)} %get-tuple-element.96), channel_id=1, source_target_pairs={{0,48},{16,0},{32,16},{48,32},{64,112},{80,64},{96,80},{112,96},{1... | collective-permute-start | bytes 442376 | tf_op jit(solution)/shard_map/ppermute | solution.py:238
  144.2 3.6 %copy-start.13 = (bf16[2,48,768]{2,1,0:T(8,128)(2,1)}, bf16[2,48,768]{2,1,0:T(8,128)(2,1)S(1)}, u32[]{:S(2)}) copy-start(bf16[2,48,768]{2,1,0:T(8,128)(2,1)S(1)} %collective-permute-done.16.refs_3_) | copy-start | bytes 442372
  144.2 3.6 %copy-start.14 = (bf16[2,48,768]{2,1,0:T(8,128)(2,1)}, bf16[2,48,768]{2,1,0:T(8,128)(2,1)S(1)}, u32[]{:S(2)}) copy-start(bf16[2,48,768]{2,1,0:T(8,128)(2,1)S(1)} %collective-permute-done.17.refs_4_) | copy-start | bytes 442372
  146.3 1.6 %copy-start.15 = (bf16[2,48,768]{2,1,0:T(8,128)(2,1)}, bf16[2,48,768]{2,1,0:T(8,128)(2,1)S(1)}, u32[]{:S(2)}) copy-start(bf16[2,48,768]{2,1,0:T(8,128)(2,1)S(1)} %collective-permute-done.18.refs_8_) | copy-start | bytes 442372
  147.8 0.7 copy-start.16

commit v3 on v2

--- a/solution.py
+++ b/solution.py
@@ -60,9 +60,8 @@
         copy.wait()
 
 
-def forward_kernel(dest, mix, out_grad, w_up, w_down, gain_first, gain_second, *refs):
-    hidden, slope, grad_wide, grad_mid = refs[:4]
-    outs, (active, stage, sems) = refs[4:12], refs[12:]
+def forward_kernel(mix, out_grad, w_up, w_down, gain_first, gain_second, *refs):
+    hidden, slope, grad_wide, grad_mid, grad_down, active = refs
     step = pl.program_id(0)
 
     @pl.when(step == 0)
@@ -96,13 +95,7 @@
 
     @pl.when(step >= SIDE)
     def _():
-        part = contract_rows(active[step - SIDE], grad_mid[...]).astype(BF16)
-        for k in range(16):
-            stage[dest[(step - SIDE) * 16 + k]] = part[k * BLOCK : (k + 1) * BLOCK]
-
-    @pl.when(step == 2 * SIDE - 1)
-    def _():
-        send_out(stage, outs, sems)
+        grad_down[...] = contract_rows(active[step - SIDE], grad_mid[...]).astype(BF16)
 
 
 def backward_kernel(
@@ -170,56 +163,30 @@
 def first_kernel(*refs):
     ins, outs = refs[:-4], refs[-4:]
     for axis in range(2):
-        for mat in range(2):
-            keep, up, down = ins[(axis * 2 + mat) * 3 : (axis * 2 + mat) * 3 + 3]
-            rows = pl.ds(mat * SIDE, SIDE)
-            outs[axis * 2][rows] = add(keep[:SIDE], up[...]).astype(BF16)
-            outs[axis * 2 + 1][rows] = add(keep[SIDE:], down[...]).astype(BF16)
+        keep, up, down = ins[axis * 3 : axis * 3 + 3]
+        outs[axis * 2][...] = add(keep[:SIDE], up[...]).astype(BF16)
+        outs[axis * 2 + 1][...] = add(keep[SIDE:], down[...]).astype(BF16)
 
 
 def second_kernel(*refs):
     ins, outs = refs[:-8], refs[-8:]
     for axis in range(2):
-        up2, down2, mid2, keep2 = outs[axis * 4 : axis * 4 + 4]
-        here = ins[axis * 8 : axis * 8 + 8]
-        for mat in range(2):
-            keep, up, down = here[mat * 3 : mat * 3 + 3]
-            rows = slice(mat * SIDE, (mat + 1) * SIDE)
-            low = add(keep[:SIDE], down[...], here[6][rows])
-            high = add(keep[SIDE:], up[...], here[7][rows])
-            up2[2 * mat] = low[2].astype(BF16)
-            up2[2 * mat + 1] = high[1].astype(BF16)
-            down2[2 * mat] = high[2].astype(BF16)
-            down2[2 * mat + 1] = low[3].astype(BF16)
-            mid2[2 * mat] = low[1].astype(BF16)
-            mid2[2 * mat + 1] = high[3].astype(BF16)
-            keep2[2 * mat] = low[0]
-            keep2[2 * mat + 1] = high[0]
-
-
-def third_kernel(*refs):
-    ins, outs = refs[:-4], refs[-4:]
+        keep, up, down, low, high = ins[axis * 5 : axis * 5 + 5]
+        totals = add(keep[:SIDE], down[...], low[...]), add(keep[SIDE:], up[...], high[...])
+        for half, total in enumerate(totals):
+            for away in range(SIDE):
+                out = outs[axis * 4 + away]
+                out[half] = total[away].astype(out.dtype)
+
+
+def last_kernel(*refs):
+    ins, grad_up = refs[:-1], refs[-1]
+    width = grad_up.shape[1] // SIDE
     for axis in range(2):
-        mid2, up2, down2 = ins[axis * 3 : axis * 3 + 3]
-        for mat in range(2):
-            outs[axis * 2][mat] = add(mid2[2 * mat], up2[2 * mat]).astype(BF16)
-            outs[axis * 2 + 1][mat] = add(mid2[2 * mat + 1], down2[2 * mat]).astype(BF16)
-
-
-def last_kernel(*refs):
-    ins, (grad_up, grad_down) = refs[:-2], refs[-2:]
-    width = grad_down.shape[1]
-    for axis in range(2):
-        keep2, up2, down2, low2, high2 = ins[axis * 5 : axis * 5 + 5]
-        for mat in range(2):
-            low = add(keep2[2 * mat], down2[2 * mat + 1], low2[mat])
-            high = add(keep2[2 * mat + 1], up2[2 * mat + 1], high2[mat])
-            for half, value in enumerate((low, high)):
-                part = 2 * axis + half
-                if mat == 0:
-                    grad_down[part * BLOCK : (part + 1) * BLOCK, :] = value
-                else:
-                    grad_up[:, part * width : (part + 1) * width] = value
+        for half in range(2):
+            part = 2 * axis + half
+            total = add(*(ref[half] for ref in ins[axis * 4 : axis * 4 + 4]))
+            grad_up[:, part * width : (part + 1) * width] = total
 
 
 def moves(axis, sign):
@@ -286,42 +253,38 @@
     clamp = lambda i: jnp.minimum(i, SIDE - 1)
     stage = [pltpu.VMEM((64, BLOCK, width), BF16), pltpu.SemaphoreType.DMA((8,))]
     matmul = 2 * rows * width * hidden_units
-    hidden, slope, grad_wide, grad_mid, *down_parts = pl.pallas_call(
+    hidden, slope, grad_wide, grad_mid, down_whole = pl.pallas_call(
         forward_kernel,
-        grid_spec=pltpu.PrefetchScalarGridSpec(
-            num_scalar_prefetch=1,
-            grid=(2 * SIDE,),
-            in_specs=[
-                tall,
-                tall,
-                pl.BlockSpec((width, chunk), lambda i, _: (0, clamp(i))),
-                pl.BlockSpec((chunk, width), lambda i, _: (clamp(i), 0)),
-                gain,
-                gain,
-            ],
-            out_specs=[
-                tall,
-                pl.BlockSpec((1, rows, chunk), lambda i, _: (clamp(i), 0, 0)),
-                tall,
-                tall,
-            ]
-            + [ANY] * 8,
-            scratch_shapes=[pltpu.VMEM((SIDE, rows, chunk), BF16)] + stage,
-        ),
+        grid=(2 * SIDE,),
+        in_specs=[
+            tall,
+            tall,
+            pl.BlockSpec((width, chunk), lambda i: (0, clamp(i))),
+            pl.BlockSpec((chunk, width), lambda i: (clamp(i), 0)),
+            gain,
+            gain,
+        ],
+        out_specs=[
+            tall,
+            pl.BlockSpec((1, rows, chunk), lambda i: (clamp(i), 0, 0)),
+            tall,
+            tall,
+            pl.BlockSpec((chunk, width), lambda i: (jnp.maximum(i - SIDE, 0), 0)),
+        ],
         out_shape=[
             jax.ShapeDtypeStruct((rows, width), BF16),
             jax.ShapeDtypeStruct((SIDE, rows, chunk), F32),
             jax.ShapeDtypeStruct((rows, width), F32),
             jax.ShapeDtypeStruct((rows, width), BF16),
-        ]
-        + [group] * 8,
+            jax.ShapeDtypeStruct((hidden_units, width), BF16),
+        ],
+        scratch_shapes=[pltpu.VMEM((SIDE, rows, chunk), BF16)],
         compiler_params=params("arbitrary"),
         cost_estimate=cost(3 * matmul, 25_000_000),
-    )(dest, mix, out_g, up_mat, down_mat, gain_first, gain_second)
-
-    down_got = [
-        (shift(down_parts[4 * a], a, 1), shift(down_parts[4 * a + 1], a, -1)) for a in range(2)
-    ]
+        name="forward_and_grad_down",
+    )(mix, out_g, up_mat, down_mat, gain_first, gain_second)
+
+    grad_down = lax.psum_scatter(down_whole, "dp", scatter_dimension=0, tiled=True).astype(F32)
 
     grad_sum, *up_parts = pl.pallas_call(
         backward_kernel,
@@ -345,12 +308,10 @@
         out_shape=[jax.ShapeDtypeStruct((width, rows), BF16)] + [group] * 8,
         compiler_params=params("arbitrary"),
         cost_estimate=cost(3 * matmul, 25_000_000),
+        name="backward_and_grad_up",
     )(dest, mix, hidden, slope, grad_wide, grad_mid, up_mat, down_mat, gain_first)
 
-    leaving = [up_parts[k] for k in (0, 1, 4, 5)]
-    leaving, grad_sum, down_got = lax.optimization_barrier((leaving, grad_sum, down_got))
-    up_parts = [*leaving[:2], *up_parts[2:4], *leaving[2:], *up_parts[6:]]
-    up_got = [(shift(up_parts[4 * a], a, 1), shift(up_parts[4 * a + 1], a, -1)) for a in range(2)]
+    got = [(shift(up_parts[4 * a], a, 1), shift(up_parts[4 * a + 1], a, -1)) for a in range(2)]
 
     swapped = lax.all_to_all(
         grad_sum.reshape(pieces, width // pieces, rows),
@@ -359,8 +320,6 @@
         concat_axis=0,
         tiled=True,
     ).reshape(width, rows)
-
-    mats = ((down_parts, down_got), (up_parts, up_got))
 
     def lines(count, part=0):
         return pl.BlockSpec((count, ROWS, width), lambda i: (part, i, 0))
@@ -379,15 +338,14 @@
             name=name,
         )(*args)
 
-    args, specs = [], []
+    args = []
     for a in range(2):
-        for parts, got in mats:
-            args += [parts[4 * a + 2], *got[a]]
-            specs += [lines(8), lines(4), lines(4)]
-    both = combine(first_kernel, specs, args, [8] * 4, [BF16] * 4, "first_sums")
-    both_got = [shift(both[2 * a + s], a, 1 - 2 * s) for a in range(2) for s in range(2)]
-
-    swapped, _ = lax.optimization_barrier((swapped, both))
+        args += [up_parts[4 * a + 2], *got[a]]
+    specs = [lines(8), lines(4), lines(4)] * 2
+    passed = combine(first_kernel, specs, args, [4] * 4, [BF16] * 4, "first_sums")
+    passed_got = [shift(passed[2 * a + s], a, 1 - 2 * s) for a in range(2) for s in range(2)]
+
+    swapped, _ = lax.optimization_barrier((swapped, passed))
     sent = pl.pallas_call(
         seat_kernel,
         out_shape=jax.ShapeDtypeStruct((owners, SEAT, width), BF16),
@@ -396,35 +354,22 @@
     )(grad_sum, swapped, owner_dev.reshape(1, rows), slot_row)
     landed = lax.all_to_all(sent, "dp", split_axis=0, concat_axis=0, tiled=True)
 
-    args, specs = [], []
-    for a in range(2):
-        for parts, got in mats:
-            args += [parts[4 * a + 3], *got[a]]
-            specs += [lines(8), lines(4, 1), lines(4, 1)]
-        args += both_got[2 * a : 2 * a + 2]
-        specs += [lines(8), lines(8)]
-    second = combine(
-        second_kernel, specs, args, [4] * 8, [BF16, BF16, BF16, F32] * 2, "second_sums"
-    )
-    second_got = [shift(second[4 * a + s], 1 - a, 1 - 2 * s) for a in range(2) for s in range(2)]
-
     args = []
     for a in range(2):
-        args += [second[4 * a + 2], *second_got[2 * a : 2 * a + 2]]
-    third = combine(third_kernel, [lines(4)] * 6, args, [2] * 4, [BF16] * 4, "third_sums")
-    third_got = [shift(third[2 * a + s], 1 - a, 1 - 2 * s) for a in range(2) for s in range(2)]
-
+        args += [up_parts[4 * a + 3], *got[a], *passed_got[2 * a : 2 * a + 2]]
+    specs = [lines(8), lines(4, 1), lines(4, 1), lines(4), lines(4)] * 2
+    lined = combine(
+        second_kernel, specs, args, [2] * 8, [F32, BF16, BF16, BF16] * 2, "second_sums"
+    )
     args = []
     for a in range(2):
-        args += [second[4 * a + 3], *second_got[2 * a : 2 * a + 2], *third_got[2 * a : 2 * a + 2]]
-    grad_up, grad_down = pl.pallas_call(
+        args += [lined[4 * a]]
+        args += [shift(lined[4 * a + away], 1 - a, away) for away in range(1, SIDE)]
+    grad_up = pl.pallas_call(
         last_kernel,
-        out_shape=[
-            jax.ShapeDtypeStruct((BLOCK, hidden_units), F32),
-            jax.ShapeDtypeStruct((4 * BLOCK, width), F32),
-        ],
+        out_shape=jax.ShapeDtypeStruct((BLOCK, hidden_units), F32),
         compiler_params=params(),
-        cost_estimate=cost(1_000_000, 4_000_000),
+        cost_estimate=cost(1_000_000, 2_000_000),
         name="last_sums",
     )(*args)
 

time: 154 us -> 155 us (level)
  between operations: 0.84 us -> 14.2 us
  Pallas kernels: 53.2 us -> 44.4 us
  starting transfers between devices: 41.8 us -> 34.2 us
  waiting for transfers between devices: 52.2 us -> 54 us
  other arithmetic: 0.61 us -> 2.34 us
    ppermute x20 -> x14, starting transfers between devices: 26.8 us -> 18.6 us  [shift(): return lax.ppermute(value, 'dp', moves(axis, sign))]
    pallas_call x3 -> x2, Pallas kernels: 13.6 us -> 7.78 us  [combine(): pl.pallas_call(kernel, grid=(BLOCK // ROWS,), in_specs=specs, out_specs=[...]
    pallas_call x2, Pallas kernels: 21.1 us -> 17.9 us  [the longest x1 15.6 us: per_device(): pl.pallas_call(forward_kernel, grid=(2 * SIDE,), in_specs=[tall, tall, pl...]
    ppermute x20 -> x14, waiting for transfers between devices: 52.1 us -> 54 us  [shift(): return lax.ppermute(value, 'dp', moves(axis, sign))]
    broadcast_in_dim x0 -> x1, other arithmetic: none -> 1.81 us  [per_device(): return (grad_up[None], grad_down[None], row_grad[None])]
    unnamed x34 -> x36, local copies, waits for them, and re-layouts: 2.86 us -> 3.38 us
  transfers between devices with their start and end apart: 22 -> 17, of which waited for: 11 -> 10; matrix products, arithmetic and copies ran while one was open for 0% -> 1% of each run, Pallas kernels for 20% -> 19%
where the time goes in v3:
time: 155 us; the launch traced here: 154 us
  waiting for transfers between devices  54 us (35%)
  Pallas kernels  44.4 us (29%)
  starting transfers between devices  34.2 us (22%)
  between operations  14.2 us (9%)
  local copies, waits for them, and re-layouts  3.38 us (2%)
  other arithmetic  2.34 us (2%)
  matrix products  1.68 us (1%)
    ppermute x14, waiting for transfers between devices, shift(): return lax.ppermute(value, 'dp', moves(axis, sign))  54 us
    ppermute x14, starting transfers between devices, shift(): return lax.ppermute(value, 'dp', moves(axis, sign))  18.6 us
    pallas_call x1, Pallas kernels, per_device(): pl.pallas_call(forward_kernel, grid=(2 * SIDE,), in_specs=[tall, tall, pl...  15.6 us
    pallas_call x1, Pallas kernels, per_device(): pl.pallas_call(backward_kernel, grid_spec=pltpu.PrefetchScalarGridSpec(nu...  14.8 us
    all_to_all x1, starting transfers between devices, per_device(): lax.all_to_all(grad_sum.reshape(pieces, width // pieces, rows), 'token',...  8.59 us
    pallas_call x2, Pallas kernels, combine(): pl.pallas_call(kernel, grid=(BLOCK // ROWS,), in_specs=specs, out_specs=[...  7.78 us
    all_to_all x1, starting transfers between devices, per_device(): landed = lax.all_to_all(sent, 'dp', split_axis=0, concat_axis=0, tiled=True)  6.93 us
    pallas_call x1, Pallas kernels, per_device(): pl.pallas_call(seat_kernel, out_shape=jax.ShapeDtypeStruct((owners, SEAT,...  3.8 us
  transfers between devices with their start and end apart: 17, of which 10 were waited for; matrix products, arithmetic and copies ran while one was open for 1% of the time, Pallas kernels for 19%

profile of v3, /device:TPU:6, one launch (start us, length us, event | category | flops | bytes accessed | tf_op | source)
XLA Modules:
  0.0 154.1 jit_solution(2166195238071850613)
XLA Ops:
  7.2 0.0 reduce-scatter.2.cloned.1.call-start
  7.2 15.6 %forward_and_grad_down.1 = (bf16[384,768]{1,0:T(8,128)(2,1)}, f32[4,384,768]{2,1,0:T(8,128)}, f32[384,768]{1,0:T(8,128)}, bf16[384,768]{1,0:T(8,128)(2,1)}, bf16[3072,768]{1,0:T(8,128)(2,1)}) custom-call(bf16[384,768]{1,0:T(8,128)(2,1)} %bitcast.26, bf16[384,768]{1,0:T(8,128)(2,1)} %bitcast.25, bf16[768,3072]{1,0:T(8,128)(2,1)} %bitcast.21, ...), custom_call_target="tpu_custom_call" | custom-call | flops 5435817984 | bytes 25000000 | tf_op jit(solution)/shard_map/forward_and_grad_down/pallas_call | solution.py:256
  22.8 0.0 reduce-scatter.2.cloned.1.call-update
  22.9 0.5 fusion.2.dest
  23.4 14.8 %backward_and_grad_up.1 = (bf16[768,384]{1,0:T(8,128)(2,1)}, bf16[8,48,768]{2,1,0:T(8,128)(2,1)}, bf16[8,48,768]{2,1,0:T(8,128)(2,1)}, bf16[8,48,768]{2,1,0:T(8,...) custom-call(s32[64]{0:T(128)} %fusion.2.dest, ...), custom_call_target="tpu_custom_call" | custom-call | flops 5435817984 | bytes 25000000 | tf_op jit(solution)/shard_map/backward_and_grad_up/pallas_call | solution.py:289
  38.2 8.6 %all-to-all-start = ((bf16[16,48,384]{2,1,0:T(8,128)(2,1)}), bf16[16,48,384]{2,1,0:T(8,128)(2,1)S(1)}, u32[]{:S(2)}, u32[]{:S(2)}) async-start(bf16[16,48,384]{2,1,0:T(8,128)(2,1)} %bitcast.16), calls=%async_computation.1 | async-start | bytes 1179648 | tf_op jit(solution)/shard_map/all_to_all | solution.py:316
  46.8 0.6 collective-permute-start
  47.4 1.5 %collective-permute-start.1 = (bf16[8,48,768]{2,1,0:T(8,128)(2,1)}, bf16[8,48,768]{2,1,0:T(8,128)(2,1)S(1)}, u32[]{:S(2)}, u32[]{:S(2)}) collective-permute-start(bf16[8,48,768]{2,1,0:T(8,128)(2,1)} %get-tuple-element.36), channel_id=1, source_target_pairs={{0,48},{16,0},{32,16},{48,32},{64,112},{80,64},{96,80},{112,96},{1... | collective-permute-start | bytes 1769480 | tf_op jit(solution)/shard_map/ppermute | solution.py:205
  48.9 1.6 %collective-permute-start.2 = (bf16[8,48,768]{2,1,0:T(8,128)(2,1)}, bf16[8,48,768]{2,1,0:T(8,128)(2,1)S(1)}, u32[]{:S(2)}, u32[]{:S(2)}) collective-permute-start(bf16[8,48,768]{2,1,0:T(8,128)(2,1)} %get-tuple-element.39), channel_id=1, source_target_pairs={{0,64},{16,80},{32,96},{48,112},{64,128},{80,144},{96,160},{112,17... | collective-permute-start | bytes 1769480 | tf_op jit(solution)/shard_map/ppermute | solution.py:205
  50.5 1.7 %collective-permute-start.3 = (bf16[8,48,768]{2,1,0:T(8,128)(2,1)}, bf16[8,48,768]{2,1,0:T(8,128)(2,1)S(1)}, u32[]{:S(2)}, u32[]{:S(2)}) collective-permute-start(bf16[8,48,768]{2,1,0:T(8,128)(2,1)} %get-tuple-element.40), channel_id=1, source_target_pairs={{0,192},{16,208},{32,224},{48,240},{64,0},{80,16},{96,32},{112,48}... | collective-permute-start | bytes 1769480 | tf_op jit(solution)/shard_map/ppermute | solution.py:205
  52.2 19.0 %collective-permute-done.refs_1_ = bf16[8,48,768]{2,1,0:T(8,128)(2,1)S(1)} collective-permute-done((bf16[8,48,768]{2,1,0:T(8,128)(2,1)}, bf16[8,48,768]{2,1,0:T(8,128)(2,1)S(1)}, u32[]{:S(2)}, u32[]{:S(2)}) %collective-permute-start) | collective-permute-done | bytes 589856 | tf_op jit(solution)/shard_map/ppermute | solution.py:205
  71.2 0.0 copy-start
  71.2 1.2 collective-permute-done.1.refs_2_
  72.4 1.2 collective-permute-done.2.refs_4_.refs_6_
  73.5 0.0 collective-permute-done.3.refs_5_.refs_7_
  73.5 0.0 copy-done
  73.6 0.0 copy-done.1
  73.6 0.8 copy-done.2
  74.4 0.2 copy-done.3
  74.6 3.7 %first_sums.1 = (bf16[4,48,768]{2,1,0:T(8,128)(2,1)}, bf16[4,48,768]{2,1,0:T(8,128)(2,1)}, bf16[4,48,768]{2,1,0:T(8,128)(2,1)}, bf16[4,48,768]{2,1,0:T(8,128)(2,1)}) custom-call(bf16[8,48,768]{2,1,0:T(8,128)(2,1)} %get-tuple-element.37.refs_0_, bf16[8,48,768]{2,1,0:T(8,128)(2,1)} %copy-done, bf16[8,48,768]{2,1,0:T(8,128)(2,1)} %copy-done.1, ...), custom_call_target="tpu_custom_call" | custom-call | flops 1000000 | bytes 7000000 | tf_op jit(solution)/shard_map/first_sums/pallas_call | solution.py:328
  78.3 0.0 all-to-all-done
  78.3 0.0 copy-start.4
  78.3 0.8 copy-done.4
  79.1 3.8 %shard_map.103 = bf16[16,64,768]{2,1,0:T(8,128)(2,1)} custom-call(bf16[768,384]{1,0:T(8,128)(2,1)} %get-tuple-element.55.grad_sum, bf16[768,384]{1,0:T(8,128)(2,1)} %bitcast.17, s32[1,384]{1,0:T(1,128)} %bitcast.20, s32[1,384]{1,0:T(1,128)} %slot.1), custom_call_target="tpu_custom_call" | custom-call | flops 603979776 | bytes 4000000 | tf_op jit(solution)/shard_map/pallas_call | solution.py:349
  82.9 6.9 %all-to-all-start.1 = ((bf16[16,64,768]{2,1,0:T(8,128)(2,1)}), bf16[16,64,768]{2,1,0:T(8,128)(2,1)S(1)}, u32[]{:S(2)}, u32[]{:S(2)}) async-start(bf16[16,64,768]{2,1,0:T(8,128)(2,1)} %shard_map.103), calls=%async_computation.2 | async-start | bytes 3145728 | tf_op jit(solution)/shard_map/all_to_all | solution.py:355
  89.9 0.2 collective-permute-start.4
  90.0 0.0 copy-done.17
  90.0 1.9 %collective-permute-start.5 = (bf16[4,48,768]{2,1,0:T(8,128)(2,1)S(1)}, bf16[4,48,768]{2,1,0:T(8,128)(2,1)S(1)}, u32[]{:S(2)}, u32[]{:S(2)}) collective-permute-start(bf16[4,48,768]{2,1,0:T(8,128)(2,1)S(1)} %copy-done.17), channel_id=1, source_target_pairs={{0,48},{16,0},{32,16},{48,32},{64,112},{80,64},{96,80},{112,96},{1... | collective-permute-start | bytes 884744 | tf_op jit(solution)/shard_map/ppermute | solution.py:205
  91.9 0.0 copy-done.16
  91.9 1.5 collective-permute-start.6
  93.3 0.0 copy-done.15
  93.4 1.8 %collective-permute-start.7 = (bf16[4,48,768]{2,1,0:T(8,128)(2,1)S(1)}, bf16[4,48,768]{2,1,0:T(8,128)(2,1)S(1)}, u32[]{:S(2)}, u32[]{:S(2)}) collective-permute-start(bf16[4,48,768]{2,1,0:T(8,128)(2,1)S(1)} %copy-done.15), channel_id=1, source_target_pairs={{0,192},{16,208},{32,224},{48,240},{64,0},{80,16},{96,32},{112,48}... | collective-permute-start | bytes 884744 | tf_op jit(solution)/shard_map/ppermute | solution.py:205
  95.1 22.8 %collective-permute-done.4.refs_3_ = bf16[4,48,768]{2,1,0:T(8,128)(2,1)S(1)} collective-permute-done((bf16[4,48,768]{2,1,0:T(8,128)(2,1)}, bf16[4,48,768]{2,1,0:T(8,128)(2,1)S(1)}, u32[]{:S(2)}, u32[]{:S(2)}) %collective-permute-start.4) | collective-permute-done | bytes 294944 | tf_op jit(solution)/shard_map/ppermute | solution.py:205
  117.9 0.0 collective-permute-done.5.refs_4_
  117.9 2.1 %collective-permute-done.6.refs_8_ = bf16[4,48,768]{2,1,0:T(8,128)(2,1)S(1)} collective-permute-done((bf16[4,48,768]{2,1,0:T(8,128)(2,1)S(1)}, bf16[4,48,768]{2,1,0:T(8,128)(2,1)S(1)}, u32[]{:S(2)}, u32[]{:S(2)}) %collective-permute-start.6) | collective-permute-done | bytes 294944 | tf_op jit(solution)/shard_map/ppermute | solution.py:205
  120.1 0.0 collective-permute-done.7.refs_9_
  120.1 0.0 copy-done.5
  120.1 0.0 copy-done.6
  120.1 0.7 copy-done.7
  120.8 0.1 copy-done.8
  120.9 4.1 %second_sums.1 = (f32[2,48,768]{2,1,0:T(8,128)}, bf16[2,48,768]{2,1,0:T(8,128)(2,1)}, bf16[2,48,768]{2,1,0:T(8,128)(2,1)}, bf16[2,48,768]{2,1,0:T(8,128)(2,1)}, ...) custom-call(bf16[8,48,768]{2,1,0:T(8,128)(2,1)} %get-tuple-element.3, ...), custom_call_target="tpu_custom_call" | custom-call | flops 1000000 | bytes 7000000 | tf_op jit(solution)/shard_map/second_sums/pallas_call | solution.py:328
  125.0 0.3 collective-permute-start.8
  125.3 2.5 %collective-permute-start.9 = (bf16[2,48,768]{2,1,0:T(8,128)(2,1)}, bf16[2,48,768]{2,1,0:T(8,128)(2,1)S(1)}, u32[]{:S(2)}, u32[]{:S(2)}) collective-permute-start(bf16[2,48,768]{2,1,0:T(8,128)(2,1)} %get-tuple-element.48), channel_id=1, source_target_pairs={{0,128},{16,144},{32,160},{48,176},{64,192},{80,208},{96,224},{112... | collective-permute-start | bytes 442376 | tf_op jit(solution)/shard_map/ppermute | solution.py:205
  127.8 1.4 collective-permute-start.10
  129.2 2.3 %collective-permute-start.11 = (bf16[2,48,768]{2,1,0:T(8,128)(2,1)}, bf16[2,48,768]{2,1,0:T(8,128)(2,1)S(1)}, u32[]{:S(2)}, u32[]{:S(2)}) collective-permute-start(bf16[2,48,768]{2,1,0:T(8,128)(2,1)} %get-tuple-element.51), channel_id=1, source_target_pairs={{0,16},{16,32},{32,48},{48,0},{64,80},{80,96},{96,112},{112,64},{1... | collective-permute-start | bytes 442376 | tf_op jit(solution)/shard_map/ppermute | solution.py:205
  131.5 1.5 collective-permute-start.12
  133.0 1.2 collective-permute-done.8.refs_1_
  134.2 0.0 collective-permute-start.13
  134.2 0.0 collective-permute-done.9.refs_2_
  134.2 0.0 copy-start.10
  134.2 0.6 collective-permute-done.10.refs_3_
  134.8 2.2 %collective-permute-done.11.refs_5_ = bf16[2,48,768]{2,1,0:T(8,128)(2,1)S(1)} collective-permute-done((bf16[2,48,768]{2,1,0:T(8,128)(2,1)}, bf16[2,48,768]{2,1,0:T(8,128)(2,1)S(1)}, u32[]{:S(2)}, u32[]{:S(2)}) %collective-permute-start.11) | collective-permute-done | bytes 147488 | tf_op jit(solution)/shard_map/ppermute | solution.py:205
  137.0 2.0 %collective-permute-done.12.refs_6_ = bf16[2,48,768]{2,1,0:T(8,128)(2,1)S(1)} collective-permute-done((bf16[2,48,768]{2,1,0:T(8,128)(2,1)}, bf16[2,48,768]{2,1,0:T(8,128)(2,1)S(1)}, u32[]{:S(2)}, u32[]{:S(2)}) %collective-permute-start.12) | collective-permute-done | bytes 147488 | tf_op jit(solution)/shard_map/ppermute | solution.py:205
  139.0 1.8 %collective-permute-done.13.refs_7_ = bf16[2,48,768]{2,1,0:T(8,128)(2,1)S(1)} collective-permute-done((bf16[2,48,768]{2,1,0:T(8,128)(2,1)}, bf16[2,48,768]{2,1,0:T(8,128)(2,1)S(1)}, u32[]{:S(2)}, u32[]{:S(2)}) %collective-permute-start.13) | collective-permute-done | bytes 147488 | tf_op jit(solution)/shard_map/ppermute | solution.py:205
  140.8 0.0 copy-done.9
  140.8 0.0 copy-done.10
  140.8 0.0 copy-done.11
  140.8 0.0 copy-done.12
  140.8 0.0 copy-done.13
  140.8 0.6 copy-done.14
  141.4 2.3 %last_sums.1 = f32[48,3072]{1,0:T(8,128)} custom-call(f32[2,48,768]{2,1,0:T(8,128)} %get-tuple-element.46.refs_0_, bf16[2,48,768]{2,1,0:T(8,128)(2,1)} %copy-done.9, bf16[2,48,768]{2,1,0:T(8,128)(2,1)} %copy-done.10, bf16[2,48,768]{2,1,0:T(8,128)(2,1)} %copy-done.11, f32[2,48,768]{2,1,0:T(8,128)} %get-tuple-element.50.refs_4_, ...), custom_call_target="tpu_custom_call" | custom-call | flops 1000000 | bytes 2000000 | tf_op jit(solution)/shard_map/last_sums/pallas_call | solution.py:368
  143.8 0.0 all-to-all-done.1
  143.8 1.7 %convolution_bitcast_fusion = f32[1,256,768]{2,1,0:T(8,128)} fusion(bf16[16,64,768]{2,1,0:T(8,128)(2,1)S(1)} %all-to-all-done.1, s32[16,64]{1,0:T(8,128)S(1)} %bitcast.19), kind=kOutput, calls=%fused_computation | convolution fusion | flops 402915328 | bytes 2363392 | tf_op jit(solution)/shard_map/dot_general | solution.py:380
  145.5 1.8 %bitcast_convert_fusion = f32[1,192,768]{2,1,0:T(8,128)} fusion(bf16[192,768]{1,0:T(8,128)(2,1)} %reduce-scatter.2.cloned.1.call-done), kind=kLoop, calls=%fused_computation.3 | loop fusion | flops 147456 | bytes 884736 | tf_op jit(solution)/shard_map/broadcast_in_dim | solution.py:385
  (17 shorter events, 0.0 us)
Async XLA Ops:
  7.2 138.3 %reduce-scatter.2.cloned.1.call-start = ((), (), s32[]{:S(2)}) async-start(), calls=%async_computation.3 | async-start | bytes 5013504 | tf_op jit(solution)/shard_map/reduce_scatter | solution.py:287
  38.2 40.0 %all-to-all-start = ((bf16[16,48,384]{2,1,0:T(8,128)(2,1)}), bf16[16,48,384]{2,1,0:T(8,128)(2,1)S(1)}, u32[]{:S(2)}, u32[]{:S(2)}) async-start(bf16[16,48,384]{2,1,0:T(8,128)(2,1)} %bitcast.16), calls=%async_computation.1 | async-start | bytes 1179648 | tf_op jit(solution)/shard_map/all_to_all | solution.py:316
  46.8 24.3 %collective-permute-start = (bf16[8,48,768]{2,1,0:T(8,128)(2,1)}, bf16[8,48,768]{2,1,0:T(8,128)(2,1)S(1)}, u32[]{:S(2)}, u32[]{:S(2)}) collective-permute-start(bf16[8,48,768]{2,1,0:T(8,128)(2,1)} %get-tuple-element.35), channel_id=1, source_target_pairs={{0,16},{16,32},{32,48},{48,0},{64,80},{80,96},{96,112},{112,64},{1... | collective-permute-start | bytes 1769480 | tf_op jit(solution)/shard_map/ppermute | solution.py:205
  47.4 25.0 %collective-permute-start.1 = (bf16[8,48,768]{2,1,0:T(8,128)(2,1)}, bf16[8,48,768]{2,1,0:T(8,128)(2,1)S(1)}, u32[]{:S(2)}, u32[]{:S(2)}) collective-permute-start(bf16[8,48,768]{2,1,0:T(8,128)(2,1)} %get-tuple-element.36), channel_id=1, source_target_pairs={{0,48},{16,0},{32,16},{48,32},{64,112},{80,64},{96,80},{112,96},{1... | collective-permute-start | bytes 1769480 | tf_op jit(solution)/shard_map/ppermute | solution.py:205
  48.9 24.6 %collective-permute-start.2 = (bf16[8,48,768]{2,1,0:T(8,128)(2,1)}, bf16[8,48,768]{2,1,0:T(8,128)(2,1)S(1)}, u32[]{:S(2)}, u32[]{:S(2)}) collective-permute-start(bf16[8,48,768]{2,1,0:T(8,128)(2,1)} %get-tuple-element.39), channel_id=1, source_target_pairs={{0,64},{16,80},{32,96},{48,112},{64,128},{80,144},{96,160},{112,17... | collective-permute-start | bytes 1769480 | tf_op jit(solution)/shard_map/ppermute | solution.py:205
  50.5 23.1 %collective-permute-start.3 = (bf16[8,48,768]{2,1,0:T(8,128)(2,1)}, bf16[8,48,768]{2,1,0:T(8,128)(2,1)S(1)}, u32[]{:S(2)}, u32[]{:S(2)}) collective-permute-start(bf16[8,48,768]{2,1,0:T(8,128)(2,1)} %get-tuple-element.40), channel_id=1, source_target_pairs={{0,192},{16,208},{32,224},{48,240},{64,0},{80,16},{96,32},{112,48}... | collective-permute-start | bytes 1769480 | tf_op jit(solution)/shard_map/ppermute | solution.py:205
  71.2 2.4 %copy-start = (bf16[8,48,768]{2,1,0:T(8,128)(2,1)}, bf16[8,48,768]{2,1,0:T(8,128)(2,1)S(1)}, u32[]{:S(2)}) copy-start(bf16[8,48,768]{2,1,0:T(8,128)(2,1)S(1)} %collective-permute-done.refs_1_) | copy-start | bytes 1769476
  72.4 1.2 copy-start.1
  73.5 0.8 copy-start.2
  73.5 1.0 copy-start.3
  78.3 0.9 copy-start.4
  82.9 7.1 %copy-start.17 = (bf16[4,48,768]{2,1,0:T(8,128)(2,1)S(1)}, bf16[4,48,768]{2,1,0:T(8,128)(2,1)}, u32[]{:S(2)}) copy-start(bf16[4,48,768]{2,1,0:T(8,128)(2,1)} %get-tuple-element.42) | copy-start | bytes 884740
  82.9 9.0 %copy-start.16 = (bf16[4,48,768]{2,1,0:T(8,128)(2,1)S(1)}, bf16[4,48,768]{2,1,0:T(8,128)(2,1)}, u32[]{:S(2)}) copy-start(bf16[4,48,768]{2,1,0:T(8,128)(2,1)} %get-tuple-element.44) | copy-start | bytes 884740
  82.9 10.4 %copy-start.15 = (bf16[4,48,768]{2,1,0:T(8,128)(2,1)S(1)}, bf16[4,48,768]{2,1,0:T(8,128)(2,1)}, u32[]{:S(2)}) copy-start(bf16[4,48,768]{2,1,0:T(8,128)(2,1)} %get-tuple-element.45) | copy-start | bytes 884740
  82.9 60.8 %all-to-all-start.1 = ((bf16[16,64,768]{2,1,0:T(8,128)(2,1)}), bf16[16,64,768]{2,1,0:T(8,128)(2,1)S(1)}, u32[]{:S(2)}, u32[]{:S(2)}) async-start(bf16[16,64,768]{2,1,0:T(8,128)(2,1)} %shard_map.103), calls=%async_computation.2 | async-start | bytes 3145728 | tf_op jit(solution)/shard_map/all_to_all | solution.py:355
  89.9 28.1 %collective-permute-start.4 = (bf16[4,48,768]{2,1,0:T(8,128)(2,1)}, bf16[4,48,768]{2,1,0:T(8,128)(2,1)S(1)}, u32[]{:S(2)}, u32[]{:S(2)}) collective-permute-start(bf16[4,48,768]{2,1,0:T(8,128)(2,1)} %get-tuple-element.41), channel_id=1, source_target_pairs={{0,16},{16,32},{32,48},{48,0},{64,80},{80,96},{96,112},{112,64},{1... | collective-permute-start | bytes 884744 | tf_op jit(solution)/shard_map/ppermute | solution.py:205
  90.0 27.9 %collective-permute-start.5 = (bf16[4,48,768]{2,1,0:T(8,128)(2,1)S(1)}, bf16[4,48,768]{2,1,0:T(8,128)(2,1)S(1)}, u32[]{:S(2)}, u32[]{:S(2)}) collective-permute-start(bf16[4,48,768]{2,1,0:T(8,128)(2,1)S(1)} %copy-done.17), channel_id=1, source_target_pairs={{0,48},{16,0},{32,16},{48,32},{64,112},{80,64},{96,80},{112,96},{1... | collective-permute-start | bytes 884744 | tf_op jit(solution)/shard_map/ppermute | solution.py:205
  91.9 28.2 %collective-permute-start.6 = (bf16[4,48,768]{2,1,0:T(8,128)(2,1)S(1)}, bf16[4,48,768]{2,1,0:T(8,128)(2,1)S(1)}, u32[]{:S(2)}, u32[]{:S(2)}) collective-permute-start(bf16[4,48,768]{2,1,0:T(8,128)(2,1)S(1)} %copy-done.16), channel_id=1, source_target_pairs={{0,64},{16,80},{32,96},{48,112},{64,128},{80,144},{96,160},{112,17... | collective-permute-start | bytes 884744 | tf_op jit(solution)/shard_map/ppermute | solution.py:205
  93.4 26.7 %collective-permute-start.7 = (bf16[4,48,768]{2,1,0:T(8,128)(2,1)S(1)}, bf16[4,48,768]{2,1,0:T(8,128)(2,1)S(1)}, u32[]{:S(2)}, u32[]{:S(2)}) collective-permute-start(bf16[4,48,768]{2,1,0:T(8,128)(2,1)S(1)} %copy-done.15), channel_id=1, source_target_pairs={{0,192},{16,208},{32,224},{48,240},{64,0},{80,16},{96,32},{112,48}... | collective-permute-start | bytes 884744 | tf_op jit(solution)/shard_map/ppermute | solution.py:205
  117.9 2.1 %copy-start.5 = (bf16[4,48,768]{2,1,0:T(8,128)(2,1)}, bf16[4,48,768]{2,1,0:T(8,128)(2,1)S(1)}, u32[]{:S(2)}) copy-start(bf16[4,48,768]{2,1,0:T(8,128)(2,1)S(1)} %collective-permute-done.4.refs_3_) | copy-start | bytes 884740
  117.9 2.1 %copy-start.6 = (bf16[4,48,768]{2,1,0:T(8,128)(2,1)}, bf16[4,48,768]{2,1,0:T(8,128)(2,1)S(1)}, u32[]{:S(2)}) copy-start(bf16[4,48,768]{2,1,0:T(8,128)(2,1)S(1)} %collective-permute-done.5.refs_4_) | copy-start | bytes 884740
  120.1 0.7 copy-start.7
  120.1 0.9 copy-start.8
  125.0 9.2 %collective-permute-start.8 = (bf16[2,48,768]{2,1,0:T(8,128)(2,1)}, bf16[2,48,768]{2,1,0:T(8,128)(2,1)S(1)}, u32[]{:S(2)}, u32[]{:S(2)}) collective-permute-start(bf16[2,48,768]{2,1,0:T(8,128)(2,1)} %get-tuple-element.47), channel_id=1, source_target_pairs={{0,64},{16,80},{32,96},{48,112},{64,128},{80,144},{96,160},{112,17... | collective-permute-start | bytes 442376 | tf_op jit(solution)/shard_map/ppermute | solution.py:205
  125.3 8.9 %collective-permute-start.9 = (bf16[2,48,768]{2,1,0:T(8,128)(2,1)}, bf16[2,48,768]{2,1,0:T(8,128)(2,1)S(1)}, u32[]{:S(2)}, u32[]{:S(2)}) collective-permute-start(bf16[2,48,768]{2,1,0:T(8,128)(2,1)} %get-tuple-element.48), channel_id=1, source_target_pairs={{0,128},{16,144},{32,160},{48,176},{64,192},{80,208},{96,224},{112... | collective-permute-start | bytes 442376 | tf_op jit(solution)/shard_map/ppermute | solution.py:205
  127.8 7.0 %collective-permute-start.10 = (bf16[2,48,768]{2,1,0:T(8,128)(2,1)}, bf16[2,48,768]{2,1,0:T(8,128)(2,1)S(1)}, u32[]{:S(2)}, u32[]{:S(2)}) collective-permute-start(bf16[2,48,768]{2,1,0:T(8,128)(2,1)} %get-tuple-element.49), channel_id=1, source_target_pairs={{0,192},{16,208},{32,224},{48,240},{64,0},{80,16},{96,32},{112,48}... | collective-permute-start | bytes 442376 | tf_op jit(solution)/shard_map/ppermute | solution.py:205
  129.2 7.8 %collective-permute-start.11 = (bf16[2,48,768]{2,1,0:T(8,128)(2,1)}, bf16[2,48,768]{2,1,0:T(8,128)(2,1)S(1)}, u32[]{:S(2)}, u32[]{:S(2)}) collective-permute-start(bf16[2,48,768]{2,1,0:T(8,128)(2,1)} %get-tuple-element.51), channel_id=1, source_target_pairs={{0,16},{16,32},{32,48},{48,0},{64,80},{80,96},{96,112},{112,64},{1... | collective-permute-start | bytes 442376 | tf_op jit(solution)/shard_map/ppermute | solution.py:205
  131.5 7.5 %collective-permute-start.12 = (bf16[2,48,768]{2,1,0:T(8,128)(2,1)}, bf16[2,48,768]{2,1,0:T(8,128)(2,1)S(1)}, u32[]{:S(2)}, u32[]{:S(2)}) collective-permute-start(bf16[2,48,768]{2,1,0:T(8,128)(2,1)} %get-tuple-element.52), channel_id=1, source_target_pairs={{0,32},{16,48},{32,0},{48,16},{64,96},{80,112},{96,64},{112,80},{1... | collective-permute-start | bytes 442376 | tf_op jit(solution)/shard_map/ppermute | solution.py:205
  134.2 6.6 %copy-start.9 = (bf16[2,48,768]{2,1,0:T(8,128)(2,1)}, bf16[2,48,768]{2,1,0:T(8,128)(2,1)S(1)}, u32[]{:S(2)}) copy-start(bf16[2,48,768]{2,1,0:T(8,128)(2,1)S(1)} %collective-permute-done.8.refs_1_) | copy-start | bytes 442372
  134.2 6.6 %collective-permute-start.13 = (bf16[2,48,768]{2,1,0:T(8,128)(2,1)}, bf16[2,48,768]{2,1,0:T(8,128)(2,1)S(1)}, u32[]{:S(2)}, u32[]{:S(2)}) collective-permute-start(bf16[2,48,768]{2,1,0:T(8,128)(2,1)} %get-tuple-element.53), channel_id=1, source_target_pairs={{0,48},{16,0},{32,16},{48,32},{64,112},{80,64},{96,80},{112,96},{1... | collective-permute-start | bytes 442376 | tf_op jit(solution)/shard_map/ppermute | solution.py:205
  134.2 6.6 %copy-start.10 = (bf16[2,48,768]{2,1,0:T(8,128)(2,1)}, bf16[2,48,768]{2,1,0:T(8,128)(2,1)S(1)}, u32[]{:S(2)}) copy-start(bf16[2,48,768]{2,1,0:T(8,128)(2,1)S(1)} %collective-permute-done.9.refs_2_) | copy-start | bytes 442372
  134.8 6.0 %copy-start.11 = (bf16[2,48,768]{2,1,0:T(8,128)(2,1)}, bf16[2,48,768]{2,1,0:T(8,128)(2,1)S(1)}, u32[]{:S(2)}) copy-start(bf16[2,48,768]{2,1,0:T(8,128)(2,1)S(1)} %collective-permute-done.10.refs_3_) | copy-start | bytes 442372
  137.0 3.8 %copy-start.12 = (bf16[2,48,768]{2,1,0:T(8,128)(2,1)}, bf16[2,48,768]{2,1,0:T(8,128)(2,1)S(1)}, u32[]{:S(2)}) copy-start(bf16[2,48,768]{2,1,0:T(8,128)(2,1)S(1)} %collective-permute-done.11.refs_5_) | copy-start | bytes 442372
  139.0 1.8 %copy-start.13 = (bf16[2,48,768]{2,1,0:T(8,128)(2,1)}, bf16[2,48,768]{2,1,0:T(8,128)(2,1)S(1)}, u32[]{:S(2)}) copy-start(bf16[2,48,768]{2,1,0:T(8,128)(2,1)S(1)} %collective-permute-done.12.refs_6_) | copy-start | bytes 442372
  140.8 0.7 copy-start.14
Sparse Core Ops, SparseCore 0:
  23.0 98.3 reduce-scatter.1

commit v4 on v2

--- a/solution.py
+++ b/solution.py
@@ -20,8 +20,6 @@
 F32 = jnp.float32
 BF16 = jnp.bfloat16
 
-ROLE = ((6, 4, 0, 3), (7, 1, 2, 5))
-
 
 def normalize(values):
     center = values - jnp.mean(values, axis=-1, keepdims=True)
@@ -51,7 +49,7 @@
 
 def send_out(stage, outs, sems):
     copies = [
-        pltpu.make_async_copy(stage.at[pl.ds(8 * k, 8)], out, sems.at[k])
+        pltpu.make_async_copy(stage.at[pl.ds(8 * k, 8)], out, sems.at[k, 0])
         for k, out in enumerate(outs)
     ]
     for copy in copies:
@@ -60,6 +58,17 @@
         copy.wait()
 
 
+def send_out(stage, outs, sems):
+    copies = [
+        pltpu.make_async_copy(stage.at[pl.ds(8 * k, 8)], out, sems.at[k, 0])
+        for k, out in enumerate(outs)
+    ]
+    for copy in copies:
+        copy.start()
+    for copy in copies:
+        copy.wait()
+
+
 def forward_kernel(dest, mix, out_grad, w_up, w_down, gain_first, gain_second, *refs):
     hidden, slope, grad_wide, grad_mid = refs[:4]
     outs, (active, stage, sems) = refs[4:12], refs[12:]
@@ -112,6 +121,17 @@
     turned, grad_hidden, stage, sems = refs[9:]
     step = pl.program_id(0)
 
+    def copies(part):
+        axis, half = part // 2, part % 2
+        return [
+            pltpu.make_async_copy(
+                stage.at[pl.ds((k * 2 + half) * SIDE, SIDE)],
+                outs[k].at[pl.ds(half * SIDE, SIDE)],
+                sems.at[k, half],
+            )
+            for k in range(axis * SIDE, (axis + 1) * SIDE)
+        ]
+
     @pl.when(step == 0)
     def _():
         turned[...] = hidden[...].T
@@ -121,6 +141,13 @@
     part = jnp.dot(turned[...], grad_pre, preferred_element_type=F32).astype(BF16)
     for k in range(16):
         stage[dest[k * 4 + step]] = part[k * BLOCK : (k + 1) * BLOCK]
+    for q in range(SIDE):
+
+        @pl.when(step == q)
+        def _():
+            for copy in copies(q):
+                copy.start()
+
     part = contract_cols(grad_pre, w_up[...])
 
     @pl.when(step == 0)
@@ -136,7 +163,9 @@
         normed, inv_scale = normalize(mix[...].astype(F32))
         total = norm_back(grad_hidden[...] * gain_first[...], normed, inv_scale)
         grad_sum[...] = total.T.astype(BF16)
-        send_out(stage, outs, sems)
+        for q in range(SIDE):
+            for copy in copies(q):
+                copy.wait()
 
 
 def seat_kernel(grad_sum, swapped, owner, slot, sent):
@@ -167,59 +196,25 @@
     return total
 
 
-def first_kernel(*refs):
-    ins, outs = refs[:-4], refs[-4:]
+def line_kernel(*refs):
+    ins, outs = refs[:8], refs[-8:]
     for axis in range(2):
-        for mat in range(2):
-            keep, up, down = ins[(axis * 2 + mat) * 3 : (axis * 2 + mat) * 3 + 3]
-            rows = pl.ds(mat * SIDE, SIDE)
-            outs[axis * 2][rows] = add(keep[:SIDE], up[...]).astype(BF16)
-            outs[axis * 2 + 1][rows] = add(keep[SIDE:], down[...]).astype(BF16)
-
-
-def second_kernel(*refs):
-    ins, outs = refs[:-8], refs[-8:]
-    for axis in range(2):
-        up2, down2, mid2, keep2 = outs[axis * 4 : axis * 4 + 4]
-        here = ins[axis * 8 : axis * 8 + 8]
-        for mat in range(2):
-            keep, up, down = here[mat * 3 : mat * 3 + 3]
-            rows = slice(mat * SIDE, (mat + 1) * SIDE)
-            low = add(keep[:SIDE], down[...], here[6][rows])
-            high = add(keep[SIDE:], up[...], here[7][rows])
-            up2[2 * mat] = low[2].astype(BF16)
-            up2[2 * mat + 1] = high[1].astype(BF16)
-            down2[2 * mat] = high[2].astype(BF16)
-            down2[2 * mat + 1] = low[3].astype(BF16)
-            mid2[2 * mat] = low[1].astype(BF16)
-            mid2[2 * mat + 1] = high[3].astype(BF16)
-            keep2[2 * mat] = low[0]
-            keep2[2 * mat + 1] = high[0]
-
-
-def third_kernel(*refs):
-    ins, outs = refs[:-4], refs[-4:]
-    for axis in range(2):
-        mid2, up2, down2 = ins[axis * 3 : axis * 3 + 3]
-        for mat in range(2):
-            outs[axis * 2][mat] = add(mid2[2 * mat], up2[2 * mat]).astype(BF16)
-            outs[axis * 2 + 1][mat] = add(mid2[2 * mat + 1], down2[2 * mat]).astype(BF16)
+        total = add(*(ref[...] for ref in ins[axis * SIDE : (axis + 1) * SIDE]))
+        for half in range(2):
+            for away in range(SIDE):
+                out = outs[axis * SIDE + away]
+                out[half] = total[half * SIDE + away].astype(out.dtype)
 
 
 def last_kernel(*refs):
     ins, (grad_up, grad_down) = refs[:-2], refs[-2:]
     width = grad_down.shape[1]
     for axis in range(2):
-        keep2, up2, down2, low2, high2 = ins[axis * 5 : axis * 5 + 5]
-        for mat in range(2):
-            low = add(keep2[2 * mat], down2[2 * mat + 1], low2[mat])
-            high = add(keep2[2 * mat + 1], up2[2 * mat + 1], high2[mat])
-            for half, value in enumerate((low, high)):
-                part = 2 * axis + half
-                if mat == 0:
-                    grad_down[part * BLOCK : (part + 1) * BLOCK, :] = value
-                else:
-                    grad_up[:, part * width : (part + 1) * width] = value
+        for half in range(2):
+            part = 2 * axis + half
+            here = ins[axis * SIDE : (axis + 1) * SIDE]
+            grad_down[part * BLOCK : (part + 1) * BLOCK, :] = add(*(ref[half] for ref in here))
+            grad_up[:, part * width : (part + 1) * width] = add(*(ref[2 + half] for ref in here))
 
 
 def moves(axis, sign):
@@ -247,11 +242,7 @@
     axis, half = part // 2, part % 2
     first = jnp.where(axis == 0, away_x, away_y)
     inner = jnp.where(axis == 0, away_y, away_x)
-    role = jnp.zeros_like(flat)
-    for h in range(2):
-        for d in range(SIDE):
-            role = jnp.where((half == h) & (first == d), ROLE[h][d], role)
-    return (axis * 8 + role) * SIDE + inner
+    return ((axis * SIDE + first) * 2 + half) * SIDE + inner
 
 
 def params(*semantics, limit=60):
@@ -284,7 +275,7 @@
     tall = whole((rows, width))
     gain = whole((1, width))
     clamp = lambda i: jnp.minimum(i, SIDE - 1)
-    stage = [pltpu.VMEM((64, BLOCK, width), BF16), pltpu.SemaphoreType.DMA((8,))]
+    stage = [pltpu.VMEM((64, BLOCK, width), BF16), pltpu.SemaphoreType.DMA((8, 2))]
     matmul = 2 * rows * width * hidden_units
     hidden, slope, grad_wide, grad_mid, *down_parts = pl.pallas_call(
         forward_kernel,
@@ -317,11 +308,14 @@
         + [group] * 8,
         compiler_params=params("arbitrary"),
         cost_estimate=cost(3 * matmul, 25_000_000),
+        name="forward_and_grad_down",
     )(dest, mix, out_g, up_mat, down_mat, gain_first, gain_second)
 
-    down_got = [
-        (shift(down_parts[4 * a], a, 1), shift(down_parts[4 * a + 1], a, -1)) for a in range(2)
-    ]
+    def send(parts, a, away):
+        return shift(parts[a * SIDE + away], a, away)
+
+    first_got = [send(down_parts, 0, 1), send(down_parts, 0, 2), send(down_parts, 0, 3)]
+    first_got += [send(down_parts, 1, 1), send(down_parts, 1, 3)]
 
     grad_sum, *up_parts = pl.pallas_call(
         backward_kernel,
@@ -345,12 +339,16 @@
         out_shape=[jax.ShapeDtypeStruct((width, rows), BF16)] + [group] * 8,
         compiler_params=params("arbitrary"),
         cost_estimate=cost(3 * matmul, 25_000_000),
+        name="backward_and_grad_up",
     )(dest, mix, hidden, slope, grad_wide, grad_mid, up_mat, down_mat, gain_first)
 
-    leaving = [up_parts[k] for k in (0, 1, 4, 5)]
-    leaving, grad_sum, down_got = lax.optimization_barrier((leaving, grad_sum, down_got))
-    up_parts = [*leaving[:2], *up_parts[2:4], *leaving[2:], *up_parts[6:]]
-    up_got = [(shift(up_parts[4 * a], a, 1), shift(up_parts[4 * a + 1], a, -1)) for a in range(2)]
+    leaving = [up_parts[a * SIDE + away] for a in range(2) for away in range(1, SIDE)]
+    leaving, last_down, grad_sum, first_got = lax.optimization_barrier(
+        (leaving, down_parts[SIDE + 2], grad_sum, first_got)
+    )
+    down_got = first_got[:4] + [shift(last_down, 1, 2)] + first_got[4:]
+    up_parts = [up_parts[0], *leaving[:3], up_parts[SIDE], *leaving[3:]]
+    up_got = [send(up_parts, a, away) for a in range(2) for away in range(1, SIDE)]
 
     swapped = lax.all_to_all(
         grad_sum.reshape(pieces, width // pieces, rows),
@@ -360,34 +358,26 @@
         tiled=True,
     ).reshape(width, rows)
 
-    mats = ((down_parts, down_got), (up_parts, up_got))
-
     def lines(count, part=0):
         return pl.BlockSpec((count, ROWS, width), lambda i: (part, i, 0))
 
-    def combine(kernel, specs, args, counts, dtypes, name):
+    def line_sums(parts, got, mat, before=()):
         return pl.pallas_call(
-            kernel,
+            line_kernel,
             grid=(BLOCK // ROWS,),
-            in_specs=specs,
-            out_specs=[lines(n) for n in counts],
+            in_specs=[lines(8)] * 8 + [ANY] * len(before),
+            out_specs=[lines(2, mat)] * 8,
             out_shape=[
-                jax.ShapeDtypeStruct((n, BLOCK, width), t) for n, t in zip(counts, dtypes)
+                jax.ShapeDtypeStruct((4, BLOCK, width), t) for t in [F32, BF16, BF16, BF16] * 2
             ],
+            input_output_aliases={8 + k: k for k in range(len(before))},
             compiler_params=params("arbitrary"),
             cost_estimate=cost(1_000_000, 7_000_000),
-            name=name,
-        )(*args)
-
-    args, specs = [], []
-    for a in range(2):
-        for parts, got in mats:
-            args += [parts[4 * a + 2], *got[a]]
-            specs += [lines(8), lines(4), lines(4)]
-    both = combine(first_kernel, specs, args, [8] * 4, [BF16] * 4, "first_sums")
-    both_got = [shift(both[2 * a + s], a, 1 - 2 * s) for a in range(2) for s in range(2)]
-
-    swapped, _ = lax.optimization_barrier((swapped, both))
+            name="line_sums",
+        )(parts[0], *got[:3], parts[SIDE], *got[3:], *before)
+
+    summed = line_sums(down_parts, down_got, 0)
+    swapped, _ = lax.optimization_barrier((swapped, up_got + down_got))
     sent = pl.pallas_call(
         seat_kernel,
         out_shape=jax.ShapeDtypeStruct((owners, SEAT, width), BF16),
@@ -396,27 +386,11 @@
     )(grad_sum, swapped, owner_dev.reshape(1, rows), slot_row)
     landed = lax.all_to_all(sent, "dp", split_axis=0, concat_axis=0, tiled=True)
 
-    args, specs = [], []
-    for a in range(2):
-        for parts, got in mats:
-            args += [parts[4 * a + 3], *got[a]]
-            specs += [lines(8), lines(4, 1), lines(4, 1)]
-        args += both_got[2 * a : 2 * a + 2]
-        specs += [lines(8), lines(8)]
-    second = combine(
-        second_kernel, specs, args, [4] * 8, [BF16, BF16, BF16, F32] * 2, "second_sums"
-    )
-    second_got = [shift(second[4 * a + s], 1 - a, 1 - 2 * s) for a in range(2) for s in range(2)]
-
+    summed = line_sums(up_parts, up_got, 1, summed)
     args = []
     for a in range(2):
-        args += [second[4 * a + 2], *second_got[2 * a : 2 * a + 2]]
-    third = combine(third_kernel, [lines(4)] * 6, args, [2] * 4, [BF16] * 4, "third_sums")
-    third_got = [shift(third[2 * a + s], 1 - a, 1 - 2 * s) for a in range(2) for s in range(2)]
-
-    args = []
-    for a in range(2):
-        args += [second[4 * a + 3], *second_got[2 * a : 2 * a + 2], *third_got[2 * a : 2 * a + 2]]
+        args += [summed[a * SIDE]]
+        args += [shift(summed[a * SIDE + away], 1 - a, away) for away in range(1, SIDE)]
     grad_up, grad_down = pl.pallas_call(
         last_kernel,
         out_shape=[

time: 154 us -> 161 us (1.045); the launches traced: 153 us -> 158 us
  waiting for transfers between devices: 52.2 us -> 60.5 us
  Pallas kernels: 53.2 us -> 47.6 us
  starting transfers between devices: 41.8 us -> 43.6 us
    ppermute x20 -> x18, waiting for transfers between devices: 52.1 us -> 60.5 us  [shift(): return lax.ppermute(value, 'dp', moves(axis, sign))]
    pallas_call x3 -> x2, Pallas kernels: 13.6 us -> 8.91 us  [line_sums(): pl.pallas_call(line_kernel, grid=(BLOCK // ROWS,), in_specs=[lines(8)] *...]
    ppermute x20 -> x18, starting transfers between devices: 26.8 us -> 28.1 us  [shift(): return lax.ppermute(value, 'dp', moves(axis, sign))]
  transfers between devices with their start and end apart: 22 -> 20, of which waited for: 11 -> 8; matrix products, arithmetic and copies ran while one was open for 0% -> 0% of each run, Pallas kernels for 20% -> 16%
where the time goes in v4:
time: 161 us; the launch traced here: 158 us
  waiting for transfers between devices  60.5 us (38%)
  Pallas kernels  47.6 us (30%)
  starting transfers between devices  43.6 us (27%)
  local copies, waits for them, and re-layouts  3.18 us (2%)
  matrix products  1.68 us (1%)
    ppermute x18, waiting for transfers between devices, shift(): return lax.ppermute(value, 'dp', moves(axis, sign))  60.5 us
    ppermute x18, starting transfers between devices, shift(): return lax.ppermute(value, 'dp', moves(axis, sign))  28.1 us
    pallas_call x1, Pallas kernels, per_device(): pl.pallas_call(forward_kernel, grid_spec=pltpu.PrefetchScalarGridSpec(num...  18.2 us
    pallas_call x1, Pallas kernels, per_device(): pl.pallas_call(backward_kernel, grid_spec=pltpu.PrefetchScalarGridSpec(nu...  13.7 us
    pallas_call x2, Pallas kernels, line_sums(): pl.pallas_call(line_kernel, grid=(BLOCK // ROWS,), in_specs=[lines(8)] *...  8.91 us
    all_to_all x1, starting transfers between devices, per_device(): lax.all_to_all(grad_sum.reshape(pieces, width // pieces, rows), 'token',...  8.56 us
    all_to_all x1, starting transfers between devices, per_device(): landed = lax.all_to_all(sent, 'dp', split_axis=0, concat_axis=0, tiled=True)  6.88 us
    pallas_call x1, Pallas kernels, per_device(): pl.pallas_call(seat_kernel, out_shape=jax.ShapeDtypeStruct((owners, SEAT,...  3.74 us
  transfers between devices with their start and end apart: 20, of which 8 were waited for; matrix products, arithmetic and copies ran while one was open for 0% of the time, Pallas kernels for 16%

profile of v4, /device:TPU:6, one launch (start us, length us, event | category | flops | bytes accessed | tf_op | source)
XLA Modules:
  0.0 158.0 jit_solution(7455207110278647264)
XLA Ops:
  0.6 0.6 fusion.4.dest
  1.3 18.2 %forward_and_grad_down.1 = (bf16[384,768]{1,0:T(8,128)(2,1)}, f32[4,384,768]{2,1,0:T(8,128)}, f32[384,768]{1,0:T(8,128)}, bf16[384,768]{1,0:T(8,128)(2,1)}, bf16...) custom-call(s32[64]{0:T(128)} %fusion.4.dest, ...), custom_call_target="tpu_custom_call" | custom-call | flops 5435817984 | bytes 25000000 | tf_op jit(solution)/shard_map/forward_and_grad_down/pallas_call | solution.py:280
  19.5 2.3 %collective-permute-start = (bf16[8,48,768]{2,1,0:T(8,128)(2,1)}, bf16[8,48,768]{2,1,0:T(8,128)(2,1)S(1)}, u32[]{:S(2)}, u32[]{:S(2)}) collective-permute-start(bf16[8,48,768]{2,1,0:T(8,128)(2,1)} %get-tuple-element.69), channel_id=1, source_target_pairs={{0,16},{16,32},{32,48},{48,0},{64,80},{80,96},{96,112},{112,64},{1... | collective-permute-start | bytes 1769480 | tf_op jit(solution)/shard_map/ppermute | solution.py:233
  21.8 0.7 collective-permute-start.1
  22.5 0.3 collective-permute-start.2
  22.8 1.3 collective-permute-start.3
  24.1 1.9 %collective-permute-start.4 = (bf16[8,48,768]{2,1,0:T(8,128)(2,1)}, bf16[8,48,768]{2,1,0:T(8,128)(2,1)}, u32[]{:S(2)}, u32[]{:S(2)}) collective-permute-start(bf16[8,48,768]{2,1,0:T(8,128)(2,1)} %get-tuple-element.73), channel_id=1, source_target_pairs={{0,192},{16,208},{32,224},{48,240},{64,0},{80,16},{96,32},{112,48}... | collective-permute-start | bytes 1769480 | tf_op jit(solution)/shard_map/ppermute | solution.py:233
  26.0 13.7 %backward_and_grad_up.1 = (bf16[768,384]{1,0:T(8,128)(2,1)}, bf16[8,48,768]{2,1,0:T(8,128)(2,1)}, bf16[8,48,768]{2,1,0:T(8,128)(2,1)}, bf16[8,48,768]{2,1,0:T(8,...) custom-call(s32[64]{0:T(128)} %fusion.4.dest, ...), custom_call_target="tpu_custom_call" | custom-call | flops 5435817984 | bytes 25000000 | tf_op jit(solution)/shard_map/backward_and_grad_up/pallas_call | solution.py:320
  39.8 0.0 collective-permute-done.refs_1_
  39.8 0.0 copy-start.1
  39.8 0.1 collective-permute-done.1.refs_2_
  39.8 9.3 %collective-permute-done.2.refs_3_ = bf16[8,48,768]{2,1,0:T(8,128)(2,1)S(1)} collective-permute-done((bf16[8,48,768]{2,1,0:T(8,128)(2,1)}, bf16[8,48,768]{2,1,0:T(8,128)(2,1)S(1)}, u32[]{:S(2)}, u32[]{:S(2)}) %collective-permute-start.2) | collective-permute-done | bytes 589856 | tf_op jit(solution)/shard_map/ppermute | solution.py:233
  49.1 0.0 collective-permute-done.3.refs_5_
  49.1 0.0 collective-permute-done.4.refs_7_
  49.1 1.2 collective-permute-start.5
  50.3 2.0 %collective-permute-start.6 = (bf16[8,48,768]{2,1,0:T(8,128)(2,1)}, bf16[8,48,768]{2,1,0:T(8,128)(2,1)}, u32[]{:S(2)}, u32[]{:S(2)}) collective-permute-start(bf16[8,48,768]{2,1,0:T(8,128)(2,1)} %get-tuple-element.75), channel_id=1, source_target_pairs={{0,32},{16,48},{32,0},{48,16},{64,96},{80,112},{96,64},{112,80},{1... | collective-permute-start | bytes 1769480 | tf_op jit(solution)/shard_map/ppermute | solution.py:233
  52.3 8.6 %all-to-all-start = ((bf16[16,48,384]{2,1,0:T(8,128)(2,1)}), bf16[16,48,384]{2,1,0:T(8,128)(2,1)S(1)}, u32[]{:S(2)}, u32[]{:S(2)}) async-start(bf16[16,48,384]{2,1,0:T(8,128)(2,1)} %bitcast.14), calls=%async_computation | async-start | bytes 1179648 | tf_op jit(solution)/shard_map/all_to_all | solution.py:353
  60.9 0.2 collective-permute-start.7
  61.1 1.7 %collective-permute-start.8 = (bf16[8,48,768]{2,1,0:T(8,128)(2,1)}, bf16[8,48,768]{2,1,0:T(8,128)(2,1)S(1)}, u32[]{:S(2)}, u32[]{:S(2)}) collective-permute-start(bf16[8,48,768]{2,1,0:T(8,128)(2,1)} %get-tuple-element.78), channel_id=1, source_target_pairs={{0,64},{16,80},{32,96},{48,112},{64,128},{80,144},{96,160},{112,17... | collective-permute-start | bytes 1769480 | tf_op jit(solution)/shard_map/ppermute | solution.py:233
  62.8 2.9 %collective-permute-start.9 = (bf16[8,48,768]{2,1,0:T(8,128)(2,1)}, bf16[8,48,768]{2,1,0:T(8,128)(2,1)S(1)}, u32[]{:S(2)}, u32[]{:S(2)}) collective-permute-start(bf16[8,48,768]{2,1,0:T(8,128)(2,1)} %get-tuple-element.79), channel_id=1, source_target_pairs={{0,128},{16,144},{32,160},{48,176},{64,192},{80,208},{96,224},{112... | collective-permute-start | bytes 1769480 | tf_op jit(solution)/shard_map/ppermute | solution.py:233
  65.7 0.0 collective-permute-done.5.refs_1_
  65.7 3.0 %collective-permute-start.10 = (bf16[8,48,768]{2,1,0:T(8,128)(2,1)}, bf16[8,48,768]{2,1,0:T(8,128)(2,1)S(1)}, u32[]{:S(2)}, u32[]{:S(2)}) collective-permute-start(bf16[8,48,768]{2,1,0:T(8,128)(2,1)} %get-tuple-element.80), channel_id=1, source_target_pairs={{0,192},{16,208},{32,224},{48,240},{64,0},{80,16},{96,32},{112,48}... | collective-permute-start | bytes 1769480 | tf_op jit(solution)/shard_map/ppermute | solution.py:233
  68.7 0.0 copy-done.5
  68.7 0.0 collective-permute-done.6.refs_2_
  68.7 0.0 copy-done.16
  68.7 2.0 %collective-permute-start.11 = (bf16[8,48,768]{2,1,0:T(8,128)(2,1)S(1)}, bf16[8,48,768]{2,1,0:T(8,128)(2,1)S(1)}, u32[]{:S(2)}, u32[]{:S(2)}) collective-permute-start(bf16[8,48,768]{2,1,0:T(8,128)(2,1)S(1)} %copy-done.16), channel_id=1, source_target_pairs={{0,128},{16,144},{32,160},{48,176},{64,192},{80,208},{96,224},{112... | collective-permute-start | bytes 1769480 | tf_op jit(solution)/shard_map/ppermute | solution.py:233
  70.7 8.2 %collective-permute-done.7.refs_3_ = bf16[8,48,768]{2,1,0:T(8,128)(2,1)S(1)} collective-permute-done((bf16[8,48,768]{2,1,0:T(8,128)(2,1)}, bf16[8,48,768]{2,1,0:T(8,128)(2,1)S(1)}, u32[]{:S(2)}, u32[]{:S(2)}) %collective-permute-start.7) | collective-permute-done | bytes 589856 | tf_op jit(solution)/shard_map/ppermute | solution.py:233
  78.9 0.0 collective-permute-done.8.refs_5_
  78.9 13.8 %collective-permute-done.9.refs_6_ = bf16[8,48,768]{2,1,0:T(8,128)(2,1)S(1)} collective-permute-done((bf16[8,48,768]{2,1,0:T(8,128)(2,1)}, bf16[8,48,768]{2,1,0:T(8,128)(2,1)S(1)}, u32[]{:S(2)}, u32[]{:S(2)}) %collective-permute-start.9) | collective-permute-done | bytes 589856 | tf_op jit(solution)/shard_map/ppermute | solution.py:233
  92.7 0.0 collective-permute-done.10.refs_7_
  92.7 0.0 copy-done.6
  92.7 0.0 copy-done.7
  92.7 0.8 copy-done.8
  93.5 0.8 copy-done.9
  94.3 10.4 %collective-permute-done.11.refs_6_ = bf16[8,48,768]{2,1,0:T(8,128)(2,1)S(1)} collective-permute-done((bf16[8,48,768]{2,1,0:T(8,128)(2,1)S(1)}, bf16[8,48,768]{2,1,0:T(8,128)(2,1)S(1)}, u32[]{:S(2)}, u32[]{:S(2)}) %collective-permute-start.11) | collective-permute-done | bytes 589856 | tf_op jit(solution)/shard_map/ppermute | solution.py:233
  104.8 0.0 all-to-all-done
  104.8 0.9 copy-done
  105.6 3.7 %shard_map.103 = bf16[16,64,768]{2,1,0:T(8,128)(2,1)} custom-call(bf16[768,384]{1,0:T(8,128)(2,1)} %get-tuple-element.107.grad_sum, bf16[768,384]{1,0:T(8,128)(2,1)} %bitcast.15, s32[1,384]{1,0:T(1,128)} %bitcast.17, s32[1,384]{1,0:T(1,128)} %slot.1), custom_call_target="tpu_custom_call" | custom-call | flops 603979776 | bytes 4000000 | tf_op jit(solution)/shard_map/pallas_call | solution.py:381
  109.4 0.0 copy-done.1
  109.4 0.0 copy-done.2
  109.4 0.0 copy-done.4
  109.4 6.9 %all-to-all-start.1 = ((bf16[16,64,768]{2,1,0:T(8,128)(2,1)}), bf16[16,64,768]{2,1,0:T(8,128)(2,1)S(1)}, u32[]{:S(2)}, u32[]{:S(2)}) async-start(bf16[16,64,768]{2,1,0:T(8,128)(2,1)} %shard_map.103), calls=%async_computation.1 | async-start | bytes 3145728 | tf_op jit(solution)/shard_map/all_to_all | solution.py:387
  116.2 0.0 copy-done.3
  116.3 4.5 %line_sums.2 = (f32[4,48,768]{2,1,0:T(8,128)}, bf16[4,48,768]{2,1,0:T(8,128)(2,1)}, bf16[4,48,768]{2,1,0:T(8,128)(2,1)}, bf16[4,48,768]{2,1,0:T(8,128)(2,1)}, f3...) custom-call(bf16[8,48,768]{2,1,0:T(8,128)(2,1)} %get-tuple-element.8, ...), custom_call_target="tpu_custom_call" | custom-call | flops 1000000 | bytes 7000000 | tf_op jit(solution)/shard_map/line_sums/pallas_call | solution.py:365
  120.7 4.4 %line_sums.3 = (f32[4,48,768]{2,1,0:T(8,128)}, bf16[4,48,768]{2,1,0:T(8,128)(2,1)}, bf16[4,48,768]{2,1,0:T(8,128)(2,1)}, bf16[4,48,768]{2,1,0:T(8,128)(2,1)}, f3...) custom-call(bf16[8,48,768]{2,1,0:T(8,128)(2,1)} %get-tuple-element.6, ...), custom_call_target="tpu_custom_call", output_to_operand_aliasing={{0}: (8, {}), {1}: (9, {}), {2}: (10, {}), {3}: (11, {}), {... | custom-call | flops 1000000 | bytes 7000000 | tf_op jit(solution)/shard_map/line_sums/pallas_call | solution.py:365
  125.2 1.5 collective-permute-start.12
  126.7 2.7 %collective-permute-start.13 = (bf16[4,48,768]{2,1,0:T(8,128)(2,1)}, bf16[4,48,768]{2,1,0:T(8,128)(2,1)S(1)}, u32[]{:S(2)}, u32[]{:S(2)}) collective-permute-start(bf16[4,48,768]{2,1,0:T(8,128)(2,1)} %get-tuple-element.99), channel_id=1, source_target_pairs={{0,128},{16,144},{32,160},{48,176},{64,192},{80,208},{96,224},{112... | collective-permute-start | bytes 884744 | tf_op jit(solution)/shard_map/ppermute | solution.py:233
  129.4 1.5 collective-permute-start.14
  130.9 0.6 collective-permute-start.15
  131.4 2.4 %collective-permute-start.16 = (bf16[4,48,768]{2,1,0:T(8,128)(2,1)}, bf16[4,48,768]{2,1,0:T(8,128)(2,1)S(1)}, u32[]{:S(2)}, u32[]{:S(2)}) collective-permute-start(bf16[4,48,768]{2,1,0:T(8,128)(2,1)} %get-tuple-element.103), channel_id=1, source_target_pairs={{0,32},{16,48},{32,0},{48,16},{64,96},{80,112},{96,64},{112,80},{1... | collective-permute-start | bytes 884744 | tf_op jit(solution)/shard_map/ppermute | solution.py:233
  133.8 9.0 %collective-permute-done.12.refs_1_ = bf16[4,48,768]{2,1,0:T(8,128)(2,1)S(1)} collective-permute-done((bf16[4,48,768]{2,1,0:T(8,128)(2,1)}, bf16[4,48,768]{2,1,0:T(8,128)(2,1)S(1)}, u32[]{:S(2)}, u32[]{:S(2)}) %collective-permute-start.12) | collective-permute-done | bytes 294944 | tf_op jit(solution)/shard_map/ppermute | solution.py:233
  142.8 0.0 collective-permute-start.17
  142.8 5.3 %collective-permute-done.13.refs_2_ = bf16[4,48,768]{2,1,0:T(8,128)(2,1)S(1)} collective-permute-done((bf16[4,48,768]{2,1,0:T(8,128)(2,1)}, bf16[4,48,768]{2,1,0:T(8,128)(2,1)S(1)}, u32[]{:S(2)}, u32[]{:S(2)}) %collective-permute-start.13) | collective-permute-done | bytes 294944 | tf_op jit(solution)/shard_map/ppermute | solution.py:233
  148.1 0.0 collective-permute-done.14.refs_3_
  148.1 0.0 collective-permute-done.15.refs_5_
  148.1 0.0 collective-permute-done.16.refs_6_
  148.1 4.4 %collective-permute-done.17.refs_7_ = bf16[4,48,768]{2,1,0:T(8,128)(2,1)S(1)} collective-permute-done((bf16[4,48,768]{2,1,0:T(8,128)(2,1)}, bf16[4,48,768]{2,1,0:T(8,128)(2,1)S(1)}, u32[]{:S(2)}, u32[]{:S(2)}) %collective-permute-start.17) | collective-permute-done | bytes 294944 | tf_op jit(solution)/shard_map/ppermute | solution.py:233
  152.6 0.0 copy-done.11
  152.6 0.0 copy-done.13
  152.6 0.0 copy-done.14
  152.6 0.7 copy-done.15
  153.3 3.0 %last_sums.1 = (f32[48,3072]{1,0:T(8,128)}, f32[192,768]{1,0:T(8,128)}) custom-call(f32[4,48,768]{2,1,0:T(8,128)} %get-tuple-element.97.refs_0_, bf16[4,48,768]{2,1,0:T(8,128)(2,1)} %copy-done.10, bf16[4,48,768]{2,1,0:T(8,128)(2,1)} %copy-done.11, bf16[4,48,768]{2,1,0:T(8,128)(2,1)} %copy-done.12, f32[4,48,768]{2,1,0:T(8,128)} %get-tuple-element.101.refs_4_, ...), custom_call_target="tpu_custom_call" | custom-call | flops 1000000 | bytes 4000000 | tf_op jit(solution)/shard_map/last_sums/pallas_call | solution.py:394
  156.2 0.0 all-to-all-done.1
  156.3 1.7 %convolution_bitcast_fusion = f32[1,256,768]{2,1,0:T(8,128)} fusion(bf16[16,64,768]{2,1,0:T(8,128)(2,1)S(1)} %all-to-all-done.1, s32[16,64]{1,0:T(8,128)S(1)} %bitcast.16), kind=kOutput, calls=%fused_computation | convolution fusion | flops 402915328 | bytes 2363392 | tf_op jit(solution)/shard_map/dot_general | solution.py:409
  (19 shorter events, 0.0 us)
Async XLA Ops:
  19.5 20.2 %collective-permute-start = (bf16[8,48,768]{2,1,0:T(8,128)(2,1)}, bf16[8,48,768]{2,1,0:T(8,128)(2,1)S(1)}, u32[]{:S(2)}, u32[]{:S(2)}) collective-permute-start(bf16[8,48,768]{2,1,0:T(8,128)(2,1)} %get-tuple-element.69), channel_id=1, source_target_pairs={{0,16},{16,32},{32,48},{48,0},{64,80},{80,96},{96,112},{112,64},{1... | collective-permute-start | bytes 1769480 | tf_op jit(solution)/shard_map/ppermute | solution.py:233
  21.8 18.0 %collective-permute-start.1 = (bf16[8,48,768]{2,1,0:T(8,128)(2,1)}, bf16[8,48,768]{2,1,0:T(8,128)(2,1)S(1)}, u32[]{:S(2)}, u32[]{:S(2)}) collective-permute-start(bf16[8,48,768]{2,1,0:T(8,128)(2,1)} %get-tuple-element.70), channel_id=1, source_target_pairs={{0,32},{16,48},{32,0},{48,16},{64,96},{80,112},{96,64},{112,80},{1... | collective-permute-start | bytes 1769480 | tf_op jit(solution)/shard_map/ppermute | solution.py:233
  22.5 26.6 %collective-permute-start.2 = (bf16[8,48,768]{2,1,0:T(8,128)(2,1)}, bf16[8,48,768]{2,1,0:T(8,128)(2,1)S(1)}, u32[]{:S(2)}, u32[]{:S(2)}) collective-permute-start(bf16[8,48,768]{2,1,0:T(8,128)(2,1)} %get-tuple-element.71), channel_id=1, source_target_pairs={{0,48},{16,0},{32,16},{48,32},{64,112},{80,64},{96,80},{112,96},{1... | collective-permute-start | bytes 1769480 | tf_op jit(solution)/shard_map/ppermute | solution.py:233
  22.8 26.4 %collective-permute-start.3 = (bf16[8,48,768]{2,1,0:T(8,128)(2,1)}, bf16[8,48,768]{2,1,0:T(8,128)(2,1)}, u32[]{:S(2)}, u32[]{:S(2)}) collective-permute-start(bf16[8,48,768]{2,1,0:T(8,128)(2,1)} %get-tuple-element.72), channel_id=1, source_target_pairs={{0,64},{16,80},{32,96},{48,112},{64,128},{80,144},{96,160},{112,17... | collective-permute-start | bytes 1769480 | tf_op jit(solution)/shard_map/ppermute | solution.py:233
  24.1 25.1 %collective-permute-start.4 = (bf16[8,48,768]{2,1,0:T(8,128)(2,1)}, bf16[8,48,768]{2,1,0:T(8,128)(2,1)}, u32[]{:S(2)}, u32[]{:S(2)}) collective-permute-start(bf16[8,48,768]{2,1,0:T(8,128)(2,1)} %get-tuple-element.73), channel_id=1, source_target_pairs={{0,192},{16,208},{32,224},{48,240},{64,0},{80,16},{96,32},{112,48}... | collective-permute-start | bytes 1769480 | tf_op jit(solution)/shard_map/ppermute | solution.py:233
  26.0 42.7 %copy-start.16 = (bf16[8,48,768]{2,1,0:T(8,128)(2,1)S(1)}, bf16[8,48,768]{2,1,0:T(8,128)(2,1)}, u32[]{:S(2)}) copy-start(bf16[8,48,768]{2,1,0:T(8,128)(2,1)} %get-tuple-element.87) | copy-start | bytes 1769476
  39.8 69.6 %copy-start.1 = (bf16[8,48,768]{2,1,0:T(8,128)(2,1)}, bf16[8,48,768]{2,1,0:T(8,128)(2,1)S(1)}, u32[]{:S(2)}) copy-start(bf16[8,48,768]{2,1,0:T(8,128)(2,1)S(1)} %collective-permute-done.refs_1_) | copy-start | bytes 1769476
  39.8 69.5 %copy-start.2 = (bf16[8,48,768]{2,1,0:T(8,128)(2,1)}, bf16[8,48,768]{2,1,0:T(8,128)(2,1)S(1)}, u32[]{:S(2)}) copy-start(bf16[8,48,768]{2,1,0:T(8,128)(2,1)S(1)} %collective-permute-done.1.refs_2_) | copy-start | bytes 1769476
  49.1 67.1 %copy-start.3 = (bf16[8,48,768]{2,1,0:T(8,128)(2,1)}, bf16[8,48,768]{2,1,0:T(8,128)(2,1)S(1)}, u32[]{:S(2)}) copy-start(bf16[8,48,768]{2,1,0:T(8,128)(2,1)S(1)} %collective-permute-done.2.refs_3_) | copy-start | bytes 1769476
  49.1 16.6 %collective-permute-start.5 = (bf16[8,48,768]{2,1,0:T(8,128)(2,1)}, bf16[8,48,768]{2,1,0:T(8,128)(2,1)S(1)}, u32[]{:S(2)}, u32[]{:S(2)}) collective-permute-start(bf16[8,48,768]{2,1,0:T(8,128)(2,1)} %get-tuple-element.74), channel_id=1, source_target_pairs={{0,16},{16,32},{32,48},{48,0},{64,80},{80,96},{96,112},{112,64},{1... | collective-permute-start | bytes 1769480 | tf_op jit(solution)/shard_map/ppermute | solution.py:233
  50.3 18.4 %collective-permute-start.6 = (bf16[8,48,768]{2,1,0:T(8,128)(2,1)}, bf16[8,48,768]{2,1,0:T(8,128)(2,1)}, u32[]{:S(2)}, u32[]{:S(2)}) collective-permute-start(bf16[8,48,768]{2,1,0:T(8,128)(2,1)} %get-tuple-element.75), channel_id=1, source_target_pairs={{0,32},{16,48},{32,0},{48,16},{64,96},{80,112},{96,64},{112,80},{1... | collective-permute-start | bytes 1769480 | tf_op jit(solution)/shard_map/ppermute | solution.py:233
  52.3 52.4 %all-to-all-start = ((bf16[16,48,384]{2,1,0:T(8,128)(2,1)}), bf16[16,48,384]{2,1,0:T(8,128)(2,1)S(1)}, u32[]{:S(2)}, u32[]{:S(2)}) async-start(bf16[16,48,384]{2,1,0:T(8,128)(2,1)} %bitcast.14), calls=%async_computation | async-start | bytes 1179648 | tf_op jit(solution)/shard_map/all_to_all | solution.py:353
  60.9 18.0 %collective-permute-start.7 = (bf16[8,48,768]{2,1,0:T(8,128)(2,1)}, bf16[8,48,768]{2,1,0:T(8,128)(2,1)S(1)}, u32[]{:S(2)}, u32[]{:S(2)}) collective-permute-start(bf16[8,48,768]{2,1,0:T(8,128)(2,1)} %get-tuple-element.76), channel_id=1, source_target_pairs={{0,48},{16,0},{32,16},{48,32},{64,112},{80,64},{96,80},{112,96},{1... | collective-permute-start | bytes 1769480 | tf_op jit(solution)/shard_map/ppermute | solution.py:233
  61.1 17.8 %collective-permute-start.8 = (bf16[8,48,768]{2,1,0:T(8,128)(2,1)}, bf16[8,48,768]{2,1,0:T(8,128)(2,1)S(1)}, u32[]{:S(2)}, u32[]{:S(2)}) collective-permute-start(bf16[8,48,768]{2,1,0:T(8,128)(2,1)} %get-tuple-element.78), channel_id=1, source_target_pairs={{0,64},{16,80},{32,96},{48,112},{64,128},{80,144},{96,160},{112,17... | collective-permute-start | bytes 1769480 | tf_op jit(solution)/shard_map/ppermute | solution.py:233
  62.8 29.9 %collective-permute-start.9 = (bf16[8,48,768]{2,1,0:T(8,128)(2,1)}, bf16[8,48,768]{2,1,0:T(8,128)(2,1)S(1)}, u32[]{:S(2)}, u32[]{:S(2)}) collective-permute-start(bf16[8,48,768]{2,1,0:T(8,128)(2,1)} %get-tuple-element.79), channel_id=1, source_target_pairs={{0,128},{16,144},{32,160},{48,176},{64,192},{80,208},{96,224},{112... | collective-permute-start | bytes 1769480 | tf_op jit(solution)/shard_map/ppermute | solution.py:233
  65.7 3.0 %copy-start.5 = (bf16[8,48,768]{2,1,0:T(8,128)(2,1)}, bf16[8,48,768]{2,1,0:T(8,128)(2,1)S(1)}, u32[]{:S(2)}) copy-start(bf16[8,48,768]{2,1,0:T(8,128)(2,1)S(1)} %collective-permute-done.5.refs_1_) | copy-start | bytes 1769476
  65.7 27.0 %collective-permute-start.10 = (bf16[8,48,768]{2,1,0:T(8,128)(2,1)}, bf16[8,48,768]{2,1,0:T(8,128)(2,1)S(1)}, u32[]{:S(2)}, u32[]{:S(2)}) collective-permute-start(bf16[8,48,768]{2,1,0:T(8,128)(2,1)} %get-tuple-element.80), channel_id=1, source_target_pairs={{0,192},{16,208},{32,224},{48,240},{64,0},{80,16},{96,32},{112,48}... | collective-permute-start | bytes 1769480 | tf_op jit(solution)/shard_map/ppermute | solution.py:233
  68.7 36.0 %collective-permute-start.11 = (bf16[8,48,768]{2,1,0:T(8,128)(2,1)S(1)}, bf16[8,48,768]{2,1,0:T(8,128)(2,1)S(1)}, u32[]{:S(2)}, u32[]{:S(2)}) collective-permute-start(bf16[8,48,768]{2,1,0:T(8,128)(2,1)S(1)} %copy-done.16), channel_id=1, source_target_pairs={{0,128},{16,144},{32,160},{48,176},{64,192},{80,208},{96,224},{112... | collective-permute-start | bytes 1769480 | tf_op jit(solution)/shard_map/ppermute | solution.py:233
  78.9 13.8 %copy-start.6 = (bf16[8,48,768]{2,1,0:T(8,128)(2,1)}, bf16[8,48,768]{2,1,0:T(8,128)(2,1)S(1)}, u32[]{:S(2)}) copy-start(bf16[8,48,768]{2,1,0:T(8,128)(2,1)S(1)} %collective-permute-done.7.refs_3_) | copy-start | bytes 1769476
  78.9 13.8 %copy-start.7 = (bf16[8,48,768]{2,1,0:T(8,128)(2,1)}, bf16[8,48,768]{2,1,0:T(8,128)(2,1)S(1)}, u32[]{:S(2)}) copy-start(bf16[8,48,768]{2,1,0:T(8,128)(2,1)S(1)} %collective-permute-done.8.refs_5_) | copy-start | bytes 1769476
  92.7 0.8 copy-start.8
  93.5 0.8 copy-start.9
  104.8 4.6 %copy-start.4 = (bf16[8,48,768]{2,1,0:T(8,128)(2,1)}, bf16[8,48,768]{2,1,0:T(8,128)(2,1)S(1)}, u32[]{:S(2)}) copy-start(bf16[8,48,768]{2,1,0:T(8,128)(2,1)S(1)} %collective-permute-done.11.refs_6_) | copy-start | bytes 1769476
  104.8 0.9 copy-start
  109.4 46.9 %all-to-all-start.1 = ((bf16[16,64,768]{2,1,0:T(8,128)(2,1)}), bf16[16,64,768]{2,1,0:T(8,128)(2,1)S(1)}, u32[]{:S(2)}, u32[]{:S(2)}) async-start(bf16[16,64,768]{2,1,0:T(8,128)(2,1)} %shard_map.103), calls=%async_computation.1 | async-start | bytes 3145728 | tf_op jit(solution)/shard_map/all_to_all | solution.py:387
  125.2 17.6 %collective-permute-start.12 = (bf16[4,48,768]{2,1,0:T(8,128)(2,1)}, bf16[4,48,768]{2,1,0:T(8,128)(2,1)S(1)}, u32[]{:S(2)}, u32[]{:S(2)}) collective-permute-start(bf16[4,48,768]{2,1,0:T(8,128)(2,1)} %get-tuple-element.98), channel_id=1, source_target_pairs={{0,64},{16,80},{32,96},{48,112},{64,128},{80,144},{96,160},{112,17... | collective-permute-start | bytes 884744 | tf_op jit(solution)/shard_map/ppermute | solution.py:233
  126.7 21.4 %collective-permute-start.13 = (bf16[4,48,768]{2,1,0:T(8,128)(2,1)}, bf16[4,48,768]{2,1,0:T(8,128)(2,1)S(1)}, u32[]{:S(2)}, u32[]{:S(2)}) collective-permute-start(bf16[4,48,768]{2,1,0:T(8,128)(2,1)} %get-tuple-element.99), channel_id=1, source_target_pairs={{0,128},{16,144},{32,160},{48,176},{64,192},{80,208},{96,224},{112... | collective-permute-start | bytes 884744 | tf_op jit(solution)/shard_map/ppermute | solution.py:233
  129.4 18.7 %collective-permute-start.14 = (bf16[4,48,768]{2,1,0:T(8,128)(2,1)}, bf16[4,48,768]{2,1,0:T(8,128)(2,1)S(1)}, u32[]{:S(2)}, u32[]{:S(2)}) collective-permute-start(bf16[4,48,768]{2,1,0:T(8,128)(2,1)} %get-tuple-element.100), channel_id=1, source_target_pairs={{0,192},{16,208},{32,224},{48,240},{64,0},{80,16},{96,32},{112,48}... | collective-permute-start | bytes 884744 | tf_op jit(solution)/shard_map/ppermute | solution.py:233
  130.9 17.2 %collective-permute-start.15 = (bf16[4,48,768]{2,1,0:T(8,128)(2,1)}, bf16[4,48,768]{2,1,0:T(8,128)(2,1)S(1)}, u32[]{:S(2)}, u32[]{:S(2)}) collective-permute-start(bf16[4,48,768]{2,1,0:T(8,128)(2,1)} %get-tuple-element.102), channel_id=1, source_target_pairs={{0,16},{16,32},{32,48},{48,0},{64,80},{80,96},{96,112},{112,64},{1... | collective-permute-start | bytes 884744 | tf_op jit(solution)/shard_map/ppermute | solution.py:233
  131.4 16.7 %collective-permute-start.16 = (bf16[4,48,768]{2,1,0:T(8,128)(2,1)}, bf16[4,48,768]{2,1,0:T(8,128)(2,1)S(1)}, u32[]{:S(2)}, u32[]{:S(2)}) collective-permute-start(bf16[4,48,768]{2,1,0:T(8,128)(2,1)} %get-tuple-element.103), channel_id=1, source_target_pairs={{0,32},{16,48},{32,0},{48,16},{64,96},{80,112},{96,64},{112,80},{1... | collective-permute-start | bytes 884744 | tf_op jit(solution)/shard_map/ppermute | solution.py:233
  142.8 9.8 %copy-start.10 = (bf16[4,48,768]{2,1,0:T(8,128)(2,1)}, bf16[4,48,768]{2,1,0:T(8,128)(2,1)S(1)}, u32[]{:S(2)}) copy-start(bf16[4,48,768]{2,1,0:T(8,128)(2,1)S(1)} %collective-permute-done.12.refs_1_) | copy-start | bytes 884740
  142.8 9.8 %collective-permute-start.17 = (bf16[4,48,768]{2,1,0:T(8,128)(2,1)}, bf16[4,48,768]{2,1,0:T(8,128)(2,1)S(1)}, u32[]{:S(2)}, u32[]{:S(2)}) collective-permute-start(bf16[4,48,768]{2,1,0:T(8,128)(2,1)} %get-tuple-element.104), channel_id=1, source_target_pairs={{0,48},{16,0},{32,16},{48,32},{64,112},{80,64},{96,80},{112,96},{1... | collective-permute-start | bytes 884744 | tf_op jit(solution)/shard_map/ppermute | solution.py:233
  148.1 4.5 %copy-start.11 = (bf16[4,48,768]{2,1,0:T(8,128)(2,1)}, bf16[4,48,768]{2,1,0:T(8,128)(2,1)S(1)}, u32[]{:S(2)}) copy-start(bf16[4,48,768]{2,1,0:T(8,128)(2,1)S(1)} %collective-permute-done.13.refs_2_) | copy-start | bytes 884740
  148.1 4.5 %copy-start.12 = (bf16[4,48,768]{2,1,0:T(8,128)(2,1)}, bf16[4,48,768]{2,1,0:T(8,128)(2,1)S(1)}, u32[]{:S(2)}) copy-start(bf16[4,48,768]{2,1,0:T(8,128)(2,1)S(1)} %collective-permute-done.14.refs_3_) | copy-start | bytes 884740
  148.1 4.5 %copy-start.13 = (bf16[4,48,768]{2,1,0:T(8,128)(2,1)}, bf16[4,48,768]{2,1,0:T(8,128)(2,1)S(1)}, u32[]{:S(2)}) copy-start(bf16[4,48,768]{2,1,0:T(8,128)(2,1)S(1)} %collective-permute-done.15.refs_5_) | copy-start | bytes 884740
  148.1 4.5 %copy-start.14 = (bf16[4,48,768]{2,1,0:T(8,128)(2,1)}, bf16[4,48,768]{2,1,0:T(8,128)(2,1)S(1)}, u32[]{:S(2)}) copy-start(bf16[4,48,768]{2,1,0:T(8,128)(2,1)S(1)} %collective-permute-done.16.refs_6_) | copy-start | bytes 884740
  152.6 0.7 copy-start.15

commit v5 on v2

--- a/solution.py
+++ b/solution.py
@@ -49,15 +49,10 @@
     return lax.dot_general(left, right, (((1,), (1,)), ((), ())), preferred_element_type=F32)
 
 
-def send_out(stage, outs, sems):
-    copies = [
-        pltpu.make_async_copy(stage.at[pl.ds(8 * k, 8)], out, sems.at[k])
-        for k, out in enumerate(outs)
-    ]
-    for copy in copies:
-        copy.start()
-    for copy in copies:
-        copy.wait()
+def copy_role(stage, outs, axis, role, first, count, sem):
+    start = (axis * 8 + role) * SIDE + first
+    target = outs[axis * SIDE + role // 2].at[pl.ds(role % 2 * SIDE + first, count)]
+    return pltpu.make_async_copy(stage.at[pl.ds(start, count)], target, sem)
 
 
 def forward_kernel(dest, mix, out_grad, w_up, w_down, gain_first, gain_second, *refs):
@@ -94,34 +89,74 @@
         grad_wide[...] = wide
         grad_mid[...] = wide.astype(BF16)
 
+    def copies(s):
+        whole_lines = [
+            copy_role(stage, outs, 1, ROLE[half][s], 0, SIDE, sems.at[s, 8 + half])
+            for half in range(2)
+        ]
+        return whole_lines + [
+            copy_role(stage, outs, 0, role, s, 1, sems.at[s, role]) for role in range(8)
+        ]
+
     @pl.when(step >= SIDE)
     def _():
-        part = contract_rows(active[step - SIDE], grad_mid[...]).astype(BF16)
+        line = lax.rem(dest[4 * SIDE * SIDE] + step - SIDE, SIDE)
+        part = contract_rows(active[line], grad_mid[...]).astype(BF16)
         for k in range(16):
-            stage[dest[(step - SIDE) * 16 + k]] = part[k * BLOCK : (k + 1) * BLOCK]
+            stage[dest[line * 16 + k]] = part[k * BLOCK : (k + 1) * BLOCK]
+
+    for s in range(SIDE):
+
+        @pl.when(step == SIDE + s)
+        def _():
+            for copy in copies(s):
+                copy.start()
 
     @pl.when(step == 2 * SIDE - 1)
     def _():
-        send_out(stage, outs, sems)
-
-
-def backward_kernel(
-    dest, mix, hidden, slope, grad_wide, grad_mid, w_up, w_down, gain_first, *refs
-):
-    grad_sum, outs = refs[0], refs[1:9]
-    turned, grad_hidden, stage, sems = refs[9:]
+        for s in range(SIDE):
+            for copy in copies(s):
+                copy.wait()
+
+
+def grad_up_kernel(dest, hidden, slope, grad_mid, w_down, *refs):
+    grad_pre, outs = refs[0], refs[1:9]
+    turned, stage, sems = refs[9:]
     step = pl.program_id(0)
 
+    def copies(part):
+        axis, half = part // 2, part % 2
+        return [
+            copy_role(stage, outs, axis, ROLE[half][d], 0, SIDE, sems.at[part, d])
+            for d in range(SIDE)
+        ]
+
     @pl.when(step == 0)
     def _():
         turned[...] = hidden[...].T
 
-    grad_act = contract_cols(grad_mid[...], w_down[...])
-    grad_pre = (grad_act * slope[0]).astype(BF16)
-    part = jnp.dot(turned[...], grad_pre, preferred_element_type=F32).astype(BF16)
+    value = (contract_cols(grad_mid[...], w_down[...]) * slope[0]).astype(BF16)
+    grad_pre[0] = value
+    part = jnp.dot(turned[...], value, preferred_element_type=F32).astype(BF16)
     for k in range(16):
         stage[dest[k * 4 + step]] = part[k * BLOCK : (k + 1) * BLOCK]
-    part = contract_cols(grad_pre, w_up[...])
+    for q in range(SIDE):
+
+        @pl.when(step == q)
+        def _():
+            for copy in copies(q):
+                copy.start()
+
+    @pl.when(step == SIDE - 1)
+    def _():
+        for q in range(SIDE):
+            for copy in copies(q):
+                copy.wait()
+
+
+def grad_sum_kernel(mix, grad_pre, grad_wide, w_up, gain_first, grad_sum, grad_hidden):
+    step = pl.program_id(0)
+    part = contract_cols(grad_pre[0], w_up[...])
 
     @pl.when(step == 0)
     def _():
@@ -136,7 +171,6 @@
         normed, inv_scale = normalize(mix[...].astype(F32))
         total = norm_back(grad_hidden[...] * gain_first[...], normed, inv_scale)
         grad_sum[...] = total.T.astype(BF16)
-        send_out(stage, outs, sems)
 
 
 def seat_kernel(grad_sum, swapped, owner, slot, sent):
@@ -180,46 +214,27 @@
 def second_kernel(*refs):
     ins, outs = refs[:-8], refs[-8:]
     for axis in range(2):
-        up2, down2, mid2, keep2 = outs[axis * 4 : axis * 4 + 4]
         here = ins[axis * 8 : axis * 8 + 8]
         for mat in range(2):
             keep, up, down = here[mat * 3 : mat * 3 + 3]
             rows = slice(mat * SIDE, (mat + 1) * SIDE)
             low = add(keep[:SIDE], down[...], here[6][rows])
             high = add(keep[SIDE:], up[...], here[7][rows])
-            up2[2 * mat] = low[2].astype(BF16)
-            up2[2 * mat + 1] = high[1].astype(BF16)
-            down2[2 * mat] = high[2].astype(BF16)
-            down2[2 * mat + 1] = low[3].astype(BF16)
-            mid2[2 * mat] = low[1].astype(BF16)
-            mid2[2 * mat + 1] = high[3].astype(BF16)
-            keep2[2 * mat] = low[0]
-            keep2[2 * mat + 1] = high[0]
-
-
-def third_kernel(*refs):
-    ins, outs = refs[:-4], refs[-4:]
-    for axis in range(2):
-        mid2, up2, down2 = ins[axis * 3 : axis * 3 + 3]
-        for mat in range(2):
-            outs[axis * 2][mat] = add(mid2[2 * mat], up2[2 * mat]).astype(BF16)
-            outs[axis * 2 + 1][mat] = add(mid2[2 * mat + 1], down2[2 * mat]).astype(BF16)
+            for half, total in enumerate((low, high)):
+                for away in range(SIDE):
+                    out = outs[axis * SIDE + away]
+                    out[2 * mat + half] = total[away].astype(out.dtype)
 
 
 def last_kernel(*refs):
     ins, (grad_up, grad_down) = refs[:-2], refs[-2:]
     width = grad_down.shape[1]
     for axis in range(2):
-        keep2, up2, down2, low2, high2 = ins[axis * 5 : axis * 5 + 5]
-        for mat in range(2):
-            low = add(keep2[2 * mat], down2[2 * mat + 1], low2[mat])
-            high = add(keep2[2 * mat + 1], up2[2 * mat + 1], high2[mat])
-            for half, value in enumerate((low, high)):
-                part = 2 * axis + half
-                if mat == 0:
-                    grad_down[part * BLOCK : (part + 1) * BLOCK, :] = value
-                else:
-                    grad_up[:, part * width : (part + 1) * width] = value
+        for half in range(2):
+            part = 2 * axis + half
+            here = ins[axis * SIDE : (axis + 1) * SIDE]
+            grad_down[part * BLOCK : (part + 1) * BLOCK, :] = add(*(ref[half] for ref in here))
+            grad_up[:, part * width : (part + 1) * width] = add(*(ref[2 + half] for ref in here))
 
 
 def moves(axis, sign):
@@ -251,7 +266,8 @@
     for h in range(2):
         for d in range(SIDE):
             role = jnp.where((half == h) & (first == d), ROLE[h][d], role)
-    return (axis * 8 + role) * SIDE + inner
+    places = (axis * 8 + role) * SIDE + inner
+    return jnp.concatenate([places, jnp.full((SIDE,), me // SIDE, jnp.int32)])
 
 
 def params(*semantics, limit=60):
@@ -284,7 +300,7 @@
     tall = whole((rows, width))
     gain = whole((1, width))
     clamp = lambda i: jnp.minimum(i, SIDE - 1)
-    stage = [pltpu.VMEM((64, BLOCK, width), BF16), pltpu.SemaphoreType.DMA((8,))]
+    stage = [pltpu.VMEM((64, BLOCK, width), BF16), pltpu.SemaphoreType.DMA((SIDE, 10))]
     matmul = 2 * rows * width * hidden_units
     hidden, slope, grad_wide, grad_mid, *down_parts = pl.pallas_call(
         forward_kernel,
@@ -317,40 +333,56 @@
         + [group] * 8,
         compiler_params=params("arbitrary"),
         cost_estimate=cost(3 * matmul, 25_000_000),
+        name="forward_and_grad_down",
     )(dest, mix, out_g, up_mat, down_mat, gain_first, gain_second)
 
-    down_got = [
-        (shift(down_parts[4 * a], a, 1), shift(down_parts[4 * a + 1], a, -1)) for a in range(2)
-    ]
-
-    grad_sum, *up_parts = pl.pallas_call(
-        backward_kernel,
+    def send(parts):
+        return [(shift(parts[4 * a], a, 1), shift(parts[4 * a + 1], a, -1)) for a in range(2)]
+
+    down_got = send(down_parts)
+
+    grad_pre, *up_parts = pl.pallas_call(
+        grad_up_kernel,
         grid_spec=pltpu.PrefetchScalarGridSpec(
             num_scalar_prefetch=1,
             grid=(SIDE,),
             in_specs=[
                 tall,
-                tall,
                 pl.BlockSpec((1, rows, chunk), lambda i, _: (i, 0, 0)),
                 tall,
-                tall,
-                pl.BlockSpec((width, chunk), lambda i, _: (0, i)),
                 pl.BlockSpec((chunk, width), lambda i, _: (i, 0)),
-                gain,
             ],
-            out_specs=[whole((width, rows))] + [ANY] * 8,
-            scratch_shapes=[pltpu.VMEM((width, rows), BF16), pltpu.VMEM((rows, width), F32)]
-            + stage,
+            out_specs=[pl.BlockSpec((1, rows, chunk), lambda i, _: (i, 0, 0))] + [ANY] * 8,
+            scratch_shapes=[pltpu.VMEM((width, rows), BF16)] + stage,
         ),
-        out_shape=[jax.ShapeDtypeStruct((width, rows), BF16)] + [group] * 8,
+        out_shape=[jax.ShapeDtypeStruct((SIDE, rows, chunk), BF16)] + [group] * 8,
         compiler_params=params("arbitrary"),
-        cost_estimate=cost(3 * matmul, 25_000_000),
-    )(dest, mix, hidden, slope, grad_wide, grad_mid, up_mat, down_mat, gain_first)
+        cost_estimate=cost(2 * matmul, 20_000_000),
+        name="grad_pre_and_grad_up",
+    )(dest, hidden, slope, grad_mid, down_mat)
 
     leaving = [up_parts[k] for k in (0, 1, 4, 5)]
-    leaving, grad_sum, down_got = lax.optimization_barrier((leaving, grad_sum, down_got))
+    leaving, grad_pre, down_got = lax.optimization_barrier((leaving, grad_pre, down_got))
     up_parts = [*leaving[:2], *up_parts[2:4], *leaving[2:], *up_parts[6:]]
-    up_got = [(shift(up_parts[4 * a], a, 1), shift(up_parts[4 * a + 1], a, -1)) for a in range(2)]
+    up_got = send(up_parts)
+
+    grad_sum = pl.pallas_call(
+        grad_sum_kernel,
+        grid=(SIDE,),
+        in_specs=[
+            tall,
+            pl.BlockSpec((1, rows, chunk), lambda i: (i, 0, 0)),
+            tall,
+            pl.BlockSpec((width, chunk), lambda i: (0, i)),
+            gain,
+        ],
+        out_specs=whole((width, rows)),
+        out_shape=jax.ShapeDtypeStruct((width, rows), BF16),
+        scratch_shapes=[pltpu.VMEM((rows, width), F32)],
+        compiler_params=params("arbitrary"),
+        cost_estimate=cost(matmul, 10_000_000),
+        name="grad_sum",
+    )(mix, grad_pre, grad_wide, up_mat, gain_first)
 
     swapped = lax.all_to_all(
         grad_sum.reshape(pieces, width // pieces, rows),
@@ -394,6 +426,7 @@
         compiler_params=params(),
         cost_estimate=cost(2 * owners * SEAT * rows * width, 4_000_000),
     )(grad_sum, swapped, owner_dev.reshape(1, rows), slot_row)
+    sent, both_got = lax.optimization_barrier((sent, both_got))
     landed = lax.all_to_all(sent, "dp", split_axis=0, concat_axis=0, tiled=True)
 
     args, specs = [], []
@@ -403,20 +436,13 @@
             specs += [lines(8), lines(4, 1), lines(4, 1)]
         args += both_got[2 * a : 2 * a + 2]
         specs += [lines(8), lines(8)]
-    second = combine(
-        second_kernel, specs, args, [4] * 8, [BF16, BF16, BF16, F32] * 2, "second_sums"
-    )
-    second_got = [shift(second[4 * a + s], 1 - a, 1 - 2 * s) for a in range(2) for s in range(2)]
-
+    summed = combine(
+        second_kernel, specs, args, [4] * 8, [F32, BF16, BF16, BF16] * 2, "second_sums"
+    )
     args = []
     for a in range(2):
-        args += [second[4 * a + 2], *second_got[2 * a : 2 * a + 2]]
-    third = combine(third_kernel, [lines(4)] * 6, args, [2] * 4, [BF16] * 4, "third_sums")
-    third_got = [shift(third[2 * a + s], 1 - a, 1 - 2 * s) for a in range(2) for s in range(2)]
-
-    args = []
-    for a in range(2):
-        args += [second[4 * a + 3], *second_got[2 * a : 2 * a + 2], *third_got[2 * a : 2 * a + 2]]
+        args += [summed[a * SIDE]]
+        args += [shift(summed[a * SIDE + away], 1 - a, away) for away in range(1, SIDE)]
     grad_up, grad_down = pl.pallas_call(
         last_kernel,
         out_shape=[

time: 154 us -> 137 us (0.89)
  the two profiles are of different devices: /device:TPU:6 before, /device:TPU:16 now
where the time goes in v5:
time: 137 us; the launch traced here: 136 us
  Pallas kernels  54.2 us (40%)
  starting transfers between devices  38.1 us (28%)
  waiting for transfers between devices  37.5 us (27%)
  local copies, waits for them, and re-layouts  3.91 us (3%)
  matrix products  1.68 us (1%)
    ppermute x18, waiting for transfers between devices, shift(): return lax.ppermute(value, 'dp', moves(axis, sign))  31.4 us
    ppermute x18, starting transfers between devices, shift(): return lax.ppermute(value, 'dp', moves(axis, sign))  23.3 us
    pallas_call x1, Pallas kernels, per_device(): pl.pallas_call(forward_kernel, grid_spec=pltpu.PrefetchScalarGridSpec(num...  17.9 us
    pallas_call x1, Pallas kernels, per_device(): pl.pallas_call(grad_up_kernel, grid_spec=pltpu.PrefetchScalarGridSpec(num...  11.6 us
    pallas_call x2, Pallas kernels, combine(): pl.pallas_call(kernel, grid=(BLOCK // ROWS,), in_specs=specs, out_specs=[...  10.4 us
    all_to_all x1, starting transfers between devices, per_device(): lax.all_to_all(grad_sum.reshape(pieces, width // pieces, rows), 'token',...  8.58 us
    pallas_call x1, Pallas kernels, per_device(): pl.pallas_call(grad_sum_kernel, grid=(SIDE,), in_specs=[tall, pl.BlockSpe...  7.6 us
    all_to_all x1, starting transfers between devices, per_device(): landed = lax.all_to_all(sent, 'dp', split_axis=0, concat_axis=0, tiled=True)  6.14 us
  transfers between devices with their start and end apart: 20, of which 10 were waited for; matrix products, arithmetic and copies ran while one was open for 0% of the time, Pallas kernels for 27%

profile of v5, /device:TPU:16, one launch (start us, length us, event | category | flops | bytes accessed | tf_op | source)
XLA Modules:
  0.0 136.2 jit_solution(5567947145741423965)
XLA Ops:
  0.7 0.5 concatenate.3.dest
  1.2 17.9 %forward_and_grad_down.1 = (bf16[384,768]{1,0:T(8,128)(2,1)}, f32[4,384,768]{2,1,0:T(8,128)}, f32[384,768]{1,0:T(8,128)}, bf16[384,768]{1,0:T(8,128)(2,1)}, bf16...) custom-call(s32[68]{0:T(128)} %concatenate.3.dest, ...), custom_call_target="tpu_custom_call" | custom-call | flops 5435817984 | bytes 25000000 | tf_op jit(solution)/shard_map/forward_and_grad_down/pallas_call | solution.py:305
  19.1 1.6 %collective-permute-start = (bf16[8,48,768]{2,1,0:T(8,128)(2,1)}, bf16[8,48,768]{2,1,0:T(8,128)(2,1)S(1)}, u32[]{:S(2)}, u32[]{:S(2)}) collective-permute-start(bf16[8,48,768]{2,1,0:T(8,128)(2,1)} %get-tuple-element.62), channel_id=1, source_target_pairs={{0,16},{16,32},{32,48},{48,0},{64,80},{80,96},{96,112},{112,64},{1... | collective-permute-start | bytes 1769480 | tf_op jit(solution)/shard_map/ppermute | solution.py:253
  20.6 1.7 %collective-permute-start.1 = (bf16[8,48,768]{2,1,0:T(8,128)(2,1)}, bf16[8,48,768]{2,1,0:T(8,128)(2,1)S(1)}, u32[]{:S(2)}, u32[]{:S(2)}) collective-permute-start(bf16[8,48,768]{2,1,0:T(8,128)(2,1)} %get-tuple-element.63), channel_id=1, source_target_pairs={{0,48},{16,0},{32,16},{48,32},{64,112},{80,64},{96,80},{112,96},{1... | collective-permute-start | bytes 1769480 | tf_op jit(solution)/shard_map/ppermute | solution.py:253
  22.4 1.3 collective-permute-start.2
  23.7 0.7 collective-permute-start.3
  24.4 11.6 %grad_pre_and_grad_up.1 = (bf16[4,384,768]{2,1,0:T(8,128)(2,1)}, bf16[8,48,768]{2,1,0:T(8,128)(2,1)}, bf16[8,48,768]{2,1,0:T(8,128)(2,1)}, bf16[8,48,768]{2,1,0:...) custom-call(s32[68]{0:T(128)} %concatenate.3.dest, ...), custom_call_target="tpu_custom_call" | custom-call | flops 3623878656 | bytes 20000000 | tf_op jit(solution)/shard_map/grad_pre_and_grad_up/pallas_call | solution.py:344
  36.0 0.0 collective-permute-done.refs_1_
  36.0 0.0 copy-start
  36.1 0.0 collective-permute-done.1.refs_2_
  36.1 0.0 copy-start.1
  36.1 1.0 collective-permute-done.2.refs_7_.refs_9_
  37.1 1.0 collective-permute-done.3.refs_8_.refs_10_
  38.1 0.3 collective-permute-start.4
  38.4 3.0 %collective-permute-start.5 = (bf16[8,48,768]{2,1,0:T(8,128)(2,1)}, bf16[8,48,768]{2,1,0:T(8,128)(2,1)S(1)}, u32[]{:S(2)}, u32[]{:S(2)}) collective-permute-start(bf16[8,48,768]{2,1,0:T(8,128)(2,1)} %get-tuple-element.70), channel_id=1, source_target_pairs={{0,48},{16,0},{32,16},{48,32},{64,112},{80,64},{96,80},{112,96},{1... | collective-permute-start | bytes 1769480 | tf_op jit(solution)/shard_map/ppermute | solution.py:253
  41.4 1.5 %collective-permute-start.6 = (bf16[8,48,768]{2,1,0:T(8,128)(2,1)}, bf16[8,48,768]{2,1,0:T(8,128)(2,1)}, u32[]{:S(2)}, u32[]{:S(2)}) collective-permute-start(bf16[8,48,768]{2,1,0:T(8,128)(2,1)} %get-tuple-element.79), channel_id=1, source_target_pairs={{0,64},{16,80},{32,96},{48,112},{64,128},{80,144},{96,160},{112,17... | collective-permute-start | bytes 1769480 | tf_op jit(solution)/shard_map/ppermute | solution.py:253
  42.8 0.5 collective-permute-start.7
  43.4 7.6 %grad_sum.1 = bf16[768,384]{1,0:T(8,128)(2,1)} custom-call(bf16[384,768]{1,0:T(8,128)(2,1)} %bitcast.19, bf16[4,384,768]{2,1,0:T(8,128)(2,1)} %get-tuple-element.71.grad_pre, f32[384,768]{1,0:T(8,128)} %get-tuple-element.72.grad_wide, bf16[768,3072]{1,0:T(8,128)(2,1)} %bitcast.16, f32[1,768]{1,0:T(1,128)} %gain_first.3), custom_call_target="tpu_custom_call" | custom-call | flops 1811939328 | bytes 10000000 | tf_op jit(solution)/shard_map/grad_sum/pallas_call | solution.py:369
  51.0 0.0 copy-done
  51.0 0.0 copy-done.1
  51.0 0.0 copy-done.2
  51.0 0.0 copy-done.3
  51.0 8.6 %all-to-all-start = ((bf16[16,48,384]{2,1,0:T(8,128)(2,1)}), bf16[16,48,384]{2,1,0:T(8,128)(2,1)S(1)}, u32[]{:S(2)}, u32[]{:S(2)}) async-start(bf16[16,48,384]{2,1,0:T(8,128)(2,1)} %bitcast.14), calls=%async_computation | async-start | bytes 1179648 | tf_op jit(solution)/shard_map/all_to_all | solution.py:387
  59.6 0.0 collective-permute-done.4.refs_4_
  59.6 0.0 copy-start.4
  59.6 0.0 collective-permute-done.5.refs_5_
  59.6 0.0 copy-start.5
  59.6 0.0 collective-permute-done.6.refs_10_.refs_12_
  59.6 0.0 collective-permute-done.7.refs_11_.refs_13_
  59.7 0.8 copy-done.4
  60.4 0.2 copy-done.5
  60.6 4.8 %first_sums.1 = (bf16[8,48,768]{2,1,0:T(8,128)(2,1)}, bf16[8,48,768]{2,1,0:T(8,128)(2,1)}, bf16[8,48,768]{2,1,0:T(8,128)(2,1)}, bf16[8,48,768]{2,1,0:T(8,128)(2,1)}) custom-call(bf16[8,48,768]{2,1,0:T(8,128)(2,1)} %get-tuple-element.73.refs_0_, bf16[8,48,768]{2,1,0:T(8,128)(2,1)} %copy-done, bf16[8,48,768]{2,1,0:T(8,128)(2,1)} %copy-done.1, ...), custom_call_target="tpu_custom_call" | custom-call | flops 1000000 | bytes 7000000 | tf_op jit(solution)/shard_map/first_sums/pallas_call | solution.py:401
  65.4 0.1 collective-permute-start.8
  65.5 3.2 %collective-permute-start.9 = (bf16[8,48,768]{2,1,0:T(8,128)(2,1)}, bf16[8,48,768]{2,1,0:T(8,128)(2,1)S(1)}, u32[]{:S(2)}, u32[]{:S(2)}) collective-permute-start(bf16[8,48,768]{2,1,0:T(8,128)(2,1)} %get-tuple-element.82), channel_id=1, source_target_pairs={{0,48},{16,0},{32,16},{48,32},{64,112},{80,64},{96,80},{112,96},{1... | collective-permute-start | bytes 1769480 | tf_op jit(solution)/shard_map/ppermute | solution.py:253
  68.7 1.5 %collective-permute-start.10 = (bf16[8,48,768]{2,1,0:T(8,128)(2,1)}, bf16[8,48,768]{2,1,0:T(8,128)(2,1)S(1)}, u32[]{:S(2)}, u32[]{:S(2)}) collective-permute-start(bf16[8,48,768]{2,1,0:T(8,128)(2,1)} %get-tuple-element.83), channel_id=1, source_target_pairs={{0,64},{16,80},{32,96},{48,112},{64,128},{80,144},{96,160},{112,17... | collective-permute-start | bytes 1769480 | tf_op jit(solution)/shard_map/ppermute | solution.py:253
  70.2 0.5 collective-permute-start.11
  70.7 6.1 %all-to-all-done = bf16[16,48,384]{2,1,0:T(8,128)(2,1)S(1)} async-done(((bf16[16,48,384]{2,1,0:T(8,128)(2,1)}), bf16[16,48,384]{2,1,0:T(8,128)(2,1)S(1)}, u32[]{:S(2)}, u32[]{:S(2)}) %all-to-all-start) | async-done | bytes 589856 | tf_op jit(solution)/shard_map/all_to_all | solution.py:387
  76.8 0.8 copy-done.6
  77.6 3.7 %shard_map.103 = bf16[16,64,768]{2,1,0:T(8,128)(2,1)} custom-call(bf16[768,384]{1,0:T(8,128)(2,1)} %grad_sum.1, bf16[768,384]{1,0:T(8,128)(2,1)} %bitcast.17, s32[1,384]{1,0:T(1,128)} %bitcast.21, s32[1,384]{1,0:T(1,128)} %slot.1), custom_call_target="tpu_custom_call" | custom-call | flops 603979776 | bytes 4000000 | tf_op jit(solution)/shard_map/pallas_call | solution.py:423
  81.4 1.2 collective-permute-done.8.refs_6_
  82.6 0.0 collective-permute-done.9.refs_7_
  82.6 1.5 %collective-permute-done.10.refs_14_ = bf16[8,48,768]{2,1,0:T(8,128)(2,1)S(1)} collective-permute-done((bf16[8,48,768]{2,1,0:T(8,128)(2,1)}, bf16[8,48,768]{2,1,0:T(8,128)(2,1)S(1)}, u32[]{:S(2)}, u32[]{:S(2)}) %collective-permute-start.10) | collective-permute-done | bytes 589856 | tf_op jit(solution)/shard_map/ppermute | solution.py:253
  84.0 1.2 collective-permute-done.11.refs_15_
  85.2 0.9 copy-done.10
  86.1 0.0 copy-done.7
  86.1 6.1 %all-to-all-start.1 = ((bf16[16,64,768]{2,1,0:T(8,128)(2,1)}), bf16[16,64,768]{2,1,0:T(8,128)(2,1)S(1)}, u32[]{:S(2)}, u32[]{:S(2)}) async-start(bf16[16,64,768]{2,1,0:T(8,128)(2,1)} %shard_map.103), calls=%async_computation.1 | async-start | bytes 3145728 | tf_op jit(solution)/shard_map/all_to_all | solution.py:430
  92.3 5.7 %second_sums.1 = (f32[4,48,768]{2,1,0:T(8,128)}, bf16[4,48,768]{2,1,0:T(8,128)(2,1)}, bf16[4,48,768]{2,1,0:T(8,128)(2,1)}, bf16[4,48,768]{2,1,0:T(8,128)(2,1)}, ...) custom-call(bf16[8,48,768]{2,1,0:T(8,128)(2,1)} %get-tuple-element.5, ...), custom_call_target="tpu_custom_call" | custom-call | flops 1000000 | bytes 7000000 | tf_op jit(solution)/shard_map/second_sums/pallas_call | solution.py:401
  97.9 1.2 collective-permute-start.12
  99.2 0.9 collective-permute-start.13
  100.0 0.7 collective-permute-start.14
  100.8 1.9 %collective-permute-start.15 = (bf16[4,48,768]{2,1,0:T(8,128)(2,1)}, bf16[4,48,768]{2,1,0:T(8,128)(2,1)S(1)}, u32[]{:S(2)}, u32[]{:S(2)}) collective-permute-start(bf16[4,48,768]{2,1,0:T(8,128)(2,1)} %get-tuple-element.97), channel_id=1, source_target_pairs={{0,16},{16,32},{32,48},{48,0},{64,80},{80,96},{96,112},{112,64},{1... | collective-permute-start | bytes 884744 | tf_op jit(solution)/shard_map/ppermute | solution.py:253
  102.7 2.7 %collective-permute-start.16 = (bf16[4,48,768]{2,1,0:T(8,128)(2,1)}, bf16[4,48,768]{2,1,0:T(8,128)(2,1)S(1)}, u32[]{:S(2)}, u32[]{:S(2)}) collective-permute-start(bf16[4,48,768]{2,1,0:T(8,128)(2,1)} %get-tuple-element.98), channel_id=1, source_target_pairs={{0,32},{16,48},{32,0},{48,16},{64,96},{80,112},{96,64},{112,80},{1... | collective-permute-start | bytes 884744 | tf_op jit(solution)/shard_map/ppermute | solution.py:253
  105.3 16.3 %collective-permute-done.12.refs_1_ = bf16[4,48,768]{2,1,0:T(8,128)(2,1)S(1)} collective-permute-done((bf16[4,48,768]{2,1,0:T(8,128)(2,1)}, bf16[4,48,768]{2,1,0:T(8,128)(2,1)S(1)}, u32[]{:S(2)}, u32[]{:S(2)}) %collective-permute-start.12) | collective-permute-done | bytes 294944 | tf_op jit(solution)/shard_map/ppermute | solution.py:253
  121.6 0.0 collective-permute-start.17
  121.6 0.0 collective-permute-done.13.refs_2_
  121.6 1.0 collective-permute-done.14.refs_3_
  122.6 0.0 collective-permute-done.15.refs_5_
  122.6 1.5 %collective-permute-done.16.refs_6_ = bf16[4,48,768]{2,1,0:T(8,128)(2,1)S(1)} collective-permute-done((bf16[4,48,768]{2,1,0:T(8,128)(2,1)}, bf16[4,48,768]{2,1,0:T(8,128)(2,1)S(1)}, u32[]{:S(2)}, u32[]{:S(2)}) %collective-permute-start.16) | collective-permute-done | bytes 294944 | tf_op jit(solution)/shard_map/ppermute | solution.py:253
  124.1 6.8 %collective-permute-done.17.refs_7_ = bf16[4,48,768]{2,1,0:T(8,128)(2,1)S(1)} collective-permute-done((bf16[4,48,768]{2,1,0:T(8,128)(2,1)}, bf16[4,48,768]{2,1,0:T(8,128)(2,1)S(1)}, u32[]{:S(2)}, u32[]{:S(2)}) %collective-permute-start.17) | collective-permute-done | bytes 294944 | tf_op jit(solution)/shard_map/ppermute | solution.py:253
  130.9 0.0 copy-done.13
  130.9 0.7 copy-done.16
  131.6 3.0 %last_sums.1 = (f32[48,3072]{1,0:T(8,128)}, f32[192,768]{1,0:T(8,128)}) custom-call(f32[4,48,768]{2,1,0:T(8,128)} %get-tuple-element.92.refs_0_, bf16[4,48,768]{2,1,0:T(8,128)(2,1)} %copy-done.11, bf16[4,48,768]{2,1,0:T(8,128)(2,1)} %copy-done.12, bf16[4,48,768]{2,1,0:T(8,128)(2,1)} %copy-done.13, f32[4,48,768]{2,1,0:T(8,128)} %get-tuple-element.96.refs_4_, ...), custom_call_target="tpu_custom_call" | custom-call | flops 1000000 | bytes 4000000 | tf_op jit(solution)/shard_map/last_sums/pallas_call | solution.py:446
  134.5 0.0 all-to-all-done.1
  134.6 1.7 %convolution_bitcast_fusion = f32[1,256,768]{2,1,0:T(8,128)} fusion(bf16[16,64,768]{2,1,0:T(8,128)(2,1)S(1)} %all-to-all-done.1, s32[16,64]{1,0:T(8,128)S(1)} %bitcast.20), kind=kOutput, calls=%fused_computation | convolution fusion | flops 402915328 | bytes 2363392 | tf_op jit(solution)/shard_map/dot_general | solution.py:461
  (21 shorter events, 0.1 us)
Async XLA Ops:
  19.1 17.0 %collective-permute-start = (bf16[8,48,768]{2,1,0:T(8,128)(2,1)}, bf16[8,48,768]{2,1,0:T(8,128)(2,1)S(1)}, u32[]{:S(2)}, u32[]{:S(2)}) collective-permute-start(bf16[8,48,768]{2,1,0:T(8,128)(2,1)} %get-tuple-element.62), channel_id=1, source_target_pairs={{0,16},{16,32},{32,48},{48,0},{64,80},{80,96},{96,112},{112,64},{1... | collective-permute-start | bytes 1769480 | tf_op jit(solution)/shard_map/ppermute | solution.py:253
  20.6 15.4 %collective-permute-start.1 = (bf16[8,48,768]{2,1,0:T(8,128)(2,1)}, bf16[8,48,768]{2,1,0:T(8,128)(2,1)S(1)}, u32[]{:S(2)}, u32[]{:S(2)}) collective-permute-start(bf16[8,48,768]{2,1,0:T(8,128)(2,1)} %get-tuple-element.63), channel_id=1, source_target_pairs={{0,48},{16,0},{32,16},{48,32},{64,112},{80,64},{96,80},{112,96},{1... | collective-permute-start | bytes 1769480 | tf_op jit(solution)/shard_map/ppermute | solution.py:253
  22.4 14.7 %collective-permute-start.2 = (bf16[8,48,768]{2,1,0:T(8,128)(2,1)}, bf16[8,48,768]{2,1,0:T(8,128)(2,1)S(1)}, u32[]{:S(2)}, u32[]{:S(2)}) collective-permute-start(bf16[8,48,768]{2,1,0:T(8,128)(2,1)} %get-tuple-element.64), channel_id=1, source_target_pairs={{0,64},{16,80},{32,96},{48,112},{64,128},{80,144},{96,160},{112,17... | collective-permute-start | bytes 1769480 | tf_op jit(solution)/shard_map/ppermute | solution.py:253
  23.7 14.4 %collective-permute-start.3 = (bf16[8,48,768]{2,1,0:T(8,128)(2,1)}, bf16[8,48,768]{2,1,0:T(8,128)(2,1)S(1)}, u32[]{:S(2)}, u32[]{:S(2)}) collective-permute-start(bf16[8,48,768]{2,1,0:T(8,128)(2,1)} %get-tuple-element.65), channel_id=1, source_target_pairs={{0,192},{16,208},{32,224},{48,240},{64,0},{80,16},{96,32},{112,48}... | collective-permute-start | bytes 1769480 | tf_op jit(solution)/shard_map/ppermute | solution.py:253
  36.0 14.9 %copy-start = (bf16[8,48,768]{2,1,0:T(8,128)(2,1)}, bf16[8,48,768]{2,1,0:T(8,128)(2,1)S(1)}, u32[]{:S(2)}) copy-start(bf16[8,48,768]{2,1,0:T(8,128)(2,1)S(1)} %collective-permute-done.refs_1_) | copy-start | bytes 1769476
  36.1 14.9 %copy-start.1 = (bf16[8,48,768]{2,1,0:T(8,128)(2,1)}, bf16[8,48,768]{2,1,0:T(8,128)(2,1)S(1)}, u32[]{:S(2)}) copy-start(bf16[8,48,768]{2,1,0:T(8,128)(2,1)S(1)} %collective-permute-done.1.refs_2_) | copy-start | bytes 1769476
  37.1 13.9 %copy-start.2 = (bf16[8,48,768]{2,1,0:T(8,128)(2,1)}, bf16[8,48,768]{2,1,0:T(8,128)(2,1)S(1)}, u32[]{:S(2)}) copy-start(bf16[8,48,768]{2,1,0:T(8,128)(2,1)S(1)} %collective-permute-done.2.refs_7_.refs_9_) | copy-start | bytes 1769476
  38.1 12.9 %copy-start.3 = (bf16[8,48,768]{2,1,0:T(8,128)(2,1)}, bf16[8,48,768]{2,1,0:T(8,128)(2,1)S(1)}, u32[]{:S(2)}) copy-start(bf16[8,48,768]{2,1,0:T(8,128)(2,1)S(1)} %collective-permute-done.3.refs_8_.refs_10_) | copy-start | bytes 1769476
  38.1 21.5 %collective-permute-start.4 = (bf16[8,48,768]{2,1,0:T(8,128)(2,1)}, bf16[8,48,768]{2,1,0:T(8,128)(2,1)S(1)}, u32[]{:S(2)}, u32[]{:S(2)}) collective-permute-start(bf16[8,48,768]{2,1,0:T(8,128)(2,1)} %get-tuple-element.69), channel_id=1, source_target_pairs={{0,16},{16,32},{32,48},{48,0},{64,80},{80,96},{96,112},{112,64},{1... | collective-permute-start | bytes 1769480 | tf_op jit(solution)/shard_map/ppermute | solution.py:253
  38.4 21.2 %collective-permute-start.5 = (bf16[8,48,768]{2,1,0:T(8,128)(2,1)}, bf16[8,48,768]{2,1,0:T(8,128)(2,1)S(1)}, u32[]{:S(2)}, u32[]{:S(2)}) collective-permute-start(bf16[8,48,768]{2,1,0:T(8,128)(2,1)} %get-tuple-element.70), channel_id=1, source_target_pairs={{0,48},{16,0},{32,16},{48,32},{64,112},{80,64},{96,80},{112,96},{1... | collective-permute-start | bytes 1769480 | tf_op jit(solution)/shard_map/ppermute | solution.py:253
  41.4 18.3 %collective-permute-start.6 = (bf16[8,48,768]{2,1,0:T(8,128)(2,1)}, bf16[8,48,768]{2,1,0:T(8,128)(2,1)}, u32[]{:S(2)}, u32[]{:S(2)}) collective-permute-start(bf16[8,48,768]{2,1,0:T(8,128)(2,1)} %get-tuple-element.79), channel_id=1, source_target_pairs={{0,64},{16,80},{32,96},{48,112},{64,128},{80,144},{96,160},{112,17... | collective-permute-start | bytes 1769480 | tf_op jit(solution)/shard_map/ppermute | solution.py:253
  42.8 16.8 %collective-permute-start.7 = (bf16[8,48,768]{2,1,0:T(8,128)(2,1)}, bf16[8,48,768]{2,1,0:T(8,128)(2,1)}, u32[]{:S(2)}, u32[]{:S(2)}) collective-permute-start(bf16[8,48,768]{2,1,0:T(8,128)(2,1)} %get-tuple-element.80), channel_id=1, source_target_pairs={{0,192},{16,208},{32,224},{48,240},{64,0},{80,16},{96,32},{112,48}... | collective-permute-start | bytes 1769480 | tf_op jit(solution)/shard_map/ppermute | solution.py:253
  51.0 25.8 %all-to-all-start = ((bf16[16,48,384]{2,1,0:T(8,128)(2,1)}), bf16[16,48,384]{2,1,0:T(8,128)(2,1)S(1)}, u32[]{:S(2)}, u32[]{:S(2)}) async-start(bf16[16,48,384]{2,1,0:T(8,128)(2,1)} %bitcast.14), calls=%async_computation | async-start | bytes 1179648 | tf_op jit(solution)/shard_map/all_to_all | solution.py:387
  59.6 0.8 copy-start.4
  59.6 1.0 copy-start.5
  65.4 17.2 %collective-permute-start.8 = (bf16[8,48,768]{2,1,0:T(8,128)(2,1)}, bf16[8,48,768]{2,1,0:T(8,128)(2,1)S(1)}, u32[]{:S(2)}, u32[]{:S(2)}) collective-permute-start(bf16[8,48,768]{2,1,0:T(8,128)(2,1)} %get-tuple-element.81), channel_id=1, source_target_pairs={{0,16},{16,32},{32,48},{48,0},{64,80},{80,96},{96,112},{112,64},{1... | collective-permute-start | bytes 1769480 | tf_op jit(solution)/shard_map/ppermute | solution.py:253
  65.5 17.1 %collective-permute-start.9 = (bf16[8,48,768]{2,1,0:T(8,128)(2,1)}, bf16[8,48,768]{2,1,0:T(8,128)(2,1)S(1)}, u32[]{:S(2)}, u32[]{:S(2)}) collective-permute-start(bf16[8,48,768]{2,1,0:T(8,128)(2,1)} %get-tuple-element.82), channel_id=1, source_target_pairs={{0,48},{16,0},{32,16},{48,32},{64,112},{80,64},{96,80},{112,96},{1... | collective-permute-start | bytes 1769480 | tf_op jit(solution)/shard_map/ppermute | solution.py:253
  68.7 15.3 %collective-permute-start.10 = (bf16[8,48,768]{2,1,0:T(8,128)(2,1)}, bf16[8,48,768]{2,1,0:T(8,128)(2,1)S(1)}, u32[]{:S(2)}, u32[]{:S(2)}) collective-permute-start(bf16[8,48,768]{2,1,0:T(8,128)(2,1)} %get-tuple-element.83), channel_id=1, source_target_pairs={{0,64},{16,80},{32,96},{48,112},{64,128},{80,144},{96,160},{112,17... | collective-permute-start | bytes 1769480 | tf_op jit(solution)/shard_map/ppermute | solution.py:253
  70.2 15.0 %collective-permute-start.11 = (bf16[8,48,768]{2,1,0:T(8,128)(2,1)}, bf16[8,48,768]{2,1,0:T(8,128)(2,1)S(1)}, u32[]{:S(2)}, u32[]{:S(2)}) collective-permute-start(bf16[8,48,768]{2,1,0:T(8,128)(2,1)} %get-tuple-element.84), channel_id=1, source_target_pairs={{0,192},{16,208},{32,224},{48,240},{64,0},{80,16},{96,32},{112,48}... | collective-permute-start | bytes 1769480 | tf_op jit(solution)/shard_map/ppermute | solution.py:253
  76.8 0.8 copy-start.6
  82.6 3.6 %copy-start.7 = (bf16[8,48,768]{2,1,0:T(8,128)(2,1)}, bf16[8,48,768]{2,1,0:T(8,128)(2,1)S(1)}, u32[]{:S(2)}) copy-start(bf16[8,48,768]{2,1,0:T(8,128)(2,1)S(1)} %collective-permute-done.8.refs_6_) | copy-start | bytes 1769476
  82.6 3.6 %copy-start.8 = (bf16[8,48,768]{2,1,0:T(8,128)(2,1)}, bf16[8,48,768]{2,1,0:T(8,128)(2,1)S(1)}, u32[]{:S(2)}) copy-start(bf16[8,48,768]{2,1,0:T(8,128)(2,1)S(1)} %collective-permute-done.9.refs_7_) | copy-start | bytes 1769476
  84.0 2.1 %copy-start.9 = (bf16[8,48,768]{2,1,0:T(8,128)(2,1)}, bf16[8,48,768]{2,1,0:T(8,128)(2,1)S(1)}, u32[]{:S(2)}) copy-start(bf16[8,48,768]{2,1,0:T(8,128)(2,1)S(1)} %collective-permute-done.10.refs_14_) | copy-start | bytes 1769476
  85.2 0.9 copy-start.10
  86.1 48.4 %all-to-all-start.1 = ((bf16[16,64,768]{2,1,0:T(8,128)(2,1)}), bf16[16,64,768]{2,1,0:T(8,128)(2,1)S(1)}, u32[]{:S(2)}, u32[]{:S(2)}) async-start(bf16[16,64,768]{2,1,0:T(8,128)(2,1)} %shard_map.103), calls=%async_computation.1 | async-start | bytes 3145728 | tf_op jit(solution)/shard_map/all_to_all | solution.py:430
  97.9 23.7 %collective-permute-start.12 = (bf16[4,48,768]{2,1,0:T(8,128)(2,1)}, bf16[4,48,768]{2,1,0:T(8,128)(2,1)S(1)}, u32[]{:S(2)}, u32[]{:S(2)}) collective-permute-start(bf16[4,48,768]{2,1,0:T(8,128)(2,1)} %get-tuple-element.93), channel_id=1, source_target_pairs={{0,64},{16,80},{32,96},{48,112},{64,128},{80,144},{96,160},{112,17... | collective-permute-start | bytes 884744 | tf_op jit(solution)/shard_map/ppermute | solution.py:253
  99.2 22.5 %collective-permute-start.13 = (bf16[4,48,768]{2,1,0:T(8,128)(2,1)}, bf16[4,48,768]{2,1,0:T(8,128)(2,1)S(1)}, u32[]{:S(2)}, u32[]{:S(2)}) collective-permute-start(bf16[4,48,768]{2,1,0:T(8,128)(2,1)} %get-tuple-element.94), channel_id=1, source_target_pairs={{0,128},{16,144},{32,160},{48,176},{64,192},{80,208},{96,224},{112... | collective-permute-start | bytes 884744 | tf_op jit(solution)/shard_map/ppermute | solution.py:253
  100.0 22.6 %collective-permute-start.14 = (bf16[4,48,768]{2,1,0:T(8,128)(2,1)}, bf16[4,48,768]{2,1,0:T(8,128)(2,1)S(1)}, u32[]{:S(2)}, u32[]{:S(2)}) collective-permute-start(bf16[4,48,768]{2,1,0:T(8,128)(2,1)} %get-tuple-element.95), channel_id=1, source_target_pairs={{0,192},{16,208},{32,224},{48,240},{64,0},{80,16},{96,32},{112,48}... | collective-permute-start | bytes 884744 | tf_op jit(solution)/shard_map/ppermute | solution.py:253
  100.8 21.8 %collective-permute-start.15 = (bf16[4,48,768]{2,1,0:T(8,128)(2,1)}, bf16[4,48,768]{2,1,0:T(8,128)(2,1)S(1)}, u32[]{:S(2)}, u32[]{:S(2)}) collective-permute-start(bf16[4,48,768]{2,1,0:T(8,128)(2,1)} %get-tuple-element.97), channel_id=1, source_target_pairs={{0,16},{16,32},{32,48},{48,0},{64,80},{80,96},{96,112},{112,64},{1... | collective-permute-start | bytes 884744 | tf_op jit(solution)/shard_map/ppermute | solution.py:253
  102.7 21.4 %collective-permute-start.16 = (bf16[4,48,768]{2,1,0:T(8,128)(2,1)}, bf16[4,48,768]{2,1,0:T(8,128)(2,1)S(1)}, u32[]{:S(2)}, u32[]{:S(2)}) collective-permute-start(bf16[4,48,768]{2,1,0:T(8,128)(2,1)} %get-tuple-element.98), channel_id=1, source_target_pairs={{0,32},{16,48},{32,0},{48,16},{64,96},{80,112},{96,64},{112,80},{1... | collective-permute-start | bytes 884744 | tf_op jit(solution)/shard_map/ppermute | solution.py:253
  121.6 9.2 %copy-start.11 = (bf16[4,48,768]{2,1,0:T(8,128)(2,1)}, bf16[4,48,768]{2,1,0:T(8,128)(2,1)S(1)}, u32[]{:S(2)}) copy-start(bf16[4,48,768]{2,1,0:T(8,128)(2,1)S(1)} %collective-permute-done.12.refs_1_) | copy-start | bytes 884740
  121.6 9.2 %collective-permute-start.17 = (bf16[4,48,768]{2,1,0:T(8,128)(2,1)}, bf16[4,48,768]{2,1,0:T(8,128)(2,1)S(1)}, u32[]{:S(2)}, u32[]{:S(2)}) collective-permute-start(bf16[4,48,768]{2,1,0:T(8,128)(2,1)} %get-tuple-element.99), channel_id=1, source_target_pairs={{0,48},{16,0},{32,16},{48,32},{64,112},{80,64},{96,80},{112,96},{1... | collective-permute-start | bytes 884744 | tf_op jit(solution)/shard_map/ppermute | solution.py:253
  121.6 9.2 %copy-start.12 = (bf16[4,48,768]{2,1,0:T(8,128)(2,1)}, bf16[4,48,768]{2,1,0:T(8,128)(2,1)S(1)}, u32[]{:S(2)}) copy-start(bf16[4,48,768]{2,1,0:T(8,128)(2,1)S(1)} %collective-permute-done.13.refs_2_) | copy-start | bytes 884740
  122.6 8.2 %copy-start.13 = (bf16[4,48,768]{2,1,0:T(8,128)(2,1)}, bf16[4,48,768]{2,1,0:T(8,128)(2,1)S(1)}, u32[]{:S(2)}) copy-start(bf16[4,48,768]{2,1,0:T(8,128)(2,1)S(1)} %collective-permute-done.14.refs_3_) | copy-start | bytes 884740
  122.6 8.3 %copy-start.14 = (bf16[4,48,768]{2,1,0:T(8,128)(2,1)}, bf16[4,48,768]{2,1,0:T(8,128)(2,1)S(1)}, u32[]{:S(2)}) copy-start(bf16[4,48,768]{2,1,0:T(8,128)(2,1)S(1)} %collective-permute-done.15.refs_5_) | copy-start | bytes 884740
  124.1 6.8 %copy-start.15 = (bf16[4,48,768]{2,1,0:T(8,128)(2,1)}, bf16[4,48,768]{2,1,0:T(8,128)(2,1)S(1)}, u32[]{:S(2)}) copy-start(bf16[4,48,768]{2,1,0:T(8,128)(2,1)S(1)} %collective-permute-done.16.refs_6_) | copy-start | bytes 884740
  130.8 0.7 copy-start.16

commit v6 on v5

--- a/solution.py
+++ b/solution.py
@@ -119,9 +119,11 @@
                 copy.wait()
 
 
-def grad_up_kernel(dest, hidden, slope, grad_mid, w_down, *refs):
-    grad_pre, outs = refs[0], refs[1:9]
-    turned, stage, sems = refs[9:]
+def backward_kernel(
+    dest, mix, hidden, slope, grad_wide, grad_mid, w_up, w_down, gain_first, *refs
+):
+    grad_sum, outs = refs[0], refs[1:9]
+    turned, grad_hidden, stage, sems = refs[9:]
     step = pl.program_id(0)
 
     def copies(part):
@@ -135,9 +137,9 @@
     def _():
         turned[...] = hidden[...].T
 
-    value = (contract_cols(grad_mid[...], w_down[...]) * slope[0]).astype(BF16)
-    grad_pre[0] = value
-    part = jnp.dot(turned[...], value, preferred_element_type=F32).astype(BF16)
+    grad_act = contract_cols(grad_mid[...], w_down[...])
+    grad_pre = (grad_act * slope[0]).astype(BF16)
+    part = jnp.dot(turned[...], grad_pre, preferred_element_type=F32).astype(BF16)
     for k in range(16):
         stage[dest[k * 4 + step]] = part[k * BLOCK : (k + 1) * BLOCK]
     for q in range(SIDE):
@@ -147,30 +149,24 @@
             for copy in copies(q):
                 copy.start()
 
+    part = contract_cols(grad_pre, w_up[...])
+
+    @pl.when(step == 0)
+    def _():
+        grad_hidden[...] = part + grad_wide[...]
+
+    @pl.when(step > 0)
+    def _():
+        grad_hidden[...] += part
+
     @pl.when(step == SIDE - 1)
     def _():
+        normed, inv_scale = normalize(mix[...].astype(F32))
+        total = norm_back(grad_hidden[...] * gain_first[...], normed, inv_scale)
+        grad_sum[...] = total.T.astype(BF16)
         for q in range(SIDE):
             for copy in copies(q):
                 copy.wait()
-
-
-def grad_sum_kernel(mix, grad_pre, grad_wide, w_up, gain_first, grad_sum, grad_hidden):
-    step = pl.program_id(0)
-    part = contract_cols(grad_pre[0], w_up[...])
-
-    @pl.when(step == 0)
-    def _():
-        grad_hidden[...] = part + grad_wide[...]
-
-    @pl.when(step > 0)
-    def _():
-        grad_hidden[...] += part
-
-    @pl.when(step == SIDE - 1)
-    def _():
-        normed, inv_scale = normalize(mix[...].astype(F32))
-        total = norm_back(grad_hidden[...] * gain_first[...], normed, inv_scale)
-        grad_sum[...] = total.T.astype(BF16)
 
 
 def seat_kernel(grad_sum, swapped, owner, slot, sent):
@@ -341,48 +337,35 @@
 
     down_got = send(down_parts)
 
-    grad_pre, *up_parts = pl.pallas_call(
-        grad_up_kernel,
+    grad_sum, *up_parts = pl.pallas_call(
+        backward_kernel,
         grid_spec=pltpu.PrefetchScalarGridSpec(
             num_scalar_prefetch=1,
             grid=(SIDE,),
             in_specs=[
                 tall,
+                tall,
                 pl.BlockSpec((1, rows, chunk), lambda i, _: (i, 0, 0)),
                 tall,
+                tall,
+                pl.BlockSpec((width, chunk), lambda i, _: (0, i)),
                 pl.BlockSpec((chunk, width), lambda i, _: (i, 0)),
+                gain,
             ],
-            out_specs=[pl.BlockSpec((1, rows, chunk), lambda i, _: (i, 0, 0))] + [ANY] * 8,
-            scratch_shapes=[pltpu.VMEM((width, rows), BF16)] + stage,
+            out_specs=[whole((width, rows))] + [ANY] * 8,
+            scratch_shapes=[pltpu.VMEM((width, rows), BF16), pltpu.VMEM((rows, width), F32)]
+            + stage,
         ),
-        out_shape=[jax.ShapeDtypeStruct((SIDE, rows, chunk), BF16)] + [group] * 8,
+        out_shape=[jax.ShapeDtypeStruct((width, rows), BF16)] + [group] * 8,
         compiler_params=params("arbitrary"),
-        cost_estimate=cost(2 * matmul, 20_000_000),
-        name="grad_pre_and_grad_up",
-    )(dest, hidden, slope, grad_mid, down_mat)
+        cost_estimate=cost(3 * matmul, 25_000_000),
+        name="backward_and_grad_up",
+    )(dest, mix, hidden, slope, grad_wide, grad_mid, up_mat, down_mat, gain_first)
 
     leaving = [up_parts[k] for k in (0, 1, 4, 5)]
-    leaving, grad_pre, down_got = lax.optimization_barrier((leaving, grad_pre, down_got))
+    leaving, grad_sum, down_got = lax.optimization_barrier((leaving, grad_sum, down_got))
     up_parts = [*leaving[:2], *up_parts[2:4], *leaving[2:], *up_parts[6:]]
     up_got = send(up_parts)
-
-    grad_sum = pl.pallas_call(
-        grad_sum_kernel,
-        grid=(SIDE,),
-        in_specs=[
-            tall,
-            pl.BlockSpec((1, rows, chunk), lambda i: (i, 0, 0)),
-            tall,
-            pl.BlockSpec((width, chunk), lambda i: (0, i)),
-            gain,
-        ],
-        out_specs=whole((width, rows)),
-        out_shape=jax.ShapeDtypeStruct((width, rows), BF16),
-        scratch_shapes=[pltpu.VMEM((rows, width), F32)],
-        compiler_params=params("arbitrary"),
-        cost_estimate=cost(matmul, 10_000_000),
-        name="grad_sum",
-    )(mix, grad_pre, grad_wide, up_mat, gain_first)
 
     swapped = lax.all_to_all(
         grad_sum.reshape(pieces, width // pieces, rows),

time: 137 us -> 127 us (0.927)
  the two profiles are of different devices: /device:TPU:16 before, /device:TPU:6 now
where the time goes in v6:
time: 127 us; the launch traced here: 126 us
  Pallas kernels  48.8 us (38%)
  starting transfers between devices  41.2 us (32%)
  waiting for transfers between devices  30 us (24%)
  local copies, waits for them, and re-layouts  3.14 us (2%)
  matrix products  1.68 us (1%)
    ppermute x18, starting transfers between devices, shift(): return lax.ppermute(value, 'dp', moves(axis, sign))  27.1 us
    ppermute x18, waiting for transfers between devices, shift(): return lax.ppermute(value, 'dp', moves(axis, sign))  26.9 us
    pallas_call x1, Pallas kernels, per_device(): pl.pallas_call(forward_kernel, grid_spec=pltpu.PrefetchScalarGridSpec(num...  17.9 us
    pallas_call x1, Pallas kernels, per_device(): pl.pallas_call(backward_kernel, grid_spec=pltpu.PrefetchScalarGridSpec(nu...  13.8 us
    pallas_call x2, Pallas kernels, combine(): pl.pallas_call(kernel, grid=(BLOCK // ROWS,), in_specs=specs, out_specs=[...  10.4 us
    all_to_all x1, starting transfers between devices, per_device(): lax.all_to_all(grad_sum.reshape(pieces, width // pieces, rows), 'token',...  7.22 us
    all_to_all x1, starting transfers between devices, per_device(): landed = lax.all_to_all(sent, 'dp', split_axis=0, concat_axis=0, tiled=True)  6.84 us
    pallas_call x1, Pallas kernels, per_device(): pl.pallas_call(seat_kernel, out_shape=jax.ShapeDtypeStruct((owners, SEAT,...  3.75 us
  transfers between devices with their start and end apart: 20, of which 9 were waited for; matrix products, arithmetic and copies ran while one was open for 0% of the time, Pallas kernels for 25%

profile of v6, /device:TPU:6, one launch (start us, length us, event | category | flops | bytes accessed | tf_op | source)
XLA Modules:
  0.0 125.8 jit_solution(6244471658177828064)
XLA Ops:
  0.7 0.6 concatenate.3.dest
  1.3 17.9 %forward_and_grad_down.1 = (bf16[384,768]{1,0:T(8,128)(2,1)}, f32[4,384,768]{2,1,0:T(8,128)}, f32[384,768]{1,0:T(8,128)}, bf16[384,768]{1,0:T(8,128)(2,1)}, bf16...) custom-call(s32[68]{0:T(128)} %concatenate.3.dest, ...), custom_call_target="tpu_custom_call" | custom-call | flops 5435817984 | bytes 25000000 | tf_op jit(solution)/shard_map/forward_and_grad_down/pallas_call | solution.py:301
  19.1 2.3 %collective-permute-start = (bf16[8,48,768]{2,1,0:T(8,128)(2,1)}, bf16[8,48,768]{2,1,0:T(8,128)(2,1)S(1)}, u32[]{:S(2)}, u32[]{:S(2)}) collective-permute-start(bf16[8,48,768]{2,1,0:T(8,128)(2,1)} %get-tuple-element.63), channel_id=1, source_target_pairs={{0,16},{16,32},{32,48},{48,0},{64,80},{80,96},{96,112},{112,64},{1... | collective-permute-start | bytes 1769480 | tf_op jit(solution)/shard_map/ppermute | solution.py:249
  21.4 0.0 collective-permute-start.1
  21.4 1.4 %collective-permute-start.2 = (bf16[8,48,768]{2,1,0:T(8,128)(2,1)}, bf16[8,48,768]{2,1,0:T(8,128)(2,1)S(1)}, u32[]{:S(2)}, u32[]{:S(2)}) collective-permute-start(bf16[8,48,768]{2,1,0:T(8,128)(2,1)} %get-tuple-element.65), channel_id=1, source_target_pairs={{0,64},{16,80},{32,96},{48,112},{64,128},{80,144},{96,160},{112,17... | collective-permute-start | bytes 1769480 | tf_op jit(solution)/shard_map/ppermute | solution.py:249
  22.8 1.9 %collective-permute-start.3 = (bf16[8,48,768]{2,1,0:T(8,128)(2,1)}, bf16[8,48,768]{2,1,0:T(8,128)(2,1)S(1)}, u32[]{:S(2)}, u32[]{:S(2)}) collective-permute-start(bf16[8,48,768]{2,1,0:T(8,128)(2,1)} %get-tuple-element.66), channel_id=1, source_target_pairs={{0,192},{16,208},{32,224},{48,240},{64,0},{80,16},{96,32},{112,48}... | collective-permute-start | bytes 1769480 | tf_op jit(solution)/shard_map/ppermute | solution.py:249
  24.7 13.8 %backward_and_grad_up.1 = (bf16[768,384]{1,0:T(8,128)(2,1)}, bf16[8,48,768]{2,1,0:T(8,128)(2,1)}, bf16[8,48,768]{2,1,0:T(8,128)(2,1)}, bf16[8,48,768]{2,1,0:T(8,...) custom-call(s32[68]{0:T(128)} %concatenate.3.dest, ...), custom_call_target="tpu_custom_call" | custom-call | flops 5435817984 | bytes 25000000 | tf_op jit(solution)/shard_map/backward_and_grad_up/pallas_call | solution.py:340
  38.5 0.0 collective-permute-done.refs_1_
  38.5 0.0 copy-start
  38.5 0.0 collective-permute-done.1.refs_2_
  38.5 0.0 copy-start.1
  38.5 0.0 collective-permute-done.2.refs_7_.refs_9_
  38.6 0.0 copy-start.2
  38.6 0.0 collective-permute-done.3.refs_8_.refs_10_
  38.6 0.0 copy-start.3
  38.6 3.3 %collective-permute-start.4 = (bf16[8,48,768]{2,1,0:T(8,128)(2,1)}, bf16[8,48,768]{2,1,0:T(8,128)(2,1)S(1)}, u32[]{:S(2)}, u32[]{:S(2)}) collective-permute-start(bf16[8,48,768]{2,1,0:T(8,128)(2,1)} %get-tuple-element.70), channel_id=1, source_target_pairs={{0,16},{16,32},{32,48},{48,0},{64,80},{80,96},{96,112},{112,64},{1... | collective-permute-start | bytes 1769480 | tf_op jit(solution)/shard_map/ppermute | solution.py:249
  41.9 0.0 collective-permute-start.5
  41.9 0.0 collective-permute-start.6
  41.9 3.2 %collective-permute-start.7 = (bf16[8,48,768]{2,1,0:T(8,128)(2,1)}, bf16[8,48,768]{2,1,0:T(8,128)(2,1)}, u32[]{:S(2)}, u32[]{:S(2)}) collective-permute-start(bf16[8,48,768]{2,1,0:T(8,128)(2,1)} %get-tuple-element.80), channel_id=1, source_target_pairs={{0,192},{16,208},{32,224},{48,240},{64,0},{80,16},{96,32},{112,48}... | collective-permute-start | bytes 1769480 | tf_op jit(solution)/shard_map/ppermute | solution.py:249
  45.1 7.2 %all-to-all-start = ((bf16[16,48,384]{2,1,0:T(8,128)(2,1)}), bf16[16,48,384]{2,1,0:T(8,128)(2,1)}, u32[]{:S(2)}, u32[]{:S(2)}) async-start(bf16[16,48,384]{2,1,0:T(8,128)(2,1)} %bitcast.14), calls=%async_computation | async-start | bytes 1179648 | tf_op jit(solution)/shard_map/all_to_all | solution.py:370
  52.4 0.3 collective-permute-done.4.refs_4_
  52.7 2.6 %collective-permute-done.5.refs_5_ = bf16[8,48,768]{2,1,0:T(8,128)(2,1)S(1)} collective-permute-done((bf16[8,48,768]{2,1,0:T(8,128)(2,1)}, bf16[8,48,768]{2,1,0:T(8,128)(2,1)S(1)}, u32[]{:S(2)}, u32[]{:S(2)}) %collective-permute-start.5) | collective-permute-done | bytes 589856 | tf_op jit(solution)/shard_map/ppermute | solution.py:249
  55.3 0.2 collective-permute-done.6.refs_10_.refs_12_
  55.5 0.0 collective-permute-done.7.refs_11_.refs_13_
  55.5 0.0 copy-done
  55.5 0.0 copy-done.1
  55.5 0.0 copy-done.2
  55.5 0.0 copy-done.3
  55.5 0.0 copy-done.4
  55.5 0.6 copy-done.5
  56.1 4.7 %first_sums.1 = (bf16[8,48,768]{2,1,0:T(8,128)(2,1)}, bf16[8,48,768]{2,1,0:T(8,128)(2,1)}, bf16[8,48,768]{2,1,0:T(8,128)(2,1)}, bf16[8,48,768]{2,1,0:T(8,128)(2,1)}) custom-call(bf16[8,48,768]{2,1,0:T(8,128)(2,1)} %get-tuple-element.73.refs_0_, bf16[8,48,768]{2,1,0:T(8,128)(2,1)} %copy-done, bf16[8,48,768]{2,1,0:T(8,128)(2,1)} %copy-done.1, ...), custom_call_target="tpu_custom_call" | custom-call | flops 1000000 | bytes 7000000 | tf_op jit(solution)/shard_map/first_sums/pallas_call | solution.py:384
  60.9 2.4 %collective-permute-start.8 = (bf16[8,48,768]{2,1,0:T(8,128)(2,1)}, bf16[8,48,768]{2,1,0:T(8,128)(2,1)S(1)}, u32[]{:S(2)}, u32[]{:S(2)}) collective-permute-start(bf16[8,48,768]{2,1,0:T(8,128)(2,1)} %get-tuple-element.81), channel_id=1, source_target_pairs={{0,16},{16,32},{32,48},{48,0},{64,80},{80,96},{96,112},{112,64},{1... | collective-permute-start | bytes 1769480 | tf_op jit(solution)/shard_map/ppermute | solution.py:249
  63.3 0.0 collective-permute-start.9
  63.3 0.4 collective-permute-start.10
  63.6 2.9 %collective-permute-start.11 = (bf16[8,48,768]{2,1,0:T(8,128)(2,1)}, bf16[8,48,768]{2,1,0:T(8,128)(2,1)S(1)}, u32[]{:S(2)}, u32[]{:S(2)}) collective-permute-start(bf16[8,48,768]{2,1,0:T(8,128)(2,1)} %get-tuple-element.84), channel_id=1, source_target_pairs={{0,192},{16,208},{32,224},{48,240},{64,0},{80,16},{96,32},{112,48}... | collective-permute-start | bytes 1769480 | tf_op jit(solution)/shard_map/ppermute | solution.py:249
  66.5 3.1 %all-to-all-done = bf16[16,48,384]{2,1,0:T(8,128)(2,1)} async-done(((bf16[16,48,384]{2,1,0:T(8,128)(2,1)}), bf16[16,48,384]{2,1,0:T(8,128)(2,1)}, u32[]{:S(2)}, u32[]{:S(2)}) %all-to-all-start) | async-done | bytes 589856 | tf_op jit(solution)/shard_map/all_to_all | solution.py:370
  69.6 3.7 %shard_map.103 = bf16[16,64,768]{2,1,0:T(8,128)(2,1)} custom-call(bf16[768,384]{1,0:T(8,128)(2,1)} %get-tuple-element.72.grad_sum, bf16[768,384]{1,0:T(8,128)(2,1)} %bitcast.5.swapped, s32[1,384]{1,0:T(1,128)} %bitcast.16, s32[1,384]{1,0:T(1,128)} %slot.1), custom_call_target="tpu_custom_call" | custom-call | flops 603979776 | bytes 4000000 | tf_op jit(solution)/shard_map/pallas_call | solution.py:406
  73.4 1.2 collective-permute-done.8.refs_6_
  74.5 3.3 %collective-permute-done.9.refs_7_ = bf16[8,48,768]{2,1,0:T(8,128)(2,1)S(1)} collective-permute-done((bf16[8,48,768]{2,1,0:T(8,128)(2,1)}, bf16[8,48,768]{2,1,0:T(8,128)(2,1)S(1)}, u32[]{:S(2)}, u32[]{:S(2)}) %collective-permute-start.9) | collective-permute-done | bytes 589856 | tf_op jit(solution)/shard_map/ppermute | solution.py:249
  77.9 0.0 collective-permute-done.10.refs_14_
  77.9 0.0 collective-permute-done.11.refs_15_
  77.9 0.9 copy-done.9
  78.7 0.1 copy-done.7
  78.9 0.2 copy-done.8
  79.1 6.8 %all-to-all-start.1 = ((bf16[16,64,768]{2,1,0:T(8,128)(2,1)}), bf16[16,64,768]{2,1,0:T(8,128)(2,1)S(1)}, u32[]{:S(2)}, u32[]{:S(2)}) async-start(bf16[16,64,768]{2,1,0:T(8,128)(2,1)} %shard_map.103), calls=%async_computation.1 | async-start | bytes 3145728 | tf_op jit(solution)/shard_map/all_to_all | solution.py:413
  85.9 5.7 %second_sums.1 = (f32[4,48,768]{2,1,0:T(8,128)}, bf16[4,48,768]{2,1,0:T(8,128)(2,1)}, bf16[4,48,768]{2,1,0:T(8,128)(2,1)}, bf16[4,48,768]{2,1,0:T(8,128)(2,1)}, ...) custom-call(bf16[8,48,768]{2,1,0:T(8,128)(2,1)} %get-tuple-element.5, ...), custom_call_target="tpu_custom_call" | custom-call | flops 1000000 | bytes 7000000 | tf_op jit(solution)/shard_map/second_sums/pallas_call | solution.py:384
  91.6 1.5 %collective-permute-start.12 = (bf16[4,48,768]{2,1,0:T(8,128)(2,1)}, bf16[4,48,768]{2,1,0:T(8,128)(2,1)S(1)}, u32[]{:S(2)}, u32[]{:S(2)}) collective-permute-start(bf16[4,48,768]{2,1,0:T(8,128)(2,1)} %get-tuple-element.93), channel_id=1, source_target_pairs={{0,64},{16,80},{32,96},{48,112},{64,128},{80,144},{96,160},{112,17... | collective-permute-start | bytes 884744 | tf_op jit(solution)/shard_map/ppermute | solution.py:249
  93.1 2.7 %collective-permute-start.13 = (bf16[4,48,768]{2,1,0:T(8,128)(2,1)}, bf16[4,48,768]{2,1,0:T(8,128)(2,1)S(1)}, u32[]{:S(2)}, u32[]{:S(2)}) collective-permute-start(bf16[4,48,768]{2,1,0:T(8,128)(2,1)} %get-tuple-element.94), channel_id=1, source_target_pairs={{0,128},{16,144},{32,160},{48,176},{64,192},{80,208},{96,224},{112... | collective-permute-start | bytes 884744 | tf_op jit(solution)/shard_map/ppermute | solution.py:249
  95.8 1.5 %collective-permute-start.14 = (bf16[4,48,768]{2,1,0:T(8,128)(2,1)}, bf16[4,48,768]{2,1,0:T(8,128)(2,1)S(1)}, u32[]{:S(2)}, u32[]{:S(2)}) collective-permute-start(bf16[4,48,768]{2,1,0:T(8,128)(2,1)} %get-tuple-element.95), channel_id=1, source_target_pairs={{0,192},{16,208},{32,224},{48,240},{64,0},{80,16},{96,32},{112,48}... | collective-permute-start | bytes 884744 | tf_op jit(solution)/shard_map/ppermute | solution.py:249
  97.3 0.6 collective-permute-start.15
  97.8 2.4 %collective-permute-start.16 = (bf16[4,48,768]{2,1,0:T(8,128)(2,1)}, bf16[4,48,768]{2,1,0:T(8,128)(2,1)S(1)}, u32[]{:S(2)}, u32[]{:S(2)}) collective-permute-start(bf16[4,48,768]{2,1,0:T(8,128)(2,1)} %get-tuple-element.98), channel_id=1, source_target_pairs={{0,32},{16,48},{32,0},{48,16},{64,96},{80,112},{96,64},{112,80},{1... | collective-permute-start | bytes 884744 | tf_op jit(solution)/shard_map/ppermute | solution.py:249
  100.2 11.5 %collective-permute-done.12.refs_1_ = bf16[4,48,768]{2,1,0:T(8,128)(2,1)S(1)} collective-permute-done((bf16[4,48,768]{2,1,0:T(8,128)(2,1)}, bf16[4,48,768]{2,1,0:T(8,128)(2,1)S(1)}, u32[]{:S(2)}, u32[]{:S(2)}) %collective-permute-start.12) | collective-permute-done | bytes 294944 | tf_op jit(solution)/shard_map/ppermute | solution.py:249
  111.7 0.9 collective-permute-start.17
  112.6 3.8 %collective-permute-done.13.refs_2_ = bf16[4,48,768]{2,1,0:T(8,128)(2,1)S(1)} collective-permute-done((bf16[4,48,768]{2,1,0:T(8,128)(2,1)}, bf16[4,48,768]{2,1,0:T(8,128)(2,1)S(1)}, u32[]{:S(2)}, u32[]{:S(2)}) %collective-permute-start.13) | collective-permute-done | bytes 294944 | tf_op jit(solution)/shard_map/ppermute | solution.py:249
  116.4 0.0 collective-permute-done.14.refs_3_
  116.4 0.0 collective-permute-done.15.refs_5_
  116.4 0.0 collective-permute-done.16.refs_6_
  116.4 0.0 copy-start.14
  116.4 4.0 %collective-permute-done.17.refs_7_ = bf16[4,48,768]{2,1,0:T(8,128)(2,1)S(1)} collective-permute-done((bf16[4,48,768]{2,1,0:T(8,128)(2,1)}, bf16[4,48,768]{2,1,0:T(8,128)(2,1)S(1)}, u32[]{:S(2)}, u32[]{:S(2)}) %collective-permute-start.17) | collective-permute-done | bytes 294944 | tf_op jit(solution)/shard_map/ppermute | solution.py:249
  120.4 0.0 copy-done.12
  120.4 0.7 copy-done.15
  121.1 3.0 %last_sums.1 = (f32[48,3072]{1,0:T(8,128)}, f32[192,768]{1,0:T(8,128)}) custom-call(f32[4,48,768]{2,1,0:T(8,128)} %get-tuple-element.92.refs_0_, bf16[4,48,768]{2,1,0:T(8,128)(2,1)} %copy-done.10, bf16[4,48,768]{2,1,0:T(8,128)(2,1)} %copy-done.11, bf16[4,48,768]{2,1,0:T(8,128)(2,1)} %copy-done.12, f32[4,48,768]{2,1,0:T(8,128)} %get-tuple-element.96.refs_4_, ...), custom_call_target="tpu_custom_call" | custom-call | flops 1000000 | bytes 4000000 | tf_op jit(solution)/shard_map/last_sums/pallas_call | solution.py:429
  124.1 0.0 all-to-all-done.1
  124.1 1.7 %convolution_bitcast_fusion = f32[1,256,768]{2,1,0:T(8,128)} fusion(bf16[16,64,768]{2,1,0:T(8,128)(2,1)S(1)} %all-to-all-done.1, s32[16,64]{1,0:T(8,128)S(1)} %bitcast.15), kind=kOutput, calls=%fused_computation | convolution fusion | flops 402915328 | bytes 2363392 | tf_op jit(solution)/shard_map/dot_general | solution.py:444
  (18 shorter events, 0.1 us)
Async XLA Ops:
  19.1 19.4 %collective-permute-start = (bf16[8,48,768]{2,1,0:T(8,128)(2,1)}, bf16[8,48,768]{2,1,0:T(8,128)(2,1)S(1)}, u32[]{:S(2)}, u32[]{:S(2)}) collective-permute-start(bf16[8,48,768]{2,1,0:T(8,128)(2,1)} %get-tuple-element.63), channel_id=1, source_target_pairs={{0,16},{16,32},{32,48},{48,0},{64,80},{80,96},{96,112},{112,64},{1... | collective-permute-start | bytes 1769480 | tf_op jit(solution)/shard_map/ppermute | solution.py:249
  21.4 17.1 %collective-permute-start.1 = (bf16[8,48,768]{2,1,0:T(8,128)(2,1)}, bf16[8,48,768]{2,1,0:T(8,128)(2,1)S(1)}, u32[]{:S(2)}, u32[]{:S(2)}) collective-permute-start(bf16[8,48,768]{2,1,0:T(8,128)(2,1)} %get-tuple-element.64), channel_id=1, source_target_pairs={{0,48},{16,0},{32,16},{48,32},{64,112},{80,64},{96,80},{112,96},{1... | collective-permute-start | bytes 1769480 | tf_op jit(solution)/shard_map/ppermute | solution.py:249
  21.4 17.1 %collective-permute-start.2 = (bf16[8,48,768]{2,1,0:T(8,128)(2,1)}, bf16[8,48,768]{2,1,0:T(8,128)(2,1)S(1)}, u32[]{:S(2)}, u32[]{:S(2)}) collective-permute-start(bf16[8,48,768]{2,1,0:T(8,128)(2,1)} %get-tuple-element.65), channel_id=1, source_target_pairs={{0,64},{16,80},{32,96},{48,112},{64,128},{80,144},{96,160},{112,17... | collective-permute-start | bytes 1769480 | tf_op jit(solution)/shard_map/ppermute | solution.py:249
  22.8 15.8 %collective-permute-start.3 = (bf16[8,48,768]{2,1,0:T(8,128)(2,1)}, bf16[8,48,768]{2,1,0:T(8,128)(2,1)S(1)}, u32[]{:S(2)}, u32[]{:S(2)}) collective-permute-start(bf16[8,48,768]{2,1,0:T(8,128)(2,1)} %get-tuple-element.66), channel_id=1, source_target_pairs={{0,192},{16,208},{32,224},{48,240},{64,0},{80,16},{96,32},{112,48}... | collective-permute-start | bytes 1769480 | tf_op jit(solution)/shard_map/ppermute | solution.py:249
  38.5 17.0 %copy-start = (bf16[8,48,768]{2,1,0:T(8,128)(2,1)}, bf16[8,48,768]{2,1,0:T(8,128)(2,1)S(1)}, u32[]{:S(2)}) copy-start(bf16[8,48,768]{2,1,0:T(8,128)(2,1)S(1)} %collective-permute-done.refs_1_) | copy-start | bytes 1769476
  38.5 16.9 %copy-start.1 = (bf16[8,48,768]{2,1,0:T(8,128)(2,1)}, bf16[8,48,768]{2,1,0:T(8,128)(2,1)S(1)}, u32[]{:S(2)}) copy-start(bf16[8,48,768]{2,1,0:T(8,128)(2,1)S(1)} %collective-permute-done.1.refs_2_) | copy-start | bytes 1769476
  38.6 16.9 %copy-start.2 = (bf16[8,48,768]{2,1,0:T(8,128)(2,1)}, bf16[8,48,768]{2,1,0:T(8,128)(2,1)S(1)}, u32[]{:S(2)}) copy-start(bf16[8,48,768]{2,1,0:T(8,128)(2,1)S(1)} %collective-permute-done.2.refs_7_.refs_9_) | copy-start | bytes 1769476
  38.6 16.9 %copy-start.3 = (bf16[8,48,768]{2,1,0:T(8,128)(2,1)}, bf16[8,48,768]{2,1,0:T(8,128)(2,1)S(1)}, u32[]{:S(2)}) copy-start(bf16[8,48,768]{2,1,0:T(8,128)(2,1)S(1)} %collective-permute-done.3.refs_8_.refs_10_) | copy-start | bytes 1769476
  38.6 14.1 %collective-permute-start.4 = (bf16[8,48,768]{2,1,0:T(8,128)(2,1)}, bf16[8,48,768]{2,1,0:T(8,128)(2,1)S(1)}, u32[]{:S(2)}, u32[]{:S(2)}) collective-permute-start(bf16[8,48,768]{2,1,0:T(8,128)(2,1)} %get-tuple-element.70), channel_id=1, source_target_pairs={{0,16},{16,32},{32,48},{48,0},{64,80},{80,96},{96,112},{112,64},{1... | collective-permute-start | bytes 1769480 | tf_op jit(solution)/shard_map/ppermute | solution.py:249
  41.9 13.4 %collective-permute-start.5 = (bf16[8,48,768]{2,1,0:T(8,128)(2,1)}, bf16[8,48,768]{2,1,0:T(8,128)(2,1)S(1)}, u32[]{:S(2)}, u32[]{:S(2)}) collective-permute-start(bf16[8,48,768]{2,1,0:T(8,128)(2,1)} %get-tuple-element.71), channel_id=1, source_target_pairs={{0,48},{16,0},{32,16},{48,32},{64,112},{80,64},{96,80},{112,96},{1... | collective-permute-start | bytes 1769480 | tf_op jit(solution)/shard_map/ppermute | solution.py:249
  41.9 13.6 %collective-permute-start.6 = (bf16[8,48,768]{2,1,0:T(8,128)(2,1)}, bf16[8,48,768]{2,1,0:T(8,128)(2,1)}, u32[]{:S(2)}, u32[]{:S(2)}) collective-permute-start(bf16[8,48,768]{2,1,0:T(8,128)(2,1)} %get-tuple-element.79), channel_id=1, source_target_pairs={{0,64},{16,80},{32,96},{48,112},{64,128},{80,144},{96,160},{112,17... | collective-permute-start | bytes 1769480 | tf_op jit(solution)/shard_map/ppermute | solution.py:249
  41.9 13.6 %collective-permute-start.7 = (bf16[8,48,768]{2,1,0:T(8,128)(2,1)}, bf16[8,48,768]{2,1,0:T(8,128)(2,1)}, u32[]{:S(2)}, u32[]{:S(2)}) collective-permute-start(bf16[8,48,768]{2,1,0:T(8,128)(2,1)} %get-tuple-element.80), channel_id=1, source_target_pairs={{0,192},{16,208},{32,224},{48,240},{64,0},{80,16},{96,32},{112,48}... | collective-permute-start | bytes 1769480 | tf_op jit(solution)/shard_map/ppermute | solution.py:249
  45.1 24.5 %all-to-all-start = ((bf16[16,48,384]{2,1,0:T(8,128)(2,1)}), bf16[16,48,384]{2,1,0:T(8,128)(2,1)}, u32[]{:S(2)}, u32[]{:S(2)}) async-start(bf16[16,48,384]{2,1,0:T(8,128)(2,1)} %bitcast.14), calls=%async_computation | async-start | bytes 1179648 | tf_op jit(solution)/shard_map/all_to_all | solution.py:370
  52.7 2.8 %copy-start.4 = (bf16[8,48,768]{2,1,0:T(8,128)(2,1)}, bf16[8,48,768]{2,1,0:T(8,128)(2,1)S(1)}, u32[]{:S(2)}) copy-start(bf16[8,48,768]{2,1,0:T(8,128)(2,1)S(1)} %collective-permute-done.4.refs_4_) | copy-start | bytes 1769476
  55.3 0.8 copy-start.5
  60.9 13.7 %collective-permute-start.8 = (bf16[8,48,768]{2,1,0:T(8,128)(2,1)}, bf16[8,48,768]{2,1,0:T(8,128)(2,1)S(1)}, u32[]{:S(2)}, u32[]{:S(2)}) collective-permute-start(bf16[8,48,768]{2,1,0:T(8,128)(2,1)} %get-tuple-element.81), channel_id=1, source_target_pairs={{0,16},{16,32},{32,48},{48,0},{64,80},{80,96},{96,112},{112,64},{1... | collective-permute-start | bytes 1769480 | tf_op jit(solution)/shard_map/ppermute | solution.py:249
  63.3 14.6 %collective-permute-start.9 = (bf16[8,48,768]{2,1,0:T(8,128)(2,1)}, bf16[8,48,768]{2,1,0:T(8,128)(2,1)S(1)}, u32[]{:S(2)}, u32[]{:S(2)}) collective-permute-start(bf16[8,48,768]{2,1,0:T(8,128)(2,1)} %get-tuple-element.82), channel_id=1, source_target_pairs={{0,48},{16,0},{32,16},{48,32},{64,112},{80,64},{96,80},{112,96},{1... | collective-permute-start | bytes 1769480 | tf_op jit(solution)/shard_map/ppermute | solution.py:249
  63.3 14.6 %collective-permute-start.10 = (bf16[8,48,768]{2,1,0:T(8,128)(2,1)}, bf16[8,48,768]{2,1,0:T(8,128)(2,1)S(1)}, u32[]{:S(2)}, u32[]{:S(2)}) collective-permute-start(bf16[8,48,768]{2,1,0:T(8,128)(2,1)} %get-tuple-element.83), channel_id=1, source_target_pairs={{0,64},{16,80},{32,96},{48,112},{64,128},{80,144},{96,160},{112,17... | collective-permute-start | bytes 1769480 | tf_op jit(solution)/shard_map/ppermute | solution.py:249
  63.6 14.2 %collective-permute-start.11 = (bf16[8,48,768]{2,1,0:T(8,128)(2,1)}, bf16[8,48,768]{2,1,0:T(8,128)(2,1)S(1)}, u32[]{:S(2)}, u32[]{:S(2)}) collective-permute-start(bf16[8,48,768]{2,1,0:T(8,128)(2,1)} %get-tuple-element.84), channel_id=1, source_target_pairs={{0,192},{16,208},{32,224},{48,240},{64,0},{80,16},{96,32},{112,48}... | collective-permute-start | bytes 1769480 | tf_op jit(solution)/shard_map/ppermute | solution.py:249
  74.5 4.2 %copy-start.6 = (bf16[8,48,768]{2,1,0:T(8,128)(2,1)}, bf16[8,48,768]{2,1,0:T(8,128)(2,1)S(1)}, u32[]{:S(2)}) copy-start(bf16[8,48,768]{2,1,0:T(8,128)(2,1)S(1)} %collective-permute-done.8.refs_6_) | copy-start | bytes 1769476
  77.9 1.0 copy-start.7
  77.9 1.2 copy-start.8
  77.9 0.9 copy-start.9
  79.1 45.0 %all-to-all-start.1 = ((bf16[16,64,768]{2,1,0:T(8,128)(2,1)}), bf16[16,64,768]{2,1,0:T(8,128)(2,1)S(1)}, u32[]{:S(2)}, u32[]{:S(2)}) async-start(bf16[16,64,768]{2,1,0:T(8,128)(2,1)} %shard_map.103), calls=%async_computation.1 | async-start | bytes 3145728 | tf_op jit(solution)/shard_map/all_to_all | solution.py:413
  91.6 20.2 %collective-permute-start.12 = (bf16[4,48,768]{2,1,0:T(8,128)(2,1)}, bf16[4,48,768]{2,1,0:T(8,128)(2,1)S(1)}, u32[]{:S(2)}, u32[]{:S(2)}) collective-permute-start(bf16[4,48,768]{2,1,0:T(8,128)(2,1)} %get-tuple-element.93), channel_id=1, source_target_pairs={{0,64},{16,80},{32,96},{48,112},{64,128},{80,144},{96,160},{112,17... | collective-permute-start | bytes 884744 | tf_op jit(solution)/shard_map/ppermute | solution.py:249
  93.1 23.3 %collective-permute-start.13 = (bf16[4,48,768]{2,1,0:T(8,128)(2,1)}, bf16[4,48,768]{2,1,0:T(8,128)(2,1)S(1)}, u32[]{:S(2)}, u32[]{:S(2)}) collective-permute-start(bf16[4,48,768]{2,1,0:T(8,128)(2,1)} %get-tuple-element.94), channel_id=1, source_target_pairs={{0,128},{16,144},{32,160},{48,176},{64,192},{80,208},{96,224},{112... | collective-permute-start | bytes 884744 | tf_op jit(solution)/shard_map/ppermute | solution.py:249
  95.8 20.6 %collective-permute-start.14 = (bf16[4,48,768]{2,1,0:T(8,128)(2,1)}, bf16[4,48,768]{2,1,0:T(8,128)(2,1)S(1)}, u32[]{:S(2)}, u32[]{:S(2)}) collective-permute-start(bf16[4,48,768]{2,1,0:T(8,128)(2,1)} %get-tuple-element.95), channel_id=1, source_target_pairs={{0,192},{16,208},{32,224},{48,240},{64,0},{80,16},{96,32},{112,48}... | collective-permute-start | bytes 884744 | tf_op jit(solution)/shard_map/ppermute | solution.py:249
  97.3 19.1 %collective-permute-start.15 = (bf16[4,48,768]{2,1,0:T(8,128)(2,1)}, bf16[4,48,768]{2,1,0:T(8,128)(2,1)S(1)}, u32[]{:S(2)}, u32[]{:S(2)}) collective-permute-start(bf16[4,48,768]{2,1,0:T(8,128)(2,1)} %get-tuple-element.97), channel_id=1, source_target_pairs={{0,16},{16,32},{32,48},{48,0},{64,80},{80,96},{96,112},{112,64},{1... | collective-permute-start | bytes 884744 | tf_op jit(solution)/shard_map/ppermute | solution.py:249
  97.8 18.6 %collective-permute-start.16 = (bf16[4,48,768]{2,1,0:T(8,128)(2,1)}, bf16[4,48,768]{2,1,0:T(8,128)(2,1)S(1)}, u32[]{:S(2)}, u32[]{:S(2)}) collective-permute-start(bf16[4,48,768]{2,1,0:T(8,128)(2,1)} %get-tuple-element.98), channel_id=1, source_target_pairs={{0,32},{16,48},{32,0},{48,16},{64,96},{80,112},{96,64},{112,80},{1... | collective-permute-start | bytes 884744 | tf_op jit(solution)/shard_map/ppermute | solution.py:249
  111.7 8.7 %copy-start.10 = (bf16[4,48,768]{2,1,0:T(8,128)(2,1)}, bf16[4,48,768]{2,1,0:T(8,128)(2,1)S(1)}, u32[]{:S(2)}) copy-start(bf16[4,48,768]{2,1,0:T(8,128)(2,1)S(1)} %collective-permute-done.12.refs_1_) | copy-start | bytes 884740
  111.7 8.7 %collective-permute-start.17 = (bf16[4,48,768]{2,1,0:T(8,128)(2,1)}, bf16[4,48,768]{2,1,0:T(8,128)(2,1)S(1)}, u32[]{:S(2)}, u32[]{:S(2)}) collective-permute-start(bf16[4,48,768]{2,1,0:T(8,128)(2,1)} %get-tuple-element.99), channel_id=1, source_target_pairs={{0,48},{16,0},{32,16},{48,32},{64,112},{80,64},{96,80},{112,96},{1... | collective-permute-start | bytes 884744 | tf_op jit(solution)/shard_map/ppermute | solution.py:249
  116.4 4.0 %copy-start.11 = (bf16[4,48,768]{2,1,0:T(8,128)(2,1)}, bf16[4,48,768]{2,1,0:T(8,128)(2,1)S(1)}, u32[]{:S(2)}) copy-start(bf16[4,48,768]{2,1,0:T(8,128)(2,1)S(1)} %collective-permute-done.13.refs_2_) | copy-start | bytes 884740
  116.4 4.0 %copy-start.12 = (bf16[4,48,768]{2,1,0:T(8,128)(2,1)}, bf16[4,48,768]{2,1,0:T(8,128)(2,1)S(1)}, u32[]{:S(2)}) copy-start(bf16[4,48,768]{2,1,0:T(8,128)(2,1)S(1)} %collective-permute-done.14.refs_3_) | copy-start | bytes 884740
  116.4 4.0 %copy-start.13 = (bf16[4,48,768]{2,1,0:T(8,128)(2,1)}, bf16[4,48,768]{2,1,0:T(8,128)(2,1)S(1)}, u32[]{:S(2)}) copy-start(bf16[4,48,768]{2,1,0:T(8,128)(2,1)S(1)} %collective-permute-done.15.refs_5_) | copy-start | bytes 884740
  116.4 4.0 %copy-start.14 = (bf16[4,48,768]{2,1,0:T(8,128)(2,1)}, bf16[4,48,768]{2,1,0:T(8,128)(2,1)S(1)}, u32[]{:S(2)}) copy-start(bf16[4,48,768]{2,1,0:T(8,128)(2,1)S(1)} %collective-permute-done.16.refs_6_) | copy-start | bytes 884740
  120.4 0.7 copy-start.15

commit v7 on v6

--- a/solution.py
+++ b/solution.py
@@ -12,7 +12,7 @@
 SEAT = 64
 SIDE = 4
 BLOCK = 48
-ROWS = 16
+ROWS = 48
 
 EPS = 1e-05
 HALF_ROOT = 0.7071067811865476
@@ -410,7 +410,6 @@
         cost_estimate=cost(2 * owners * SEAT * rows * width, 4_000_000),
     )(grad_sum, swapped, owner_dev.reshape(1, rows), slot_row)
     sent, both_got = lax.optimization_barrier((sent, both_got))
-    landed = lax.all_to_all(sent, "dp", split_axis=0, concat_axis=0, tiled=True)
 
     args, specs = [], []
     for a in range(2):
@@ -422,10 +421,10 @@
     summed = combine(
         second_kernel, specs, args, [4] * 8, [F32, BF16, BF16, BF16] * 2, "second_sums"
     )
-    args = []
-    for a in range(2):
-        args += [summed[a * SIDE]]
-        args += [shift(summed[a * SIDE + away], 1 - a, away) for away in range(1, SIDE)]
+    lined = [shift(summed[a * SIDE + d], 1 - a, d) for a in range(2) for d in range(1, SIDE)]
+    sent, lined[0] = lax.optimization_barrier((sent, lined[0]))
+    landed = lax.all_to_all(sent, "dp", split_axis=0, concat_axis=0, tiled=True)
+    args = [summed[0], *lined[:3], summed[SIDE], *lined[3:]]
     grad_up, grad_down = pl.pallas_call(
         last_kernel,
         out_shape=[

time: 127 us -> 136 us (1.071)
  waiting for transfers between devices: 30 us -> 42.1 us
  starting transfers between devices: 41.2 us -> 38.4 us
  Pallas kernels: 48.8 us -> 47.2 us
    ppermute x18, waiting for transfers between devices: 26.9 us -> 38 us  [shift(): return lax.ppermute(value, 'dp', moves(axis, sign))]
    ppermute x18, starting transfers between devices: 27.1 us -> 24.8 us  [shift(): return lax.ppermute(value, 'dp', moves(axis, sign))]
    pallas_call x2, Pallas kernels: 10.4 us -> 8.79 us  [combine(): pl.pallas_call(kernel, grid=(BLOCK // ROWS,), in_specs=specs, out_specs=[...]
    unnamed x32 -> x36, local copies, waits for them, and re-layouts: 2.56 us -> 3.54 us
  transfers between devices with their start and end apart: 20 -> 20, of which waited for: 9 -> 9; matrix products, arithmetic and copies ran while one was open for 0% -> 0% of each run, Pallas kernels for 25% -> 18%
where the time goes in v7:
time: 136 us; the launch traced here: 134 us
  Pallas kernels  47.2 us (35%)
  waiting for transfers between devices  42.1 us (31%)
  starting transfers between devices  38.4 us (28%)
  local copies, waits for them, and re-layouts  4.09 us (3%)
  matrix products  1.68 us (1%)
    ppermute x18, waiting for transfers between devices, shift(): return lax.ppermute(value, 'dp', moves(axis, sign))  38 us
    ppermute x18, starting transfers between devices, shift(): return lax.ppermute(value, 'dp', moves(axis, sign))  24.8 us
    pallas_call x1, Pallas kernels, per_device(): pl.pallas_call(forward_kernel, grid_spec=pltpu.PrefetchScalarGridSpec(num...  17.9 us
    pallas_call x1, Pallas kernels, per_device(): pl.pallas_call(backward_kernel, grid_spec=pltpu.PrefetchScalarGridSpec(nu...  13.8 us
    pallas_call x2, Pallas kernels, combine(): pl.pallas_call(kernel, grid=(BLOCK // ROWS,), in_specs=specs, out_specs=[...  8.79 us
    all_to_all x1, starting transfers between devices, per_device(): lax.all_to_all(grad_sum.reshape(pieces, width // pieces, rows), 'token',...  7.22 us
    all_to_all x1, starting transfers between devices, per_device(): landed = lax.all_to_all(sent, 'dp', split_axis=0, concat_axis=0, tiled=True)  6.4 us
    all_to_all x1, waiting for transfers between devices, per_device(): lax.all_to_all(grad_sum.reshape(pieces, width // pieces, rows), 'token',...  4.05 us
  transfers between devices with their start and end apart: 20, of which 9 were waited for; matrix products, arithmetic and copies ran while one was open for 0% of the time, Pallas kernels for 18%

profile of v7, /device:TPU:6, one launch (start us, length us, event | category | flops | bytes accessed | tf_op | source)
XLA Modules:
  0.0 134.4 jit_solution(14616555408272317262)
XLA Ops:
  0.7 0.5 concatenate.3.dest
  1.2 17.9 %forward_and_grad_down.1 = (bf16[384,768]{1,0:T(8,128)(2,1)}, f32[4,384,768]{2,1,0:T(8,128)}, f32[384,768]{1,0:T(8,128)}, bf16[384,768]{1,0:T(8,128)(2,1)}, bf16...) custom-call(s32[68]{0:T(128)} %concatenate.3.dest, ...), custom_call_target="tpu_custom_call" | custom-call | flops 5435817984 | bytes 25000000 | tf_op jit(solution)/shard_map/forward_and_grad_down/pallas_call | solution.py:301
  19.1 2.3 %collective-permute-start = (bf16[8,48,768]{2,1,0:T(8,128)(2,1)}, bf16[8,48,768]{2,1,0:T(8,128)(2,1)S(1)}, u32[]{:S(2)}, u32[]{:S(2)}) collective-permute-start(bf16[8,48,768]{2,1,0:T(8,128)(2,1)} %get-tuple-element.65), channel_id=1, source_target_pairs={{0,16},{16,32},{32,48},{48,0},{64,80},{80,96},{96,112},{112,64},{1... | collective-permute-start | bytes 1769480 | tf_op jit(solution)/shard_map/ppermute | solution.py:249
  21.4 0.0 collective-permute-start.1
  21.4 1.4 %collective-permute-start.2 = (bf16[8,48,768]{2,1,0:T(8,128)(2,1)}, bf16[8,48,768]{2,1,0:T(8,128)(2,1)S(1)}, u32[]{:S(2)}, u32[]{:S(2)}) collective-permute-start(bf16[8,48,768]{2,1,0:T(8,128)(2,1)} %get-tuple-element.67), channel_id=1, source_target_pairs={{0,64},{16,80},{32,96},{48,112},{64,128},{80,144},{96,160},{112,17... | collective-permute-start | bytes 1769480 | tf_op jit(solution)/shard_map/ppermute | solution.py:249
  22.8 1.8 %collective-permute-start.3 = (bf16[8,48,768]{2,1,0:T(8,128)(2,1)}, bf16[8,48,768]{2,1,0:T(8,128)(2,1)S(1)}, u32[]{:S(2)}, u32[]{:S(2)}) collective-permute-start(bf16[8,48,768]{2,1,0:T(8,128)(2,1)} %get-tuple-element.68), channel_id=1, source_target_pairs={{0,192},{16,208},{32,224},{48,240},{64,0},{80,16},{96,32},{112,48}... | collective-permute-start | bytes 1769480 | tf_op jit(solution)/shard_map/ppermute | solution.py:249
  24.6 13.8 %backward_and_grad_up.1 = (bf16[768,384]{1,0:T(8,128)(2,1)}, bf16[8,48,768]{2,1,0:T(8,128)(2,1)}, bf16[8,48,768]{2,1,0:T(8,128)(2,1)}, bf16[8,48,768]{2,1,0:T(8,...) custom-call(s32[68]{0:T(128)} %concatenate.3.dest, ...), custom_call_target="tpu_custom_call" | custom-call | flops 5435817984 | bytes 25000000 | tf_op jit(solution)/shard_map/backward_and_grad_up/pallas_call | solution.py:340
  38.5 0.0 collective-permute-done.refs_1_
  38.5 0.0 copy-start
  38.5 0.0 collective-permute-done.1.refs_2_
  38.5 0.0 copy-start.1
  38.5 0.0 collective-permute-done.2.refs_7_.refs_9_
  38.5 0.0 copy-start.2
  38.6 0.0 collective-permute-done.3.refs_8_.refs_10_
  38.6 0.0 copy-start.3
  38.6 3.3 %collective-permute-start.4 = (bf16[8,48,768]{2,1,0:T(8,128)(2,1)}, bf16[8,48,768]{2,1,0:T(8,128)(2,1)S(1)}, u32[]{:S(2)}, u32[]{:S(2)}) collective-permute-start(bf16[8,48,768]{2,1,0:T(8,128)(2,1)} %get-tuple-element.72), channel_id=1, source_target_pairs={{0,16},{16,32},{32,48},{48,0},{64,80},{80,96},{96,112},{112,64},{1... | collective-permute-start | bytes 1769480 | tf_op jit(solution)/shard_map/ppermute | solution.py:249
  41.9 0.0 collective-permute-start.5
  41.9 0.0 collective-permute-start.6
  41.9 3.2 %collective-permute-start.7 = (bf16[8,48,768]{2,1,0:T(8,128)(2,1)}, bf16[8,48,768]{2,1,0:T(8,128)(2,1)}, u32[]{:S(2)}, u32[]{:S(2)}) collective-permute-start(bf16[8,48,768]{2,1,0:T(8,128)(2,1)} %get-tuple-element.82), channel_id=1, source_target_pairs={{0,192},{16,208},{32,224},{48,240},{64,0},{80,16},{96,32},{112,48}... | collective-permute-start | bytes 1769480 | tf_op jit(solution)/shard_map/ppermute | solution.py:249
  45.1 7.2 %all-to-all-start = ((bf16[16,48,384]{2,1,0:T(8,128)(2,1)}), bf16[16,48,384]{2,1,0:T(8,128)(2,1)}, u32[]{:S(2)}, u32[]{:S(2)}) async-start(bf16[16,48,384]{2,1,0:T(8,128)(2,1)} %bitcast.14), calls=%async_computation | async-start | bytes 1179648 | tf_op jit(solution)/shard_map/all_to_all | solution.py:370
  52.4 0.3 collective-permute-done.4.refs_4_
  52.7 2.6 %collective-permute-done.5.refs_5_ = bf16[8,48,768]{2,1,0:T(8,128)(2,1)S(1)} collective-permute-done((bf16[8,48,768]{2,1,0:T(8,128)(2,1)}, bf16[8,48,768]{2,1,0:T(8,128)(2,1)S(1)}, u32[]{:S(2)}, u32[]{:S(2)}) %collective-permute-start.5) | collective-permute-done | bytes 589856 | tf_op jit(solution)/shard_map/ppermute | solution.py:249
  55.3 0.2 collective-permute-done.6.refs_10_.refs_12_
  55.5 0.0 collective-permute-done.7.refs_11_.refs_13_
  55.5 0.0 copy-done
  55.5 0.0 copy-done.1
  55.5 0.6 copy-done.5
  56.1 3.9 %first_sums.1 = (bf16[8,48,768]{2,1,0:T(8,128)(2,1)}, bf16[8,48,768]{2,1,0:T(8,128)(2,1)}, bf16[8,48,768]{2,1,0:T(8,128)(2,1)}, bf16[8,48,768]{2,1,0:T(8,128)(2,1)}) custom-call(bf16[8,48,768]{2,1,0:T(8,128)(2,1)} %get-tuple-element.75.refs_0_, bf16[8,48,768]{2,1,0:T(8,128)(2,1)} %copy-done, bf16[8,48,768]{2,1,0:T(8,128)(2,1)} %copy-done.1, ...), custom_call_target="tpu_custom_call" | custom-call | flops 1000000 | bytes 7000000 | tf_op jit(solution)/shard_map/first_sums/pallas_call | solution.py:384
  60.0 2.3 %collective-permute-start.8 = (bf16[8,48,768]{2,1,0:T(8,128)(2,1)}, bf16[8,48,768]{2,1,0:T(8,128)(2,1)S(1)}, u32[]{:S(2)}, u32[]{:S(2)}) collective-permute-start(bf16[8,48,768]{2,1,0:T(8,128)(2,1)} %get-tuple-element.83), channel_id=1, source_target_pairs={{0,16},{16,32},{32,48},{48,0},{64,80},{80,96},{96,112},{112,64},{1... | collective-permute-start | bytes 1769480 | tf_op jit(solution)/shard_map/ppermute | solution.py:249
  62.3 0.0 collective-permute-start.9
  62.3 0.4 collective-permute-start.10
  62.7 2.8 %collective-permute-start.11 = (bf16[8,48,768]{2,1,0:T(8,128)(2,1)}, bf16[8,48,768]{2,1,0:T(8,128)(2,1)S(1)}, u32[]{:S(2)}, u32[]{:S(2)}) collective-permute-start(bf16[8,48,768]{2,1,0:T(8,128)(2,1)} %get-tuple-element.86), channel_id=1, source_target_pairs={{0,192},{16,208},{32,224},{48,240},{64,0},{80,16},{96,32},{112,48}... | collective-permute-start | bytes 1769480 | tf_op jit(solution)/shard_map/ppermute | solution.py:249
  65.6 4.0 %all-to-all-done = bf16[16,48,384]{2,1,0:T(8,128)(2,1)} async-done(((bf16[16,48,384]{2,1,0:T(8,128)(2,1)}), bf16[16,48,384]{2,1,0:T(8,128)(2,1)}, u32[]{:S(2)}, u32[]{:S(2)}) %all-to-all-start) | async-done | bytes 589856 | tf_op jit(solution)/shard_map/all_to_all | solution.py:370
  69.6 3.7 %shard_map.103 = bf16[16,64,768]{2,1,0:T(8,128)(2,1)} custom-call(bf16[768,384]{1,0:T(8,128)(2,1)} %get-tuple-element.74.grad_sum, bf16[768,384]{1,0:T(8,128)(2,1)} %bitcast.5.swapped, s32[1,384]{1,0:T(1,128)} %bitcast.16, s32[1,384]{1,0:T(1,128)} %slot.1), custom_call_target="tpu_custom_call" | custom-call | flops 603979776 | bytes 4000000 | tf_op jit(solution)/shard_map/pallas_call | solution.py:406
  73.4 0.3 collective-permute-done.8.refs_6_
  73.6 3.3 %collective-permute-done.9.refs_7_ = bf16[8,48,768]{2,1,0:T(8,128)(2,1)S(1)} collective-permute-done((bf16[8,48,768]{2,1,0:T(8,128)(2,1)}, bf16[8,48,768]{2,1,0:T(8,128)(2,1)S(1)}, u32[]{:S(2)}, u32[]{:S(2)}) %collective-permute-start.9) | collective-permute-done | bytes 589856 | tf_op jit(solution)/shard_map/ppermute | solution.py:249
  76.9 0.0 collective-permute-done.10.refs_14_
  76.9 0.0 collective-permute-done.11.refs_15_
  77.0 0.8 copy-done.7
  77.8 0.2 copy-done.8
  77.9 0.2 copy-done.9
  78.1 4.9 %second_sums.1 = (f32[4,48,768]{2,1,0:T(8,128)}, bf16[4,48,768]{2,1,0:T(8,128)(2,1)}, bf16[4,48,768]{2,1,0:T(8,128)(2,1)}, bf16[4,48,768]{2,1,0:T(8,128)(2,1)}, ...) custom-call(bf16[8,48,768]{2,1,0:T(8,128)(2,1)} %get-tuple-element.5, ...), custom_call_target="tpu_custom_call" | custom-call | flops 1000000 | bytes 7000000 | tf_op jit(solution)/shard_map/second_sums/pallas_call | solution.py:384
  83.0 0.1 collective-permute-start.12
  83.1 8.9 %collective-permute-done.12.refs_1_ = bf16[4,48,768]{2,1,0:T(8,128)(2,1)S(1)} collective-permute-done((bf16[4,48,768]{2,1,0:T(8,128)(2,1)}, bf16[4,48,768]{2,1,0:T(8,128)(2,1)S(1)}, u32[]{:S(2)}, u32[]{:S(2)}) %collective-permute-start.12) | collective-permute-done | bytes 294944 | tf_op jit(solution)/shard_map/ppermute | solution.py:249
  92.0 0.7 copy-done.10
  92.7 6.4 %all-to-all-start.1 = ((bf16[16,64,768]{2,1,0:T(8,128)(2,1)}), bf16[16,64,768]{2,1,0:T(8,128)(2,1)S(1)}, u32[]{:S(2)}, u32[]{:S(2)}) async-start(bf16[16,64,768]{2,1,0:T(8,128)(2,1)} %shard_map.103), calls=%async_computation.1 | async-start | bytes 3145728 | tf_op jit(solution)/shard_map/all_to_all | solution.py:426
  99.1 3.0 %collective-permute-start.13 = (bf16[4,48,768]{2,1,0:T(8,128)(2,1)}, bf16[4,48,768]{2,1,0:T(8,128)(2,1)S(1)}, u32[]{:S(2)}, u32[]{:S(2)}) collective-permute-start(bf16[4,48,768]{2,1,0:T(8,128)(2,1)} %get-tuple-element.98), channel_id=1, source_target_pairs={{0,128},{16,144},{32,160},{48,176},{64,192},{80,208},{96,224},{112... | collective-permute-start | bytes 884744 | tf_op jit(solution)/shard_map/ppermute | solution.py:249
  102.1 1.1 collective-permute-start.14
  103.3 0.5 collective-permute-start.15
  103.8 0.0 copy-done.17
  103.8 2.4 %collective-permute-start.16 = (bf16[4,48,768]{2,1,0:T(8,128)(2,1)S(1)}, bf16[4,48,768]{2,1,0:T(8,128)(2,1)S(1)}, u32[]{:S(2)}, u32[]{:S(2)}) collective-permute-start(bf16[4,48,768]{2,1,0:T(8,128)(2,1)S(1)} %copy-done.17), channel_id=1, source_target_pairs={{0,32},{16,48},{32,0},{48,16},{64,96},{80,112},{96,64},{112,80},{1... | collective-permute-start | bytes 884744 | tf_op jit(solution)/shard_map/ppermute | solution.py:249
  106.2 0.0 collective-permute-start.17
  106.2 17.6 %collective-permute-done.13.refs_2_ = bf16[4,48,768]{2,1,0:T(8,128)(2,1)S(1)} collective-permute-done((bf16[4,48,768]{2,1,0:T(8,128)(2,1)}, bf16[4,48,768]{2,1,0:T(8,128)(2,1)S(1)}, u32[]{:S(2)}, u32[]{:S(2)}) %collective-permute-start.13) | collective-permute-done | bytes 294944 | tf_op jit(solution)/shard_map/ppermute | solution.py:249
  123.8 4.8 %collective-permute-done.14.refs_3_ = bf16[4,48,768]{2,1,0:T(8,128)(2,1)S(1)} collective-permute-done((bf16[4,48,768]{2,1,0:T(8,128)(2,1)}, bf16[4,48,768]{2,1,0:T(8,128)(2,1)S(1)}, u32[]{:S(2)}, u32[]{:S(2)}) %collective-permute-start.14) | collective-permute-done | bytes 294944 | tf_op jit(solution)/shard_map/ppermute | solution.py:249
  128.7 0.0 collective-permute-done.15.refs_5_
  128.7 0.0 collective-permute-done.16.refs_6_
  128.7 0.0 collective-permute-done.17.refs_7_
  128.7 0.7 copy-done.12
  129.4 0.1 copy-done.13
  129.5 0.1 copy-done.14
  129.6 0.1 copy-done.15
  129.7 3.0 %last_sums.1 = (f32[48,3072]{1,0:T(8,128)}, f32[192,768]{1,0:T(8,128)}) custom-call(f32[4,48,768]{2,1,0:T(8,128)} %get-tuple-element.94.refs_0_, bf16[4,48,768]{2,1,0:T(8,128)(2,1)} %copy-done.10, bf16[4,48,768]{2,1,0:T(8,128)(2,1)} %copy-done.11, bf16[4,48,768]{2,1,0:T(8,128)(2,1)} %copy-done.12, f32[4,48,768]{2,1,0:T(8,128)} %get-tuple-element.100.refs_4_, ...), custom_call_target="tpu_custom_call" | custom-call | flops 1000000 | bytes 4000000 | tf_op jit(solution)/shard_map/last_sums/pallas_call | solution.py:428
  132.7 0.0 all-to-all-done.1
  132.7 1.7 %convolution_bitcast_fusion = f32[1,256,768]{2,1,0:T(8,128)} fusion(bf16[16,64,768]{2,1,0:T(8,128)(2,1)S(1)} %all-to-all-done.1, s32[16,64]{1,0:T(8,128)S(1)} %bitcast.15), kind=kOutput, calls=%fused_computation | convolution fusion | flops 402915328 | bytes 2363392 | tf_op jit(solution)/shard_map/dot_general | solution.py:443
  (22 shorter events, 0.1 us)
Async XLA Ops:
  19.1 19.4 %collective-permute-start = (bf16[8,48,768]{2,1,0:T(8,128)(2,1)}, bf16[8,48,768]{2,1,0:T(8,128)(2,1)S(1)}, u32[]{:S(2)}, u32[]{:S(2)}) collective-permute-start(bf16[8,48,768]{2,1,0:T(8,128)(2,1)} %get-tuple-element.65), channel_id=1, source_target_pairs={{0,16},{16,32},{32,48},{48,0},{64,80},{80,96},{96,112},{112,64},{1... | collective-permute-start | bytes 1769480 | tf_op jit(solution)/shard_map/ppermute | solution.py:249
  21.4 17.1 %collective-permute-start.1 = (bf16[8,48,768]{2,1,0:T(8,128)(2,1)}, bf16[8,48,768]{2,1,0:T(8,128)(2,1)S(1)}, u32[]{:S(2)}, u32[]{:S(2)}) collective-permute-start(bf16[8,48,768]{2,1,0:T(8,128)(2,1)} %get-tuple-element.66), channel_id=1, source_target_pairs={{0,48},{16,0},{32,16},{48,32},{64,112},{80,64},{96,80},{112,96},{1... | collective-permute-start | bytes 1769480 | tf_op jit(solution)/shard_map/ppermute | solution.py:249
  21.4 17.1 %collective-permute-start.2 = (bf16[8,48,768]{2,1,0:T(8,128)(2,1)}, bf16[8,48,768]{2,1,0:T(8,128)(2,1)S(1)}, u32[]{:S(2)}, u32[]{:S(2)}) collective-permute-start(bf16[8,48,768]{2,1,0:T(8,128)(2,1)} %get-tuple-element.67), channel_id=1, source_target_pairs={{0,64},{16,80},{32,96},{48,112},{64,128},{80,144},{96,160},{112,17... | collective-permute-start | bytes 1769480 | tf_op jit(solution)/shard_map/ppermute | solution.py:249
  22.8 15.8 %collective-permute-start.3 = (bf16[8,48,768]{2,1,0:T(8,128)(2,1)}, bf16[8,48,768]{2,1,0:T(8,128)(2,1)S(1)}, u32[]{:S(2)}, u32[]{:S(2)}) collective-permute-start(bf16[8,48,768]{2,1,0:T(8,128)(2,1)} %get-tuple-element.68), channel_id=1, source_target_pairs={{0,192},{16,208},{32,224},{48,240},{64,0},{80,16},{96,32},{112,48}... | collective-permute-start | bytes 1769480 | tf_op jit(solution)/shard_map/ppermute | solution.py:249
  38.5 17.0 %copy-start = (bf16[8,48,768]{2,1,0:T(8,128)(2,1)}, bf16[8,48,768]{2,1,0:T(8,128)(2,1)S(1)}, u32[]{:S(2)}) copy-start(bf16[8,48,768]{2,1,0:T(8,128)(2,1)S(1)} %collective-permute-done.refs_1_) | copy-start | bytes 1769476
  38.5 16.9 %copy-start.1 = (bf16[8,48,768]{2,1,0:T(8,128)(2,1)}, bf16[8,48,768]{2,1,0:T(8,128)(2,1)S(1)}, u32[]{:S(2)}) copy-start(bf16[8,48,768]{2,1,0:T(8,128)(2,1)S(1)} %collective-permute-done.1.refs_2_) | copy-start | bytes 1769476
  38.5 16.9 %copy-start.2 = (bf16[8,48,768]{2,1,0:T(8,128)(2,1)}, bf16[8,48,768]{2,1,0:T(8,128)(2,1)S(1)}, u32[]{:S(2)}) copy-start(bf16[8,48,768]{2,1,0:T(8,128)(2,1)S(1)} %collective-permute-done.2.refs_7_.refs_9_) | copy-start | bytes 1769476
  38.6 16.9 %copy-start.3 = (bf16[8,48,768]{2,1,0:T(8,128)(2,1)}, bf16[8,48,768]{2,1,0:T(8,128)(2,1)S(1)}, u32[]{:S(2)}) copy-start(bf16[8,48,768]{2,1,0:T(8,128)(2,1)S(1)} %collective-permute-done.3.refs_8_.refs_10_) | copy-start | bytes 1769476
  38.6 14.1 %collective-permute-start.4 = (bf16[8,48,768]{2,1,0:T(8,128)(2,1)}, bf16[8,48,768]{2,1,0:T(8,128)(2,1)S(1)}, u32[]{:S(2)}, u32[]{:S(2)}) collective-permute-start(bf16[8,48,768]{2,1,0:T(8,128)(2,1)} %get-tuple-element.72), channel_id=1, source_target_pairs={{0,16},{16,32},{32,48},{48,0},{64,80},{80,96},{96,112},{112,64},{1... | collective-permute-start | bytes 1769480 | tf_op jit(solution)/shard_map/ppermute | solution.py:249
  41.9 13.4 %collective-permute-start.5 = (bf16[8,48,768]{2,1,0:T(8,128)(2,1)}, bf16[8,48,768]{2,1,0:T(8,128)(2,1)S(1)}, u32[]{:S(2)}, u32[]{:S(2)}) collective-permute-start(bf16[8,48,768]{2,1,0:T(8,128)(2,1)} %get-tuple-element.73), channel_id=1, source_target_pairs={{0,48},{16,0},{32,16},{48,32},{64,112},{80,64},{96,80},{112,96},{1... | collective-permute-start | bytes 1769480 | tf_op jit(solution)/shard_map/ppermute | solution.py:249
  41.9 13.6 %collective-permute-start.6 = (bf16[8,48,768]{2,1,0:T(8,128)(2,1)}, bf16[8,48,768]{2,1,0:T(8,128)(2,1)}, u32[]{:S(2)}, u32[]{:S(2)}) collective-permute-start(bf16[8,48,768]{2,1,0:T(8,128)(2,1)} %get-tuple-element.81), channel_id=1, source_target_pairs={{0,64},{16,80},{32,96},{48,112},{64,128},{80,144},{96,160},{112,17... | collective-permute-start | bytes 1769480 | tf_op jit(solution)/shard_map/ppermute | solution.py:249
  41.9 13.6 %collective-permute-start.7 = (bf16[8,48,768]{2,1,0:T(8,128)(2,1)}, bf16[8,48,768]{2,1,0:T(8,128)(2,1)}, u32[]{:S(2)}, u32[]{:S(2)}) collective-permute-start(bf16[8,48,768]{2,1,0:T(8,128)(2,1)} %get-tuple-element.82), channel_id=1, source_target_pairs={{0,192},{16,208},{32,224},{48,240},{64,0},{80,16},{96,32},{112,48}... | collective-permute-start | bytes 1769480 | tf_op jit(solution)/shard_map/ppermute | solution.py:249
  45.1 24.5 %all-to-all-start = ((bf16[16,48,384]{2,1,0:T(8,128)(2,1)}), bf16[16,48,384]{2,1,0:T(8,128)(2,1)}, u32[]{:S(2)}, u32[]{:S(2)}) async-start(bf16[16,48,384]{2,1,0:T(8,128)(2,1)} %bitcast.14), calls=%async_computation | async-start | bytes 1179648 | tf_op jit(solution)/shard_map/all_to_all | solution.py:370
  52.7 2.8 %copy-start.4 = (bf16[8,48,768]{2,1,0:T(8,128)(2,1)}, bf16[8,48,768]{2,1,0:T(8,128)(2,1)S(1)}, u32[]{:S(2)}) copy-start(bf16[8,48,768]{2,1,0:T(8,128)(2,1)S(1)} %collective-permute-done.4.refs_4_) | copy-start | bytes 1769476
  55.3 0.8 copy-start.5
  60.0 13.6 %collective-permute-start.8 = (bf16[8,48,768]{2,1,0:T(8,128)(2,1)}, bf16[8,48,768]{2,1,0:T(8,128)(2,1)S(1)}, u32[]{:S(2)}, u32[]{:S(2)}) collective-permute-start(bf16[8,48,768]{2,1,0:T(8,128)(2,1)} %get-tuple-element.83), channel_id=1, source_target_pairs={{0,16},{16,32},{32,48},{48,0},{64,80},{80,96},{96,112},{112,64},{1... | collective-permute-start | bytes 1769480 | tf_op jit(solution)/shard_map/ppermute | solution.py:249
  62.3 14.6 %collective-permute-start.9 = (bf16[8,48,768]{2,1,0:T(8,128)(2,1)}, bf16[8,48,768]{2,1,0:T(8,128)(2,1)S(1)}, u32[]{:S(2)}, u32[]{:S(2)}) collective-permute-start(bf16[8,48,768]{2,1,0:T(8,128)(2,1)} %get-tuple-element.84), channel_id=1, source_target_pairs={{0,48},{16,0},{32,16},{48,32},{64,112},{80,64},{96,80},{112,96},{1... | collective-permute-start | bytes 1769480 | tf_op jit(solution)/shard_map/ppermute | solution.py:249
  62.3 14.6 %collective-permute-start.10 = (bf16[8,48,768]{2,1,0:T(8,128)(2,1)}, bf16[8,48,768]{2,1,0:T(8,128)(2,1)S(1)}, u32[]{:S(2)}, u32[]{:S(2)}) collective-permute-start(bf16[8,48,768]{2,1,0:T(8,128)(2,1)} %get-tuple-element.85), channel_id=1, source_target_pairs={{0,64},{16,80},{32,96},{48,112},{64,128},{80,144},{96,160},{112,17... | collective-permute-start | bytes 1769480 | tf_op jit(solution)/shard_map/ppermute | solution.py:249
  62.7 14.2 %collective-permute-start.11 = (bf16[8,48,768]{2,1,0:T(8,128)(2,1)}, bf16[8,48,768]{2,1,0:T(8,128)(2,1)S(1)}, u32[]{:S(2)}, u32[]{:S(2)}) collective-permute-start(bf16[8,48,768]{2,1,0:T(8,128)(2,1)} %get-tuple-element.86), channel_id=1, source_target_pairs={{0,192},{16,208},{32,224},{48,240},{64,0},{80,16},{96,32},{112,48}... | collective-permute-start | bytes 1769480 | tf_op jit(solution)/shard_map/ppermute | solution.py:249
  73.6 3.3 %copy-start.6 = (bf16[8,48,768]{2,1,0:T(8,128)(2,1)}, bf16[8,48,768]{2,1,0:T(8,128)(2,1)S(1)}, u32[]{:S(2)}) copy-start(bf16[8,48,768]{2,1,0:T(8,128)(2,1)S(1)} %collective-permute-done.8.refs_6_) | copy-start | bytes 1769476
  76.9 0.8 copy-start.7
  76.9 1.0 copy-start.8
  76.9 1.2 copy-start.9
  83.0 20.8 %copy-start.17 = (bf16[4,48,768]{2,1,0:T(8,128)(2,1)S(1)}, bf16[4,48,768]{2,1,0:T(8,128)(2,1)}, u32[]{:S(2)}) copy-start(bf16[4,48,768]{2,1,0:T(8,128)(2,1)} %get-tuple-element.102) | copy-start | bytes 884740
  83.0 23.2 %copy-start.16 = (bf16[4,48,768]{2,1,0:T(8,128)(2,1)S(1)}, bf16[4,48,768]{2,1,0:T(8,128)(2,1)}, u32[]{:S(2)}) copy-start(bf16[4,48,768]{2,1,0:T(8,128)(2,1)} %get-tuple-element.103) | copy-start | bytes 884740
  83.0 9.0 %collective-permute-start.12 = (bf16[4,48,768]{2,1,0:T(8,128)(2,1)}, bf16[4,48,768]{2,1,0:T(8,128)(2,1)S(1)}, u32[]{:S(2)}, u32[]{:S(2)}) collective-permute-start(bf16[4,48,768]{2,1,0:T(8,128)(2,1)} %get-tuple-element.96), channel_id=1, source_target_pairs={{0,64},{16,80},{32,96},{48,112},{64,128},{80,144},{96,160},{112,17... | collective-permute-start | bytes 884744 | tf_op jit(solution)/shard_map/ppermute | solution.py:249
  92.0 0.7 copy-start.10
  92.7 40.0 %all-to-all-start.1 = ((bf16[16,64,768]{2,1,0:T(8,128)(2,1)}), bf16[16,64,768]{2,1,0:T(8,128)(2,1)S(1)}, u32[]{:S(2)}, u32[]{:S(2)}) async-start(bf16[16,64,768]{2,1,0:T(8,128)(2,1)} %shard_map.103), calls=%async_computation.1 | async-start | bytes 3145728 | tf_op jit(solution)/shard_map/all_to_all | solution.py:426
  99.1 24.7 %collective-permute-start.13 = (bf16[4,48,768]{2,1,0:T(8,128)(2,1)}, bf16[4,48,768]{2,1,0:T(8,128)(2,1)S(1)}, u32[]{:S(2)}, u32[]{:S(2)}) collective-permute-start(bf16[4,48,768]{2,1,0:T(8,128)(2,1)} %get-tuple-element.98), channel_id=1, source_target_pairs={{0,128},{16,144},{32,160},{48,176},{64,192},{80,208},{96,224},{112... | collective-permute-start | bytes 884744 | tf_op jit(solution)/shard_map/ppermute | solution.py:249
  102.1 26.5 %collective-permute-start.14 = (bf16[4,48,768]{2,1,0:T(8,128)(2,1)}, bf16[4,48,768]{2,1,0:T(8,128)(2,1)S(1)}, u32[]{:S(2)}, u32[]{:S(2)}) collective-permute-start(bf16[4,48,768]{2,1,0:T(8,128)(2,1)} %get-tuple-element.99), channel_id=1, source_target_pairs={{0,192},{16,208},{32,224},{48,240},{64,0},{80,16},{96,32},{112,48}... | collective-permute-start | bytes 884744 | tf_op jit(solution)/shard_map/ppermute | solution.py:249
  103.3 25.4 %collective-permute-start.15 = (bf16[4,48,768]{2,1,0:T(8,128)(2,1)}, bf16[4,48,768]{2,1,0:T(8,128)(2,1)S(1)}, u32[]{:S(2)}, u32[]{:S(2)}) collective-permute-start(bf16[4,48,768]{2,1,0:T(8,128)(2,1)} %get-tuple-element.101), channel_id=1, source_target_pairs={{0,16},{16,32},{32,48},{48,0},{64,80},{80,96},{96,112},{112,64},{1... | collective-permute-start | bytes 884744 | tf_op jit(solution)/shard_map/ppermute | solution.py:249
  103.8 24.9 %collective-permute-start.16 = (bf16[4,48,768]{2,1,0:T(8,128)(2,1)S(1)}, bf16[4,48,768]{2,1,0:T(8,128)(2,1)S(1)}, u32[]{:S(2)}, u32[]{:S(2)}) collective-permute-start(bf16[4,48,768]{2,1,0:T(8,128)(2,1)S(1)} %copy-done.17), channel_id=1, source_target_pairs={{0,32},{16,48},{32,0},{48,16},{64,96},{80,112},{96,64},{112,80},{1... | collective-permute-start | bytes 884744 | tf_op jit(solution)/shard_map/ppermute | solution.py:249
  106.2 22.5 %collective-permute-start.17 = (bf16[4,48,768]{2,1,0:T(8,128)(2,1)S(1)}, bf16[4,48,768]{2,1,0:T(8,128)(2,1)S(1)}, u32[]{:S(2)}, u32[]{:S(2)}) collective-permute-start(bf16[4,48,768]{2,1,0:T(8,128)(2,1)S(1)} %copy-done.16), channel_id=1, source_target_pairs={{0,48},{16,0},{32,16},{48,32},{64,112},{80,64},{96,80},{112,96},{1... | collective-permute-start | bytes 884744 | tf_op jit(solution)/shard_map/ppermute | solution.py:249
  123.8 4.9 %copy-start.11 = (bf16[4,48,768]{2,1,0:T(8,128)(2,1)}, bf16[4,48,768]{2,1,0:T(8,128)(2,1)S(1)}, u32[]{:S(2)}) copy-start(bf16[4,48,768]{2,1,0:T(8,128)(2,1)S(1)} %collective-permute-done.13.refs_2_) | copy-start | bytes 884740
  128.7 0.7 copy-start.12
  128.7 0.8 copy-start.13
  128.7 0.9 copy-start.14
  128.7 1.0 copy-start.15

commit v8 on v7

--- a/solution.py
+++ b/solution.py
@@ -422,7 +422,7 @@
         second_kernel, specs, args, [4] * 8, [F32, BF16, BF16, BF16] * 2, "second_sums"
     )
     lined = [shift(summed[a * SIDE + d], 1 - a, d) for a in range(2) for d in range(1, SIDE)]
-    sent, lined[0] = lax.optimization_barrier((sent, lined[0]))
+    sent, lined = lax.optimization_barrier((sent, lined))
     landed = lax.all_to_all(sent, "dp", split_axis=0, concat_axis=0, tiled=True)
     args = [summed[0], *lined[:3], summed[SIDE], *lined[3:]]
     grad_up, grad_down = pl.pallas_call(

time: 136 us -> 135 us (level)
    ppermute x18, waiting for transfers between devices: 38 us -> 22.2 us  [shift(): return lax.ppermute(value, 'dp', moves(axis, sign))]
    all_to_all x1, waiting for transfers between devices: 0.01 us -> 15.1 us  [per_device(): landed = lax.all_to_all(sent, 'dp', split_axis=0, concat_axis=0, tiled=True)]
    unnamed x36 -> x32, local copies, waits for them, and re-layouts: 3.54 us -> 2.55 us
  transfers between devices with their start and end apart: 20 -> 20, of which waited for: 9 -> 10; matrix products, arithmetic and copies ran while one was open for 0% -> 0% of each run, Pallas kernels for 18% -> 18%
where the time goes in v8:
time: 135 us; the launch traced here: 132 us
  Pallas kernels  47.2 us (35%)
  waiting for transfers between devices  41.4 us (31%)
  starting transfers between devices  37.8 us (28%)
  local copies, waits for them, and re-layouts  3.13 us (2%)
  matrix products  1.68 us (1%)
    ppermute x18, starting transfers between devices, shift(): return lax.ppermute(value, 'dp', moves(axis, sign))  25.4 us
    ppermute x18, waiting for transfers between devices, shift(): return lax.ppermute(value, 'dp', moves(axis, sign))  22.2 us
    pallas_call x1, Pallas kernels, per_device(): pl.pallas_call(forward_kernel, grid_spec=pltpu.PrefetchScalarGridSpec(num...  17.9 us
    all_to_all x1, waiting for transfers between devices, per_device(): landed = lax.all_to_all(sent, 'dp', split_axis=0, concat_axis=0, tiled=True)  15.1 us
    pallas_call x1, Pallas kernels, per_device(): pl.pallas_call(backward_kernel, grid_spec=pltpu.PrefetchScalarGridSpec(nu...  13.8 us
    pallas_call x2, Pallas kernels, combine(): pl.pallas_call(kernel, grid=(BLOCK // ROWS,), in_specs=specs, out_specs=[...  8.79 us
    all_to_all x1, starting transfers between devices, per_device(): lax.all_to_all(grad_sum.reshape(pieces, width // pieces, rows), 'token',...  7.22 us
    all_to_all x1, starting transfers between devices, per_device(): landed = lax.all_to_all(sent, 'dp', split_axis=0, concat_axis=0, tiled=True)  5.19 us
  transfers between devices with their start and end apart: 20, of which 10 were waited for; matrix products, arithmetic and copies ran while one was open for 0% of the time, Pallas kernels for 18%

profile of v8, /device:TPU:6, one launch (start us, length us, event | category | flops | bytes accessed | tf_op | source)
XLA Modules:
  0.0 132.1 jit_solution(17081447301256960309)
XLA Ops:
  0.7 0.6 concatenate.3.dest
  1.3 17.9 %forward_and_grad_down.1 = (bf16[384,768]{1,0:T(8,128)(2,1)}, f32[4,384,768]{2,1,0:T(8,128)}, f32[384,768]{1,0:T(8,128)}, bf16[384,768]{1,0:T(8,128)(2,1)}, bf16...) custom-call(s32[68]{0:T(128)} %concatenate.3.dest, ...), custom_call_target="tpu_custom_call" | custom-call | flops 5435817984 | bytes 25000000 | tf_op jit(solution)/shard_map/forward_and_grad_down/pallas_call | solution.py:301
  19.1 2.3 %collective-permute-start = (bf16[8,48,768]{2,1,0:T(8,128)(2,1)}, bf16[8,48,768]{2,1,0:T(8,128)(2,1)S(1)}, u32[]{:S(2)}, u32[]{:S(2)}) collective-permute-start(bf16[8,48,768]{2,1,0:T(8,128)(2,1)} %get-tuple-element.70), channel_id=1, source_target_pairs={{0,16},{16,32},{32,48},{48,0},{64,80},{80,96},{96,112},{112,64},{1... | collective-permute-start | bytes 1769480 | tf_op jit(solution)/shard_map/ppermute | solution.py:249
  21.4 0.0 collective-permute-start.1
  21.4 1.4 %collective-permute-start.2 = (bf16[8,48,768]{2,1,0:T(8,128)(2,1)}, bf16[8,48,768]{2,1,0:T(8,128)(2,1)S(1)}, u32[]{:S(2)}, u32[]{:S(2)}) collective-permute-start(bf16[8,48,768]{2,1,0:T(8,128)(2,1)} %get-tuple-element.72), channel_id=1, source_target_pairs={{0,64},{16,80},{32,96},{48,112},{64,128},{80,144},{96,160},{112,17... | collective-permute-start | bytes 1769480 | tf_op jit(solution)/shard_map/ppermute | solution.py:249
  22.8 1.9 %collective-permute-start.3 = (bf16[8,48,768]{2,1,0:T(8,128)(2,1)}, bf16[8,48,768]{2,1,0:T(8,128)(2,1)S(1)}, u32[]{:S(2)}, u32[]{:S(2)}) collective-permute-start(bf16[8,48,768]{2,1,0:T(8,128)(2,1)} %get-tuple-element.73), channel_id=1, source_target_pairs={{0,192},{16,208},{32,224},{48,240},{64,0},{80,16},{96,32},{112,48}... | collective-permute-start | bytes 1769480 | tf_op jit(solution)/shard_map/ppermute | solution.py:249
  24.7 13.8 %backward_and_grad_up.1 = (bf16[768,384]{1,0:T(8,128)(2,1)}, bf16[8,48,768]{2,1,0:T(8,128)(2,1)}, bf16[8,48,768]{2,1,0:T(8,128)(2,1)}, bf16[8,48,768]{2,1,0:T(8,...) custom-call(s32[68]{0:T(128)} %concatenate.3.dest, ...), custom_call_target="tpu_custom_call" | custom-call | flops 5435817984 | bytes 25000000 | tf_op jit(solution)/shard_map/backward_and_grad_up/pallas_call | solution.py:340
  38.5 0.0 collective-permute-done.refs_1_
  38.5 0.0 copy-start
  38.5 0.0 collective-permute-done.1.refs_2_
  38.5 0.0 copy-start.1
  38.5 0.0 collective-permute-done.2.refs_7_.refs_9_
  38.6 0.0 copy-start.2
  38.6 0.0 collective-permute-done.3.refs_8_.refs_10_
  38.6 0.0 copy-start.3
  38.6 3.3 %collective-permute-start.4 = (bf16[8,48,768]{2,1,0:T(8,128)(2,1)}, bf16[8,48,768]{2,1,0:T(8,128)(2,1)S(1)}, u32[]{:S(2)}, u32[]{:S(2)}) collective-permute-start(bf16[8,48,768]{2,1,0:T(8,128)(2,1)} %get-tuple-element.77), channel_id=1, source_target_pairs={{0,16},{16,32},{32,48},{48,0},{64,80},{80,96},{96,112},{112,64},{1... | collective-permute-start | bytes 1769480 | tf_op jit(solution)/shard_map/ppermute | solution.py:249
  41.9 0.0 collective-permute-start.5
  41.9 0.0 collective-permute-start.6
  41.9 3.2 %collective-permute-start.7 = (bf16[8,48,768]{2,1,0:T(8,128)(2,1)}, bf16[8,48,768]{2,1,0:T(8,128)(2,1)}, u32[]{:S(2)}, u32[]{:S(2)}) collective-permute-start(bf16[8,48,768]{2,1,0:T(8,128)(2,1)} %get-tuple-element.87), channel_id=1, source_target_pairs={{0,192},{16,208},{32,224},{48,240},{64,0},{80,16},{96,32},{112,48}... | collective-permute-start | bytes 1769480 | tf_op jit(solution)/shard_map/ppermute | solution.py:249
  45.1 7.2 %all-to-all-start = ((bf16[16,48,384]{2,1,0:T(8,128)(2,1)}), bf16[16,48,384]{2,1,0:T(8,128)(2,1)}, u32[]{:S(2)}, u32[]{:S(2)}) async-start(bf16[16,48,384]{2,1,0:T(8,128)(2,1)} %bitcast.14), calls=%async_computation | async-start | bytes 1179648 | tf_op jit(solution)/shard_map/all_to_all | solution.py:370
  52.4 0.3 collective-permute-done.4.refs_4_
  52.7 2.6 %collective-permute-done.5.refs_5_ = bf16[8,48,768]{2,1,0:T(8,128)(2,1)S(1)} collective-permute-done((bf16[8,48,768]{2,1,0:T(8,128)(2,1)}, bf16[8,48,768]{2,1,0:T(8,128)(2,1)S(1)}, u32[]{:S(2)}, u32[]{:S(2)}) %collective-permute-start.5) | collective-permute-done | bytes 589856 | tf_op jit(solution)/shard_map/ppermute | solution.py:249
  55.3 0.2 collective-permute-done.6.refs_10_.refs_12_
  55.5 0.0 collective-permute-done.7.refs_11_.refs_13_
  55.5 0.0 copy-done
  55.5 0.0 copy-done.1
  55.5 0.0 copy-done.2
  55.5 0.0 copy-done.3
  55.5 0.0 copy-done.4
  55.5 0.6 copy-done.5
  56.1 3.9 %first_sums.1 = (bf16[8,48,768]{2,1,0:T(8,128)(2,1)}, bf16[8,48,768]{2,1,0:T(8,128)(2,1)}, bf16[8,48,768]{2,1,0:T(8,128)(2,1)}, bf16[8,48,768]{2,1,0:T(8,128)(2,1)}) custom-call(bf16[8,48,768]{2,1,0:T(8,128)(2,1)} %get-tuple-element.80.refs_0_, bf16[8,48,768]{2,1,0:T(8,128)(2,1)} %copy-done, bf16[8,48,768]{2,1,0:T(8,128)(2,1)} %copy-done.1, ...), custom_call_target="tpu_custom_call" | custom-call | flops 1000000 | bytes 7000000 | tf_op jit(solution)/shard_map/first_sums/pallas_call | solution.py:384
  60.0 2.3 %collective-permute-start.8 = (bf16[8,48,768]{2,1,0:T(8,128)(2,1)}, bf16[8,48,768]{2,1,0:T(8,128)(2,1)S(1)}, u32[]{:S(2)}, u32[]{:S(2)}) collective-permute-start(bf16[8,48,768]{2,1,0:T(8,128)(2,1)} %get-tuple-element.88), channel_id=1, source_target_pairs={{0,16},{16,32},{32,48},{48,0},{64,80},{80,96},{96,112},{112,64},{1... | collective-permute-start | bytes 1769480 | tf_op jit(solution)/shard_map/ppermute | solution.py:249
  62.3 0.0 collective-permute-start.9
  62.3 0.4 collective-permute-start.10
  62.7 2.9 %collective-permute-start.11 = (bf16[8,48,768]{2,1,0:T(8,128)(2,1)}, bf16[8,48,768]{2,1,0:T(8,128)(2,1)S(1)}, u32[]{:S(2)}, u32[]{:S(2)}) collective-permute-start(bf16[8,48,768]{2,1,0:T(8,128)(2,1)} %get-tuple-element.91), channel_id=1, source_target_pairs={{0,192},{16,208},{32,224},{48,240},{64,0},{80,16},{96,32},{112,48}... | collective-permute-start | bytes 1769480 | tf_op jit(solution)/shard_map/ppermute | solution.py:249
  65.5 4.1 %all-to-all-done = bf16[16,48,384]{2,1,0:T(8,128)(2,1)} async-done(((bf16[16,48,384]{2,1,0:T(8,128)(2,1)}), bf16[16,48,384]{2,1,0:T(8,128)(2,1)}, u32[]{:S(2)}, u32[]{:S(2)}) %all-to-all-start) | async-done | bytes 589856 | tf_op jit(solution)/shard_map/all_to_all | solution.py:370
  69.6 3.7 %shard_map.103 = bf16[16,64,768]{2,1,0:T(8,128)(2,1)} custom-call(bf16[768,384]{1,0:T(8,128)(2,1)} %get-tuple-element.79.grad_sum, bf16[768,384]{1,0:T(8,128)(2,1)} %bitcast.5.swapped, s32[1,384]{1,0:T(1,128)} %bitcast.16, s32[1,384]{1,0:T(1,128)} %slot.1), custom_call_target="tpu_custom_call" | custom-call | flops 603979776 | bytes 4000000 | tf_op jit(solution)/shard_map/pallas_call | solution.py:406
  73.4 0.2 collective-permute-done.8.refs_6_
  73.6 3.3 %collective-permute-done.9.refs_7_ = bf16[8,48,768]{2,1,0:T(8,128)(2,1)S(1)} collective-permute-done((bf16[8,48,768]{2,1,0:T(8,128)(2,1)}, bf16[8,48,768]{2,1,0:T(8,128)(2,1)S(1)}, u32[]{:S(2)}, u32[]{:S(2)}) %collective-permute-start.9) | collective-permute-done | bytes 589856 | tf_op jit(solution)/shard_map/ppermute | solution.py:249
  76.9 0.0 collective-permute-done.10.refs_14_
  76.9 0.0 collective-permute-done.11.refs_15_
  76.9 0.0 copy-start.9
  76.9 0.8 copy-done.7
  77.7 0.2 copy-done.8
  77.9 0.2 copy-done.9
  78.1 4.9 %second_sums.1 = (f32[4,48,768]{2,1,0:T(8,128)}, bf16[4,48,768]{2,1,0:T(8,128)(2,1)}, bf16[4,48,768]{2,1,0:T(8,128)(2,1)}, bf16[4,48,768]{2,1,0:T(8,128)(2,1)}, ...) custom-call(bf16[8,48,768]{2,1,0:T(8,128)(2,1)} %get-tuple-element.6, ...), custom_call_target="tpu_custom_call" | custom-call | flops 1000000 | bytes 7000000 | tf_op jit(solution)/shard_map/second_sums/pallas_call | solution.py:384
  83.0 0.0 collective-permute-start.12
  83.1 4.0 %collective-permute-start.13 = (bf16[4,48,768]{2,1,0:T(8,128)(2,1)}, bf16[4,48,768]{2,1,0:T(8,128)(2,1)S(1)}, u32[]{:S(2)}, u32[]{:S(2)}) collective-permute-start(bf16[4,48,768]{2,1,0:T(8,128)(2,1)} %get-tuple-element.102), channel_id=1, source_target_pairs={{0,128},{16,144},{32,160},{48,176},{64,192},{80,208},{96,224},{112... | collective-permute-start | bytes 884744 | tf_op jit(solution)/shard_map/ppermute | solution.py:249
  87.1 0.0 collective-permute-start.14
  87.1 3.0 %collective-permute-start.15 = (bf16[4,48,768]{2,1,0:T(8,128)(2,1)}, bf16[4,48,768]{2,1,0:T(8,128)(2,1)S(1)}, u32[]{:S(2)}, u32[]{:S(2)}) collective-permute-start(bf16[4,48,768]{2,1,0:T(8,128)(2,1)} %get-tuple-element.104), channel_id=1, source_target_pairs={{0,16},{16,32},{32,48},{48,0},{64,80},{80,96},{96,112},{112,64},{1... | collective-permute-start | bytes 884744 | tf_op jit(solution)/shard_map/ppermute | solution.py:249
  90.1 0.0 collective-permute-start.16
  90.1 8.2 %collective-permute-done.12.refs_1_ = bf16[4,48,768]{2,1,0:T(8,128)(2,1)S(1)} collective-permute-done((bf16[4,48,768]{2,1,0:T(8,128)(2,1)}, bf16[4,48,768]{2,1,0:T(8,128)(2,1)S(1)}, u32[]{:S(2)}, u32[]{:S(2)}) %collective-permute-start.12) | collective-permute-done | bytes 294944 | tf_op jit(solution)/shard_map/ppermute | solution.py:249
  98.3 0.8 collective-permute-start.17
  99.1 0.0 collective-permute-done.13.refs_2_
  99.1 0.0 collective-permute-done.14.refs_3_
  99.1 1.1 collective-permute-done.15.refs_5_
  100.3 0.0 collective-permute-done.16.refs_6_
  100.3 6.2 %collective-permute-done.17.refs_7_ = bf16[4,48,768]{2,1,0:T(8,128)(2,1)S(1)} collective-permute-done((bf16[4,48,768]{2,1,0:T(8,128)(2,1)}, bf16[4,48,768]{2,1,0:T(8,128)(2,1)S(1)}, u32[]{:S(2)}, u32[]{:S(2)}) %collective-permute-start.17) | collective-permute-done | bytes 294944 | tf_op jit(solution)/shard_map/ppermute | solution.py:249
  106.4 0.0 copy-done.10
  106.5 0.7 copy-done.15
  107.2 5.2 %all-to-all-start.1 = ((bf16[16,64,768]{2,1,0:T(8,128)(2,1)}), bf16[16,64,768]{2,1,0:T(8,128)(2,1)S(1)}, u32[]{:S(2)}, u32[]{:S(2)}) async-start(bf16[16,64,768]{2,1,0:T(8,128)(2,1)} %shard_map.103), calls=%async_computation.1 | async-start | bytes 3145728 | tf_op jit(solution)/shard_map/all_to_all | solution.py:426
  112.3 3.0 %last_sums.1 = (f32[48,3072]{1,0:T(8,128)}, f32[192,768]{1,0:T(8,128)}) custom-call(f32[4,48,768]{2,1,0:T(8,128)} %get-tuple-element.99.refs_0_, bf16[4,48,768]{2,1,0:T(8,128)(2,1)} %copy-done.10, bf16[4,48,768]{2,1,0:T(8,128)(2,1)} %copy-done.11, bf16[4,48,768]{2,1,0:T(8,128)(2,1)} %copy-done.12, f32[4,48,768]{2,1,0:T(8,128)} %get-tuple-element.110.refs_4_, ...), custom_call_target="tpu_custom_call" | custom-call | flops 1000000 | bytes 4000000 | tf_op jit(solution)/shard_map/last_sums/pallas_call | solution.py:428
  115.3 15.1 %all-to-all-done.1 = bf16[16,64,768]{2,1,0:T(8,128)(2,1)S(1)} async-done(((bf16[16,64,768]{2,1,0:T(8,128)(2,1)}), bf16[16,64,768]{2,1,0:T(8,128)(2,1)S(1)}, u32[]{:S(2)}, u32[]{:S(2)}) %all-to-all-start.1) | async-done | bytes 1572896 | tf_op jit(solution)/shard_map/all_to_all | solution.py:426
  130.4 1.7 %convolution_bitcast_fusion = f32[1,256,768]{2,1,0:T(8,128)} fusion(bf16[16,64,768]{2,1,0:T(8,128)(2,1)S(1)} %all-to-all-done.1, s32[16,64]{1,0:T(8,128)S(1)} %bitcast.15), kind=kOutput, calls=%fused_computation | convolution fusion | flops 402915328 | bytes 2363392 | tf_op jit(solution)/shard_map/dot_general | solution.py:443
  (18 shorter events, 0.1 us)
Async XLA Ops:
  19.1 19.4 %collective-permute-start = (bf16[8,48,768]{2,1,0:T(8,128)(2,1)}, bf16[8,48,768]{2,1,0:T(8,128)(2,1)S(1)}, u32[]{:S(2)}, u32[]{:S(2)}) collective-permute-start(bf16[8,48,768]{2,1,0:T(8,128)(2,1)} %get-tuple-element.70), channel_id=1, source_target_pairs={{0,16},{16,32},{32,48},{48,0},{64,80},{80,96},{96,112},{112,64},{1... | collective-permute-start | bytes 1769480 | tf_op jit(solution)/shard_map/ppermute | solution.py:249
  21.4 17.1 %collective-permute-start.1 = (bf16[8,48,768]{2,1,0:T(8,128)(2,1)}, bf16[8,48,768]{2,1,0:T(8,128)(2,1)S(1)}, u32[]{:S(2)}, u32[]{:S(2)}) collective-permute-start(bf16[8,48,768]{2,1,0:T(8,128)(2,1)} %get-tuple-element.71), channel_id=1, source_target_pairs={{0,48},{16,0},{32,16},{48,32},{64,112},{80,64},{96,80},{112,96},{1... | collective-permute-start | bytes 1769480 | tf_op jit(solution)/shard_map/ppermute | solution.py:249
  21.4 17.1 %collective-permute-start.2 = (bf16[8,48,768]{2,1,0:T(8,128)(2,1)}, bf16[8,48,768]{2,1,0:T(8,128)(2,1)S(1)}, u32[]{:S(2)}, u32[]{:S(2)}) collective-permute-start(bf16[8,48,768]{2,1,0:T(8,128)(2,1)} %get-tuple-element.72), channel_id=1, source_target_pairs={{0,64},{16,80},{32,96},{48,112},{64,128},{80,144},{96,160},{112,17... | collective-permute-start | bytes 1769480 | tf_op jit(solution)/shard_map/ppermute | solution.py:249
  22.8 15.8 %collective-permute-start.3 = (bf16[8,48,768]{2,1,0:T(8,128)(2,1)}, bf16[8,48,768]{2,1,0:T(8,128)(2,1)S(1)}, u32[]{:S(2)}, u32[]{:S(2)}) collective-permute-start(bf16[8,48,768]{2,1,0:T(8,128)(2,1)} %get-tuple-element.73), channel_id=1, source_target_pairs={{0,192},{16,208},{32,224},{48,240},{64,0},{80,16},{96,32},{112,48}... | collective-permute-start | bytes 1769480 | tf_op jit(solution)/shard_map/ppermute | solution.py:249
  38.5 17.0 %copy-start = (bf16[8,48,768]{2,1,0:T(8,128)(2,1)}, bf16[8,48,768]{2,1,0:T(8,128)(2,1)S(1)}, u32[]{:S(2)}) copy-start(bf16[8,48,768]{2,1,0:T(8,128)(2,1)S(1)} %collective-permute-done.refs_1_) | copy-start | bytes 1769476
  38.5 16.9 %copy-start.1 = (bf16[8,48,768]{2,1,0:T(8,128)(2,1)}, bf16[8,48,768]{2,1,0:T(8,128)(2,1)S(1)}, u32[]{:S(2)}) copy-start(bf16[8,48,768]{2,1,0:T(8,128)(2,1)S(1)} %collective-permute-done.1.refs_2_) | copy-start | bytes 1769476
  38.6 16.9 %copy-start.2 = (bf16[8,48,768]{2,1,0:T(8,128)(2,1)}, bf16[8,48,768]{2,1,0:T(8,128)(2,1)S(1)}, u32[]{:S(2)}) copy-start(bf16[8,48,768]{2,1,0:T(8,128)(2,1)S(1)} %collective-permute-done.2.refs_7_.refs_9_) | copy-start | bytes 1769476
  38.6 16.9 %copy-start.3 = (bf16[8,48,768]{2,1,0:T(8,128)(2,1)}, bf16[8,48,768]{2,1,0:T(8,128)(2,1)S(1)}, u32[]{:S(2)}) copy-start(bf16[8,48,768]{2,1,0:T(8,128)(2,1)S(1)} %collective-permute-done.3.refs_8_.refs_10_) | copy-start | bytes 1769476
  38.6 14.1 %collective-permute-start.4 = (bf16[8,48,768]{2,1,0:T(8,128)(2,1)}, bf16[8,48,768]{2,1,0:T(8,128)(2,1)S(1)}, u32[]{:S(2)}, u32[]{:S(2)}) collective-permute-start(bf16[8,48,768]{2,1,0:T(8,128)(2,1)} %get-tuple-element.77), channel_id=1, source_target_pairs={{0,16},{16,32},{32,48},{48,0},{64,80},{80,96},{96,112},{112,64},{1... | collective-permute-start | bytes 1769480 | tf_op jit(solution)/shard_map/ppermute | solution.py:249
  41.9 13.4 %collective-permute-start.5 = (bf16[8,48,768]{2,1,0:T(8,128)(2,1)}, bf16[8,48,768]{2,1,0:T(8,128)(2,1)S(1)}, u32[]{:S(2)}, u32[]{:S(2)}) collective-permute-start(bf16[8,48,768]{2,1,0:T(8,128)(2,1)} %get-tuple-element.78), channel_id=1, source_target_pairs={{0,48},{16,0},{32,16},{48,32},{64,112},{80,64},{96,80},{112,96},{1... | collective-permute-start | bytes 1769480 | tf_op jit(solution)/shard_map/ppermute | solution.py:249
  41.9 13.6 %collective-permute-start.6 = (bf16[8,48,768]{2,1,0:T(8,128)(2,1)}, bf16[8,48,768]{2,1,0:T(8,128)(2,1)}, u32[]{:S(2)}, u32[]{:S(2)}) collective-permute-start(bf16[8,48,768]{2,1,0:T(8,128)(2,1)} %get-tuple-element.86), channel_id=1, source_target_pairs={{0,64},{16,80},{32,96},{48,112},{64,128},{80,144},{96,160},{112,17... | collective-permute-start | bytes 1769480 | tf_op jit(solution)/shard_map/ppermute | solution.py:249
  41.9 13.6 %collective-permute-start.7 = (bf16[8,48,768]{2,1,0:T(8,128)(2,1)}, bf16[8,48,768]{2,1,0:T(8,128)(2,1)}, u32[]{:S(2)}, u32[]{:S(2)}) collective-permute-start(bf16[8,48,768]{2,1,0:T(8,128)(2,1)} %get-tuple-element.87), channel_id=1, source_target_pairs={{0,192},{16,208},{32,224},{48,240},{64,0},{80,16},{96,32},{112,48}... | collective-permute-start | bytes 1769480 | tf_op jit(solution)/shard_map/ppermute | solution.py:249
  45.1 24.5 %all-to-all-start = ((bf16[16,48,384]{2,1,0:T(8,128)(2,1)}), bf16[16,48,384]{2,1,0:T(8,128)(2,1)}, u32[]{:S(2)}, u32[]{:S(2)}) async-start(bf16[16,48,384]{2,1,0:T(8,128)(2,1)} %bitcast.14), calls=%async_computation | async-start | bytes 1179648 | tf_op jit(solution)/shard_map/all_to_all | solution.py:370
  52.7 2.8 %copy-start.4 = (bf16[8,48,768]{2,1,0:T(8,128)(2,1)}, bf16[8,48,768]{2,1,0:T(8,128)(2,1)S(1)}, u32[]{:S(2)}) copy-start(bf16[8,48,768]{2,1,0:T(8,128)(2,1)S(1)} %collective-permute-done.4.refs_4_) | copy-start | bytes 1769476
  55.3 0.8 copy-start.5
  60.0 13.6 %collective-permute-start.8 = (bf16[8,48,768]{2,1,0:T(8,128)(2,1)}, bf16[8,48,768]{2,1,0:T(8,128)(2,1)S(1)}, u32[]{:S(2)}, u32[]{:S(2)}) collective-permute-start(bf16[8,48,768]{2,1,0:T(8,128)(2,1)} %get-tuple-element.88), channel_id=1, source_target_pairs={{0,16},{16,32},{32,48},{48,0},{64,80},{80,96},{96,112},{112,64},{1... | collective-permute-start | bytes 1769480 | tf_op jit(solution)/shard_map/ppermute | solution.py:249
  62.3 14.6 %collective-permute-start.9 = (bf16[8,48,768]{2,1,0:T(8,128)(2,1)}, bf16[8,48,768]{2,1,0:T(8,128)(2,1)S(1)}, u32[]{:S(2)}, u32[]{:S(2)}) collective-permute-start(bf16[8,48,768]{2,1,0:T(8,128)(2,1)} %get-tuple-element.89), channel_id=1, source_target_pairs={{0,48},{16,0},{32,16},{48,32},{64,112},{80,64},{96,80},{112,96},{1... | collective-permute-start | bytes 1769480 | tf_op jit(solution)/shard_map/ppermute | solution.py:249
  62.3 14.6 %collective-permute-start.10 = (bf16[8,48,768]{2,1,0:T(8,128)(2,1)}, bf16[8,48,768]{2,1,0:T(8,128)(2,1)S(1)}, u32[]{:S(2)}, u32[]{:S(2)}) collective-permute-start(bf16[8,48,768]{2,1,0:T(8,128)(2,1)} %get-tuple-element.90), channel_id=1, source_target_pairs={{0,64},{16,80},{32,96},{48,112},{64,128},{80,144},{96,160},{112,17... | collective-permute-start | bytes 1769480 | tf_op jit(solution)/shard_map/ppermute | solution.py:249
  62.7 14.2 %collective-permute-start.11 = (bf16[8,48,768]{2,1,0:T(8,128)(2,1)}, bf16[8,48,768]{2,1,0:T(8,128)(2,1)S(1)}, u32[]{:S(2)}, u32[]{:S(2)}) collective-permute-start(bf16[8,48,768]{2,1,0:T(8,128)(2,1)} %get-tuple-element.91), channel_id=1, source_target_pairs={{0,192},{16,208},{32,224},{48,240},{64,0},{80,16},{96,32},{112,48}... | collective-permute-start | bytes 1769480 | tf_op jit(solution)/shard_map/ppermute | solution.py:249
  73.6 3.3 %copy-start.6 = (bf16[8,48,768]{2,1,0:T(8,128)(2,1)}, bf16[8,48,768]{2,1,0:T(8,128)(2,1)S(1)}, u32[]{:S(2)}) copy-start(bf16[8,48,768]{2,1,0:T(8,128)(2,1)S(1)} %collective-permute-done.8.refs_6_) | copy-start | bytes 1769476
  76.9 0.8 copy-start.7
  76.9 1.0 copy-start.8
  76.9 1.2 copy-start.9
  83.0 15.3 %collective-permute-start.12 = (bf16[4,48,768]{2,1,0:T(8,128)(2,1)}, bf16[4,48,768]{2,1,0:T(8,128)(2,1)S(1)}, u32[]{:S(2)}, u32[]{:S(2)}) collective-permute-start(bf16[4,48,768]{2,1,0:T(8,128)(2,1)} %get-tuple-element.101), channel_id=1, source_target_pairs={{0,64},{16,80},{32,96},{48,112},{64,128},{80,144},{96,160},{112,17... | collective-permute-start | bytes 884744 | tf_op jit(solution)/shard_map/ppermute | solution.py:249
  83.1 16.0 %collective-permute-start.13 = (bf16[4,48,768]{2,1,0:T(8,128)(2,1)}, bf16[4,48,768]{2,1,0:T(8,128)(2,1)S(1)}, u32[]{:S(2)}, u32[]{:S(2)}) collective-permute-start(bf16[4,48,768]{2,1,0:T(8,128)(2,1)} %get-tuple-element.102), channel_id=1, source_target_pairs={{0,128},{16,144},{32,160},{48,176},{64,192},{80,208},{96,224},{112... | collective-permute-start | bytes 884744 | tf_op jit(solution)/shard_map/ppermute | solution.py:249
  87.1 12.0 %collective-permute-start.14 = (bf16[4,48,768]{2,1,0:T(8,128)(2,1)}, bf16[4,48,768]{2,1,0:T(8,128)(2,1)S(1)}, u32[]{:S(2)}, u32[]{:S(2)}) collective-permute-start(bf16[4,48,768]{2,1,0:T(8,128)(2,1)} %get-tuple-element.103), channel_id=1, source_target_pairs={{0,192},{16,208},{32,224},{48,240},{64,0},{80,16},{96,32},{112,48}... | collective-permute-start | bytes 884744 | tf_op jit(solution)/shard_map/ppermute | solution.py:249
  87.1 13.2 %collective-permute-start.15 = (bf16[4,48,768]{2,1,0:T(8,128)(2,1)}, bf16[4,48,768]{2,1,0:T(8,128)(2,1)S(1)}, u32[]{:S(2)}, u32[]{:S(2)}) collective-permute-start(bf16[4,48,768]{2,1,0:T(8,128)(2,1)} %get-tuple-element.104), channel_id=1, source_target_pairs={{0,16},{16,32},{32,48},{48,0},{64,80},{80,96},{96,112},{112,64},{1... | collective-permute-start | bytes 884744 | tf_op jit(solution)/shard_map/ppermute | solution.py:249
  90.1 10.2 %collective-permute-start.16 = (bf16[4,48,768]{2,1,0:T(8,128)(2,1)}, bf16[4,48,768]{2,1,0:T(8,128)(2,1)S(1)}, u32[]{:S(2)}, u32[]{:S(2)}) collective-permute-start(bf16[4,48,768]{2,1,0:T(8,128)(2,1)} %get-tuple-element.105), channel_id=1, source_target_pairs={{0,32},{16,48},{32,0},{48,16},{64,96},{80,112},{96,64},{112,80},{1... | collective-permute-start | bytes 884744 | tf_op jit(solution)/shard_map/ppermute | solution.py:249
  98.3 8.2 %copy-start.10 = (bf16[4,48,768]{2,1,0:T(8,128)(2,1)}, bf16[4,48,768]{2,1,0:T(8,128)(2,1)S(1)}, u32[]{:S(2)}) copy-start(bf16[4,48,768]{2,1,0:T(8,128)(2,1)S(1)} %collective-permute-done.12.refs_1_) | copy-start | bytes 884740
  98.3 8.1 %collective-permute-start.17 = (bf16[4,48,768]{2,1,0:T(8,128)(2,1)}, bf16[4,48,768]{2,1,0:T(8,128)(2,1)S(1)}, u32[]{:S(2)}, u32[]{:S(2)}) collective-permute-start(bf16[4,48,768]{2,1,0:T(8,128)(2,1)} %get-tuple-element.106), channel_id=1, source_target_pairs={{0,48},{16,0},{32,16},{48,32},{64,112},{80,64},{96,80},{112,96},{1... | collective-permute-start | bytes 884744 | tf_op jit(solution)/shard_map/ppermute | solution.py:249
  99.1 7.3 %copy-start.11 = (bf16[4,48,768]{2,1,0:T(8,128)(2,1)}, bf16[4,48,768]{2,1,0:T(8,128)(2,1)S(1)}, u32[]{:S(2)}) copy-start(bf16[4,48,768]{2,1,0:T(8,128)(2,1)S(1)} %collective-permute-done.13.refs_2_) | copy-start | bytes 884740
  99.1 7.3 %copy-start.12 = (bf16[4,48,768]{2,1,0:T(8,128)(2,1)}, bf16[4,48,768]{2,1,0:T(8,128)(2,1)S(1)}, u32[]{:S(2)}) copy-start(bf16[4,48,768]{2,1,0:T(8,128)(2,1)S(1)} %collective-permute-done.14.refs_3_) | copy-start | bytes 884740
  100.3 6.2 %copy-start.13 = (bf16[4,48,768]{2,1,0:T(8,128)(2,1)}, bf16[4,48,768]{2,1,0:T(8,128)(2,1)S(1)}, u32[]{:S(2)}) copy-start(bf16[4,48,768]{2,1,0:T(8,128)(2,1)S(1)} %collective-permute-done.15.refs_5_) | copy-start | bytes 884740
  100.3 6.2 %copy-start.14 = (bf16[4,48,768]{2,1,0:T(8,128)(2,1)}, bf16[4,48,768]{2,1,0:T(8,128)(2,1)S(1)}, u32[]{:S(2)}) copy-start(bf16[4,48,768]{2,1,0:T(8,128)(2,1)S(1)} %collective-permute-done.16.refs_6_) | copy-start | bytes 884740
  106.4 0.7 copy-start.15
  107.2 23.3 %all-to-all-start.1 = ((bf16[16,64,768]{2,1,0:T(8,128)(2,1)}), bf16[16,64,768]{2,1,0:T(8,128)(2,1)S(1)}, u32[]{:S(2)}, u32[]{:S(2)}) async-start(bf16[16,64,768]{2,1,0:T(8,128)(2,1)} %shard_map.103), calls=%async_computation.1 | async-start | bytes 3145728 | tf_op jit(solution)/shard_map/all_to_all | solution.py:426

commit v9 on v6

--- a/solution.py
+++ b/solution.py
@@ -12,7 +12,7 @@
 SEAT = 64
 SIDE = 4
 BLOCK = 48
-ROWS = 16
+ROWS = 48
 
 EPS = 1e-05
 HALF_ROOT = 0.7071067811865476

time: 127 us -> 126 us (level)
  waiting for transfers between devices: 30 us -> 32.4 us
  Pallas kernels: 48.8 us -> 47.2 us
    pallas_call x2, Pallas kernels: 10.4 us -> 8.79 us  [combine(): pl.pallas_call(kernel, grid=(BLOCK // ROWS,), in_specs=specs, out_specs=[...]
    ppermute x18, waiting for transfers between devices: 26.9 us -> 28.3 us  [shift(): return lax.ppermute(value, 'dp', moves(axis, sign))]
  transfers between devices with their start and end apart: 20 -> 20, of which waited for: 9 -> 9; matrix products, arithmetic and copies ran while one was open for 0% -> 0% of each run, Pallas kernels for 25% -> 23%
where the time goes in v9:
time: 126 us
  Pallas kernels  47.2 us (37%)
  starting transfers between devices  40.2 us (32%)
  waiting for transfers between devices  32.4 us (26%)
  local copies, waits for them, and re-layouts  3.14 us (2%)
  matrix products  1.68 us (1%)
    ppermute x18, waiting for transfers between devices, shift(): return lax.ppermute(value, 'dp', moves(axis, sign))  28.3 us
    ppermute x18, starting transfers between devices, shift(): return lax.ppermute(value, 'dp', moves(axis, sign))  26.2 us
    pallas_call x1, Pallas kernels, per_device(): pl.pallas_call(forward_kernel, grid_spec=pltpu.PrefetchScalarGridSpec(num...  17.9 us
    pallas_call x1, Pallas kernels, per_device(): pl.pallas_call(backward_kernel, grid_spec=pltpu.PrefetchScalarGridSpec(nu...  13.8 us
    pallas_call x2, Pallas kernels, combine(): pl.pallas_call(kernel, grid=(BLOCK // ROWS,), in_specs=specs, out_specs=[...  8.79 us
    all_to_all x1, starting transfers between devices, per_device(): lax.all_to_all(grad_sum.reshape(pieces, width // pieces, rows), 'token',...  7.22 us
    all_to_all x1, starting transfers between devices, per_device(): landed = lax.all_to_all(sent, 'dp', split_axis=0, concat_axis=0, tiled=True)  6.84 us
    all_to_all x1, waiting for transfers between devices, per_device(): lax.all_to_all(grad_sum.reshape(pieces, width // pieces, rows), 'token',...  4.08 us
  transfers between devices with their start and end apart: 20, of which 9 were waited for; matrix products, arithmetic and copies ran while one was open for 0% of the time, Pallas kernels for 23%

profile of v9, /device:TPU:6, one launch (start us, length us, event | category | flops | bytes accessed | tf_op | source)
XLA Modules:
  0.0 125.5 jit_solution(10227939142947329447)
XLA Ops:
  0.7 0.6 concatenate.3.dest
  1.3 17.9 %forward_and_grad_down.1 = (bf16[384,768]{1,0:T(8,128)(2,1)}, f32[4,384,768]{2,1,0:T(8,128)}, f32[384,768]{1,0:T(8,128)}, bf16[384,768]{1,0:T(8,128)(2,1)}, bf16...) custom-call(s32[68]{0:T(128)} %concatenate.3.dest, ...), custom_call_target="tpu_custom_call" | custom-call | flops 5435817984 | bytes 25000000 | tf_op jit(solution)/shard_map/forward_and_grad_down/pallas_call | solution.py:301
  19.1 2.3 %collective-permute-start = (bf16[8,48,768]{2,1,0:T(8,128)(2,1)}, bf16[8,48,768]{2,1,0:T(8,128)(2,1)S(1)}, u32[]{:S(2)}, u32[]{:S(2)}) collective-permute-start(bf16[8,48,768]{2,1,0:T(8,128)(2,1)} %get-tuple-element.63), channel_id=1, source_target_pairs={{0,16},{16,32},{32,48},{48,0},{64,80},{80,96},{96,112},{112,64},{1... | collective-permute-start | bytes 1769480 | tf_op jit(solution)/shard_map/ppermute | solution.py:249
  21.4 0.0 collective-permute-start.1
  21.4 1.4 %collective-permute-start.2 = (bf16[8,48,768]{2,1,0:T(8,128)(2,1)}, bf16[8,48,768]{2,1,0:T(8,128)(2,1)S(1)}, u32[]{:S(2)}, u32[]{:S(2)}) collective-permute-start(bf16[8,48,768]{2,1,0:T(8,128)(2,1)} %get-tuple-element.65), channel_id=1, source_target_pairs={{0,64},{16,80},{32,96},{48,112},{64,128},{80,144},{96,160},{112,17... | collective-permute-start | bytes 1769480 | tf_op jit(solution)/shard_map/ppermute | solution.py:249
  22.8 1.9 %collective-permute-start.3 = (bf16[8,48,768]{2,1,0:T(8,128)(2,1)}, bf16[8,48,768]{2,1,0:T(8,128)(2,1)S(1)}, u32[]{:S(2)}, u32[]{:S(2)}) collective-permute-start(bf16[8,48,768]{2,1,0:T(8,128)(2,1)} %get-tuple-element.66), channel_id=1, source_target_pairs={{0,192},{16,208},{32,224},{48,240},{64,0},{80,16},{96,32},{112,48}... | collective-permute-start | bytes 1769480 | tf_op jit(solution)/shard_map/ppermute | solution.py:249
  24.7 13.8 %backward_and_grad_up.1 = (bf16[768,384]{1,0:T(8,128)(2,1)}, bf16[8,48,768]{2,1,0:T(8,128)(2,1)}, bf16[8,48,768]{2,1,0:T(8,128)(2,1)}, bf16[8,48,768]{2,1,0:T(8,...) custom-call(s32[68]{0:T(128)} %concatenate.3.dest, ...), custom_call_target="tpu_custom_call" | custom-call | flops 5435817984 | bytes 25000000 | tf_op jit(solution)/shard_map/backward_and_grad_up/pallas_call | solution.py:340
  38.5 0.0 collective-permute-done.refs_1_
  38.5 0.0 copy-start
  38.5 0.0 collective-permute-done.1.refs_2_
  38.5 0.0 copy-start.1
  38.5 0.0 collective-permute-done.2.refs_7_.refs_9_
  38.6 0.0 copy-start.2
  38.6 0.0 collective-permute-done.3.refs_8_.refs_10_
  38.6 0.0 copy-start.3
  38.6 3.3 %collective-permute-start.4 = (bf16[8,48,768]{2,1,0:T(8,128)(2,1)}, bf16[8,48,768]{2,1,0:T(8,128)(2,1)S(1)}, u32[]{:S(2)}, u32[]{:S(2)}) collective-permute-start(bf16[8,48,768]{2,1,0:T(8,128)(2,1)} %get-tuple-element.70), channel_id=1, source_target_pairs={{0,16},{16,32},{32,48},{48,0},{64,80},{80,96},{96,112},{112,64},{1... | collective-permute-start | bytes 1769480 | tf_op jit(solution)/shard_map/ppermute | solution.py:249
  41.9 0.0 collective-permute-start.5
  41.9 0.0 collective-permute-start.6
  41.9 3.2 %collective-permute-start.7 = (bf16[8,48,768]{2,1,0:T(8,128)(2,1)}, bf16[8,48,768]{2,1,0:T(8,128)(2,1)}, u32[]{:S(2)}, u32[]{:S(2)}) collective-permute-start(bf16[8,48,768]{2,1,0:T(8,128)(2,1)} %get-tuple-element.80), channel_id=1, source_target_pairs={{0,192},{16,208},{32,224},{48,240},{64,0},{80,16},{96,32},{112,48}... | collective-permute-start | bytes 1769480 | tf_op jit(solution)/shard_map/ppermute | solution.py:249
  45.1 7.2 %all-to-all-start = ((bf16[16,48,384]{2,1,0:T(8,128)(2,1)}), bf16[16,48,384]{2,1,0:T(8,128)(2,1)}, u32[]{:S(2)}, u32[]{:S(2)}) async-start(bf16[16,48,384]{2,1,0:T(8,128)(2,1)} %bitcast.14), calls=%async_computation | async-start | bytes 1179648 | tf_op jit(solution)/shard_map/all_to_all | solution.py:370
  52.4 0.3 collective-permute-done.4.refs_4_
  52.7 2.6 %collective-permute-done.5.refs_5_ = bf16[8,48,768]{2,1,0:T(8,128)(2,1)S(1)} collective-permute-done((bf16[8,48,768]{2,1,0:T(8,128)(2,1)}, bf16[8,48,768]{2,1,0:T(8,128)(2,1)S(1)}, u32[]{:S(2)}, u32[]{:S(2)}) %collective-permute-start.5) | collective-permute-done | bytes 589856 | tf_op jit(solution)/shard_map/ppermute | solution.py:249
  55.3 0.2 collective-permute-done.6.refs_10_.refs_12_
  55.5 0.0 collective-permute-done.7.refs_11_.refs_13_
  55.5 0.0 copy-done.1
  55.5 0.0 copy-done.2
  55.5 0.0 copy-done.3
  55.5 0.0 copy-done.4
  55.5 0.6 copy-done.5
  56.1 3.9 %first_sums.1 = (bf16[8,48,768]{2,1,0:T(8,128)(2,1)}, bf16[8,48,768]{2,1,0:T(8,128)(2,1)}, bf16[8,48,768]{2,1,0:T(8,128)(2,1)}, bf16[8,48,768]{2,1,0:T(8,128)(2,1)}) custom-call(bf16[8,48,768]{2,1,0:T(8,128)(2,1)} %get-tuple-element.73.refs_0_, bf16[8,48,768]{2,1,0:T(8,128)(2,1)} %copy-done, bf16[8,48,768]{2,1,0:T(8,128)(2,1)} %copy-done.1, ...), custom_call_target="tpu_custom_call" | custom-call | flops 1000000 | bytes 7000000 | tf_op jit(solution)/shard_map/first_sums/pallas_call | solution.py:384
  60.0 2.3 %collective-permute-start.8 = (bf16[8,48,768]{2,1,0:T(8,128)(2,1)}, bf16[8,48,768]{2,1,0:T(8,128)(2,1)S(1)}, u32[]{:S(2)}, u32[]{:S(2)}) collective-permute-start(bf16[8,48,768]{2,1,0:T(8,128)(2,1)} %get-tuple-element.81), channel_id=1, source_target_pairs={{0,16},{16,32},{32,48},{48,0},{64,80},{80,96},{96,112},{112,64},{1... | collective-permute-start | bytes 1769480 | tf_op jit(solution)/shard_map/ppermute | solution.py:249
  62.3 0.0 collective-permute-start.9
  62.3 0.4 collective-permute-start.10
  62.7 2.9 %collective-permute-start.11 = (bf16[8,48,768]{2,1,0:T(8,128)(2,1)}, bf16[8,48,768]{2,1,0:T(8,128)(2,1)S(1)}, u32[]{:S(2)}, u32[]{:S(2)}) collective-permute-start(bf16[8,48,768]{2,1,0:T(8,128)(2,1)} %get-tuple-element.84), channel_id=1, source_target_pairs={{0,192},{16,208},{32,224},{48,240},{64,0},{80,16},{96,32},{112,48}... | collective-permute-start | bytes 1769480 | tf_op jit(solution)/shard_map/ppermute | solution.py:249
  65.5 4.1 %all-to-all-done = bf16[16,48,384]{2,1,0:T(8,128)(2,1)} async-done(((bf16[16,48,384]{2,1,0:T(8,128)(2,1)}), bf16[16,48,384]{2,1,0:T(8,128)(2,1)}, u32[]{:S(2)}, u32[]{:S(2)}) %all-to-all-start) | async-done | bytes 589856 | tf_op jit(solution)/shard_map/all_to_all | solution.py:370
  69.6 3.7 %shard_map.103 = bf16[16,64,768]{2,1,0:T(8,128)(2,1)} custom-call(bf16[768,384]{1,0:T(8,128)(2,1)} %get-tuple-element.72.grad_sum, bf16[768,384]{1,0:T(8,128)(2,1)} %bitcast.5.swapped, s32[1,384]{1,0:T(1,128)} %bitcast.16, s32[1,384]{1,0:T(1,128)} %slot.1), custom_call_target="tpu_custom_call" | custom-call | flops 603979776 | bytes 4000000 | tf_op jit(solution)/shard_map/pallas_call | solution.py:406
  73.4 0.2 collective-permute-done.8.refs_6_
  73.6 3.3 %collective-permute-done.9.refs_7_ = bf16[8,48,768]{2,1,0:T(8,128)(2,1)S(1)} collective-permute-done((bf16[8,48,768]{2,1,0:T(8,128)(2,1)}, bf16[8,48,768]{2,1,0:T(8,128)(2,1)S(1)}, u32[]{:S(2)}, u32[]{:S(2)}) %collective-permute-start.9) | collective-permute-done | bytes 589856 | tf_op jit(solution)/shard_map/ppermute | solution.py:249
  76.9 0.0 collective-permute-done.10.refs_14_
  76.9 0.0 collective-permute-done.11.refs_15_
  76.9 0.0 copy-start.9
  76.9 0.9 copy-done.9
  77.8 0.1 copy-done.7
  77.9 0.2 copy-done.8
  78.1 6.8 %all-to-all-start.1 = ((bf16[16,64,768]{2,1,0:T(8,128)(2,1)}), bf16[16,64,768]{2,1,0:T(8,128)(2,1)S(1)}, u32[]{:S(2)}, u32[]{:S(2)}) async-start(bf16[16,64,768]{2,1,0:T(8,128)(2,1)} %shard_map.103), calls=%async_computation.1 | async-start | bytes 3145728 | tf_op jit(solution)/shard_map/all_to_all | solution.py:413
  85.0 4.9 %second_sums.1 = (f32[4,48,768]{2,1,0:T(8,128)}, bf16[4,48,768]{2,1,0:T(8,128)(2,1)}, bf16[4,48,768]{2,1,0:T(8,128)(2,1)}, bf16[4,48,768]{2,1,0:T(8,128)(2,1)}, ...) custom-call(bf16[8,48,768]{2,1,0:T(8,128)(2,1)} %get-tuple-element.5, ...), custom_call_target="tpu_custom_call" | custom-call | flops 1000000 | bytes 7000000 | tf_op jit(solution)/shard_map/second_sums/pallas_call | solution.py:384
  89.9 1.5 %collective-permute-start.12 = (bf16[4,48,768]{2,1,0:T(8,128)(2,1)}, bf16[4,48,768]{2,1,0:T(8,128)(2,1)S(1)}, u32[]{:S(2)}, u32[]{:S(2)}) collective-permute-start(bf16[4,48,768]{2,1,0:T(8,128)(2,1)} %get-tuple-element.93), channel_id=1, source_target_pairs={{0,64},{16,80},{32,96},{48,112},{64,128},{80,144},{96,160},{112,17... | collective-permute-start | bytes 884744 | tf_op jit(solution)/shard_map/ppermute | solution.py:249
  91.4 2.7 %collective-permute-start.13 = (bf16[4,48,768]{2,1,0:T(8,128)(2,1)}, bf16[4,48,768]{2,1,0:T(8,128)(2,1)S(1)}, u32[]{:S(2)}, u32[]{:S(2)}) collective-permute-start(bf16[4,48,768]{2,1,0:T(8,128)(2,1)} %get-tuple-element.94), channel_id=1, source_target_pairs={{0,128},{16,144},{32,160},{48,176},{64,192},{80,208},{96,224},{112... | collective-permute-start | bytes 884744 | tf_op jit(solution)/shard_map/ppermute | solution.py:249
  94.0 1.5 %collective-permute-start.14 = (bf16[4,48,768]{2,1,0:T(8,128)(2,1)}, bf16[4,48,768]{2,1,0:T(8,128)(2,1)S(1)}, u32[]{:S(2)}, u32[]{:S(2)}) collective-permute-start(bf16[4,48,768]{2,1,0:T(8,128)(2,1)} %get-tuple-element.95), channel_id=1, source_target_pairs={{0,192},{16,208},{32,224},{48,240},{64,0},{80,16},{96,32},{112,48}... | collective-permute-start | bytes 884744 | tf_op jit(solution)/shard_map/ppermute | solution.py:249
  95.5 0.6 collective-permute-start.15
  96.1 2.4 %collective-permute-start.16 = (bf16[4,48,768]{2,1,0:T(8,128)(2,1)}, bf16[4,48,768]{2,1,0:T(8,128)(2,1)S(1)}, u32[]{:S(2)}, u32[]{:S(2)}) collective-permute-start(bf16[4,48,768]{2,1,0:T(8,128)(2,1)} %get-tuple-element.98), channel_id=1, source_target_pairs={{0,32},{16,48},{32,0},{48,16},{64,96},{80,112},{96,64},{112,80},{1... | collective-permute-start | bytes 884744 | tf_op jit(solution)/shard_map/ppermute | solution.py:249
  98.4 12.7 %collective-permute-done.12.refs_1_ = bf16[4,48,768]{2,1,0:T(8,128)(2,1)S(1)} collective-permute-done((bf16[4,48,768]{2,1,0:T(8,128)(2,1)}, bf16[4,48,768]{2,1,0:T(8,128)(2,1)S(1)}, u32[]{:S(2)}, u32[]{:S(2)}) %collective-permute-start.12) | collective-permute-done | bytes 294944 | tf_op jit(solution)/shard_map/ppermute | solution.py:249
  111.1 0.0 collective-permute-start.17
  111.1 5.2 %collective-permute-done.13.refs_2_ = bf16[4,48,768]{2,1,0:T(8,128)(2,1)S(1)} collective-permute-done((bf16[4,48,768]{2,1,0:T(8,128)(2,1)}, bf16[4,48,768]{2,1,0:T(8,128)(2,1)S(1)}, u32[]{:S(2)}, u32[]{:S(2)}) %collective-permute-start.13) | collective-permute-done | bytes 294944 | tf_op jit(solution)/shard_map/ppermute | solution.py:249
  116.4 0.0 collective-permute-done.14.refs_3_
  116.4 0.0 collective-permute-done.15.refs_5_
  116.4 0.0 collective-permute-done.16.refs_6_
  116.4 0.0 copy-start.14
  116.4 3.7 %collective-permute-done.17.refs_7_ = bf16[4,48,768]{2,1,0:T(8,128)(2,1)S(1)} collective-permute-done((bf16[4,48,768]{2,1,0:T(8,128)(2,1)}, bf16[4,48,768]{2,1,0:T(8,128)(2,1)S(1)}, u32[]{:S(2)}, u32[]{:S(2)}) %collective-permute-start.17) | collective-permute-done | bytes 294944 | tf_op jit(solution)/shard_map/ppermute | solution.py:249
  120.1 0.0 copy-done.10
  120.2 0.7 copy-done.15
  120.9 3.0 %last_sums.1 = (f32[48,3072]{1,0:T(8,128)}, f32[192,768]{1,0:T(8,128)}) custom-call(f32[4,48,768]{2,1,0:T(8,128)} %get-tuple-element.92.refs_0_, bf16[4,48,768]{2,1,0:T(8,128)(2,1)} %copy-done.10, bf16[4,48,768]{2,1,0:T(8,128)(2,1)} %copy-done.11, bf16[4,48,768]{2,1,0:T(8,128)(2,1)} %copy-done.12, f32[4,48,768]{2,1,0:T(8,128)} %get-tuple-element.96.refs_4_, ...), custom_call_target="tpu_custom_call" | custom-call | flops 1000000 | bytes 4000000 | tf_op jit(solution)/shard_map/last_sums/pallas_call | solution.py:429
  123.8 0.0 all-to-all-done.1
  123.9 1.7 %convolution_bitcast_fusion = f32[1,256,768]{2,1,0:T(8,128)} fusion(bf16[16,64,768]{2,1,0:T(8,128)(2,1)S(1)} %all-to-all-done.1, s32[16,64]{1,0:T(8,128)S(1)} %bitcast.15), kind=kOutput, calls=%fused_computation | convolution fusion | flops 402915328 | bytes 2363392 | tf_op jit(solution)/shard_map/dot_general | solution.py:444
  (18 shorter events, 0.1 us)
Async XLA Ops:
  19.1 19.4 %collective-permute-start = (bf16[8,48,768]{2,1,0:T(8,128)(2,1)}, bf16[8,48,768]{2,1,0:T(8,128)(2,1)S(1)}, u32[]{:S(2)}, u32[]{:S(2)}) collective-permute-start(bf16[8,48,768]{2,1,0:T(8,128)(2,1)} %get-tuple-element.63), channel_id=1, source_target_pairs={{0,16},{16,32},{32,48},{48,0},{64,80},{80,96},{96,112},{112,64},{1... | collective-permute-start | bytes 1769480 | tf_op jit(solution)/shard_map/ppermute | solution.py:249
  21.4 17.1 %collective-permute-start.1 = (bf16[8,48,768]{2,1,0:T(8,128)(2,1)}, bf16[8,48,768]{2,1,0:T(8,128)(2,1)S(1)}, u32[]{:S(2)}, u32[]{:S(2)}) collective-permute-start(bf16[8,48,768]{2,1,0:T(8,128)(2,1)} %get-tuple-element.64), channel_id=1, source_target_pairs={{0,48},{16,0},{32,16},{48,32},{64,112},{80,64},{96,80},{112,96},{1... | collective-permute-start | bytes 1769480 | tf_op jit(solution)/shard_map/ppermute | solution.py:249
  21.4 17.1 %collective-permute-start.2 = (bf16[8,48,768]{2,1,0:T(8,128)(2,1)}, bf16[8,48,768]{2,1,0:T(8,128)(2,1)S(1)}, u32[]{:S(2)}, u32[]{:S(2)}) collective-permute-start(bf16[8,48,768]{2,1,0:T(8,128)(2,1)} %get-tuple-element.65), channel_id=1, source_target_pairs={{0,64},{16,80},{32,96},{48,112},{64,128},{80,144},{96,160},{112,17... | collective-permute-start | bytes 1769480 | tf_op jit(solution)/shard_map/ppermute | solution.py:249
  22.8 15.8 %collective-permute-start.3 = (bf16[8,48,768]{2,1,0:T(8,128)(2,1)}, bf16[8,48,768]{2,1,0:T(8,128)(2,1)S(1)}, u32[]{:S(2)}, u32[]{:S(2)}) collective-permute-start(bf16[8,48,768]{2,1,0:T(8,128)(2,1)} %get-tuple-element.66), channel_id=1, source_target_pairs={{0,192},{16,208},{32,224},{48,240},{64,0},{80,16},{96,32},{112,48}... | collective-permute-start | bytes 1769480 | tf_op jit(solution)/shard_map/ppermute | solution.py:249
  38.5 17.0 %copy-start = (bf16[8,48,768]{2,1,0:T(8,128)(2,1)}, bf16[8,48,768]{2,1,0:T(8,128)(2,1)S(1)}, u32[]{:S(2)}) copy-start(bf16[8,48,768]{2,1,0:T(8,128)(2,1)S(1)} %collective-permute-done.refs_1_) | copy-start | bytes 1769476
  38.5 16.9 %copy-start.1 = (bf16[8,48,768]{2,1,0:T(8,128)(2,1)}, bf16[8,48,768]{2,1,0:T(8,128)(2,1)S(1)}, u32[]{:S(2)}) copy-start(bf16[8,48,768]{2,1,0:T(8,128)(2,1)S(1)} %collective-permute-done.1.refs_2_) | copy-start | bytes 1769476
  38.6 16.9 %copy-start.2 = (bf16[8,48,768]{2,1,0:T(8,128)(2,1)}, bf16[8,48,768]{2,1,0:T(8,128)(2,1)S(1)}, u32[]{:S(2)}) copy-start(bf16[8,48,768]{2,1,0:T(8,128)(2,1)S(1)} %collective-permute-done.2.refs_7_.refs_9_) | copy-start | bytes 1769476
  38.6 16.9 %copy-start.3 = (bf16[8,48,768]{2,1,0:T(8,128)(2,1)}, bf16[8,48,768]{2,1,0:T(8,128)(2,1)S(1)}, u32[]{:S(2)}) copy-start(bf16[8,48,768]{2,1,0:T(8,128)(2,1)S(1)} %collective-permute-done.3.refs_8_.refs_10_) | copy-start | bytes 1769476
  38.6 14.1 %collective-permute-start.4 = (bf16[8,48,768]{2,1,0:T(8,128)(2,1)}, bf16[8,48,768]{2,1,0:T(8,128)(2,1)S(1)}, u32[]{:S(2)}, u32[]{:S(2)}) collective-permute-start(bf16[8,48,768]{2,1,0:T(8,128)(2,1)} %get-tuple-element.70), channel_id=1, source_target_pairs={{0,16},{16,32},{32,48},{48,0},{64,80},{80,96},{96,112},{112,64},{1... | collective-permute-start | bytes 1769480 | tf_op jit(solution)/shard_map/ppermute | solution.py:249
  41.9 13.4 %collective-permute-start.5 = (bf16[8,48,768]{2,1,0:T(8,128)(2,1)}, bf16[8,48,768]{2,1,0:T(8,128)(2,1)S(1)}, u32[]{:S(2)}, u32[]{:S(2)}) collective-permute-start(bf16[8,48,768]{2,1,0:T(8,128)(2,1)} %get-tuple-element.71), channel_id=1, source_target_pairs={{0,48},{16,0},{32,16},{48,32},{64,112},{80,64},{96,80},{112,96},{1... | collective-permute-start | bytes 1769480 | tf_op jit(solution)/shard_map/ppermute | solution.py:249
  41.9 13.6 %collective-permute-start.6 = (bf16[8,48,768]{2,1,0:T(8,128)(2,1)}, bf16[8,48,768]{2,1,0:T(8,128)(2,1)}, u32[]{:S(2)}, u32[]{:S(2)}) collective-permute-start(bf16[8,48,768]{2,1,0:T(8,128)(2,1)} %get-tuple-element.79), channel_id=1, source_target_pairs={{0,64},{16,80},{32,96},{48,112},{64,128},{80,144},{96,160},{112,17... | collective-permute-start | bytes 1769480 | tf_op jit(solution)/shard_map/ppermute | solution.py:249
  41.9 13.6 %collective-permute-start.7 = (bf16[8,48,768]{2,1,0:T(8,128)(2,1)}, bf16[8,48,768]{2,1,0:T(8,128)(2,1)}, u32[]{:S(2)}, u32[]{:S(2)}) collective-permute-start(bf16[8,48,768]{2,1,0:T(8,128)(2,1)} %get-tuple-element.80), channel_id=1, source_target_pairs={{0,192},{16,208},{32,224},{48,240},{64,0},{80,16},{96,32},{112,48}... | collective-permute-start | bytes 1769480 | tf_op jit(solution)/shard_map/ppermute | solution.py:249
  45.1 24.5 %all-to-all-start = ((bf16[16,48,384]{2,1,0:T(8,128)(2,1)}), bf16[16,48,384]{2,1,0:T(8,128)(2,1)}, u32[]{:S(2)}, u32[]{:S(2)}) async-start(bf16[16,48,384]{2,1,0:T(8,128)(2,1)} %bitcast.14), calls=%async_computation | async-start | bytes 1179648 | tf_op jit(solution)/shard_map/all_to_all | solution.py:370
  52.7 2.8 %copy-start.4 = (bf16[8,48,768]{2,1,0:T(8,128)(2,1)}, bf16[8,48,768]{2,1,0:T(8,128)(2,1)S(1)}, u32[]{:S(2)}) copy-start(bf16[8,48,768]{2,1,0:T(8,128)(2,1)S(1)} %collective-permute-done.4.refs_4_) | copy-start | bytes 1769476
  55.3 0.8 copy-start.5
  60.0 13.6 %collective-permute-start.8 = (bf16[8,48,768]{2,1,0:T(8,128)(2,1)}, bf16[8,48,768]{2,1,0:T(8,128)(2,1)S(1)}, u32[]{:S(2)}, u32[]{:S(2)}) collective-permute-start(bf16[8,48,768]{2,1,0:T(8,128)(2,1)} %get-tuple-element.81), channel_id=1, source_target_pairs={{0,16},{16,32},{32,48},{48,0},{64,80},{80,96},{96,112},{112,64},{1... | collective-permute-start | bytes 1769480 | tf_op jit(solution)/shard_map/ppermute | solution.py:249
  62.3 14.6 %collective-permute-start.9 = (bf16[8,48,768]{2,1,0:T(8,128)(2,1)}, bf16[8,48,768]{2,1,0:T(8,128)(2,1)S(1)}, u32[]{:S(2)}, u32[]{:S(2)}) collective-permute-start(bf16[8,48,768]{2,1,0:T(8,128)(2,1)} %get-tuple-element.82), channel_id=1, source_target_pairs={{0,48},{16,0},{32,16},{48,32},{64,112},{80,64},{96,80},{112,96},{1... | collective-permute-start | bytes 1769480 | tf_op jit(solution)/shard_map/ppermute | solution.py:249
  62.3 14.6 %collective-permute-start.10 = (bf16[8,48,768]{2,1,0:T(8,128)(2,1)}, bf16[8,48,768]{2,1,0:T(8,128)(2,1)S(1)}, u32[]{:S(2)}, u32[]{:S(2)}) collective-permute-start(bf16[8,48,768]{2,1,0:T(8,128)(2,1)} %get-tuple-element.83), channel_id=1, source_target_pairs={{0,64},{16,80},{32,96},{48,112},{64,128},{80,144},{96,160},{112,17... | collective-permute-start | bytes 1769480 | tf_op jit(solution)/shard_map/ppermute | solution.py:249
  62.7 14.2 %collective-permute-start.11 = (bf16[8,48,768]{2,1,0:T(8,128)(2,1)}, bf16[8,48,768]{2,1,0:T(8,128)(2,1)S(1)}, u32[]{:S(2)}, u32[]{:S(2)}) collective-permute-start(bf16[8,48,768]{2,1,0:T(8,128)(2,1)} %get-tuple-element.84), channel_id=1, source_target_pairs={{0,192},{16,208},{32,224},{48,240},{64,0},{80,16},{96,32},{112,48}... | collective-permute-start | bytes 1769480 | tf_op jit(solution)/shard_map/ppermute | solution.py:249
  73.6 4.2 %copy-start.6 = (bf16[8,48,768]{2,1,0:T(8,128)(2,1)}, bf16[8,48,768]{2,1,0:T(8,128)(2,1)S(1)}, u32[]{:S(2)}) copy-start(bf16[8,48,768]{2,1,0:T(8,128)(2,1)S(1)} %collective-permute-done.8.refs_6_) | copy-start | bytes 1769476
  76.9 1.0 copy-start.7
  76.9 1.2 copy-start.8
  76.9 0.9 copy-start.9
  78.1 45.7 %all-to-all-start.1 = ((bf16[16,64,768]{2,1,0:T(8,128)(2,1)}), bf16[16,64,768]{2,1,0:T(8,128)(2,1)S(1)}, u32[]{:S(2)}, u32[]{:S(2)}) async-start(bf16[16,64,768]{2,1,0:T(8,128)(2,1)} %shard_map.103), calls=%async_computation.1 | async-start | bytes 3145728 | tf_op jit(solution)/shard_map/all_to_all | solution.py:413
  89.9 21.3 %collective-permute-start.12 = (bf16[4,48,768]{2,1,0:T(8,128)(2,1)}, bf16[4,48,768]{2,1,0:T(8,128)(2,1)S(1)}, u32[]{:S(2)}, u32[]{:S(2)}) collective-permute-start(bf16[4,48,768]{2,1,0:T(8,128)(2,1)} %get-tuple-element.93), channel_id=1, source_target_pairs={{0,64},{16,80},{32,96},{48,112},{64,128},{80,144},{96,160},{112,17... | collective-permute-start | bytes 884744 | tf_op jit(solution)/shard_map/ppermute | solution.py:249
  91.4 25.0 %collective-permute-start.13 = (bf16[4,48,768]{2,1,0:T(8,128)(2,1)}, bf16[4,48,768]{2,1,0:T(8,128)(2,1)S(1)}, u32[]{:S(2)}, u32[]{:S(2)}) collective-permute-start(bf16[4,48,768]{2,1,0:T(8,128)(2,1)} %get-tuple-element.94), channel_id=1, source_target_pairs={{0,128},{16,144},{32,160},{48,176},{64,192},{80,208},{96,224},{112... | collective-permute-start | bytes 884744 | tf_op jit(solution)/shard_map/ppermute | solution.py:249
  94.0 22.4 %collective-permute-start.14 = (bf16[4,48,768]{2,1,0:T(8,128)(2,1)}, bf16[4,48,768]{2,1,0:T(8,128)(2,1)S(1)}, u32[]{:S(2)}, u32[]{:S(2)}) collective-permute-start(bf16[4,48,768]{2,1,0:T(8,128)(2,1)} %get-tuple-element.95), channel_id=1, source_target_pairs={{0,192},{16,208},{32,224},{48,240},{64,0},{80,16},{96,32},{112,48}... | collective-permute-start | bytes 884744 | tf_op jit(solution)/shard_map/ppermute | solution.py:249
  95.5 20.9 %collective-permute-start.15 = (bf16[4,48,768]{2,1,0:T(8,128)(2,1)}, bf16[4,48,768]{2,1,0:T(8,128)(2,1)S(1)}, u32[]{:S(2)}, u32[]{:S(2)}) collective-permute-start(bf16[4,48,768]{2,1,0:T(8,128)(2,1)} %get-tuple-element.97), channel_id=1, source_target_pairs={{0,16},{16,32},{32,48},{48,0},{64,80},{80,96},{96,112},{112,64},{1... | collective-permute-start | bytes 884744 | tf_op jit(solution)/shard_map/ppermute | solution.py:249
  96.1 20.4 %collective-permute-start.16 = (bf16[4,48,768]{2,1,0:T(8,128)(2,1)}, bf16[4,48,768]{2,1,0:T(8,128)(2,1)S(1)}, u32[]{:S(2)}, u32[]{:S(2)}) collective-permute-start(bf16[4,48,768]{2,1,0:T(8,128)(2,1)} %get-tuple-element.98), channel_id=1, source_target_pairs={{0,32},{16,48},{32,0},{48,16},{64,96},{80,112},{96,64},{112,80},{1... | collective-permute-start | bytes 884744 | tf_op jit(solution)/shard_map/ppermute | solution.py:249
  111.1 9.0 %copy-start.10 = (bf16[4,48,768]{2,1,0:T(8,128)(2,1)}, bf16[4,48,768]{2,1,0:T(8,128)(2,1)S(1)}, u32[]{:S(2)}) copy-start(bf16[4,48,768]{2,1,0:T(8,128)(2,1)S(1)} %collective-permute-done.12.refs_1_) | copy-start | bytes 884740
  111.1 9.0 %collective-permute-start.17 = (bf16[4,48,768]{2,1,0:T(8,128)(2,1)}, bf16[4,48,768]{2,1,0:T(8,128)(2,1)S(1)}, u32[]{:S(2)}, u32[]{:S(2)}) collective-permute-start(bf16[4,48,768]{2,1,0:T(8,128)(2,1)} %get-tuple-element.99), channel_id=1, source_target_pairs={{0,48},{16,0},{32,16},{48,32},{64,112},{80,64},{96,80},{112,96},{1... | collective-permute-start | bytes 884744 | tf_op jit(solution)/shard_map/ppermute | solution.py:249
  116.4 3.8 %copy-start.11 = (bf16[4,48,768]{2,1,0:T(8,128)(2,1)}, bf16[4,48,768]{2,1,0:T(8,128)(2,1)S(1)}, u32[]{:S(2)}) copy-start(bf16[4,48,768]{2,1,0:T(8,128)(2,1)S(1)} %collective-permute-done.13.refs_2_) | copy-start | bytes 884740
  116.4 3.8 %copy-start.12 = (bf16[4,48,768]{2,1,0:T(8,128)(2,1)}, bf16[4,48,768]{2,1,0:T(8,128)(2,1)S(1)}, u32[]{:S(2)}) copy-start(bf16[4,48,768]{2,1,0:T(8,128)(2,1)S(1)} %collective-permute-done.14.refs_3_) | copy-start | bytes 884740
  116.4 3.8 %copy-start.13 = (bf16[4,48,768]{2,1,0:T(8,128)(2,1)}, bf16[4,48,768]{2,1,0:T(8,128)(2,1)S(1)}, u32[]{:S(2)}) copy-start(bf16[4,48,768]{2,1,0:T(8,128)(2,1)S(1)} %collective-permute-done.15.refs_5_) | copy-start | bytes 884740
  116.4 3.8 %copy-start.14 = (bf16[4,48,768]{2,1,0:T(8,128)(2,1)}, bf16[4,48,768]{2,1,0:T(8,128)(2,1)S(1)}, u32[]{:S(2)}) copy-start(bf16[4,48,768]{2,1,0:T(8,128)(2,1)S(1)} %collective-permute-done.16.refs_6_) | copy-start | bytes 884740
  120.1 0.7 copy-start.15
